TPU v7x, 32 devices: a whole 2x2x4 slice. The times are simulated.
32 devices in a mesh: gx: 4 (over y, x), gy: 2 (over core), gz: 4 (over z).
Axes of the slice: x: 2, y: 2, z: 4, core: 2. Of those that a mesh axis runs over, the one named last changes fastest.
Arguments:
- right_side: float32 [128, 32, 512], P('gx', 'gy', 'gz'), may hold values from -24 to 24
- conductivity: float32 [128, 32, 512], P('gx', 'gy', 'gz'), may hold values from 0.2 to 5
Outputs:
- solution: float32 [128, 32, 512], P('gx', 'gy', 'gz')
- final_residual: float32 [128, 32, 512], P('gx', 'gy', 'gz')
All inputs are finite; a program needn't handle non-finite values.
Results may differ from a plain program's by a relative error of at most 0.0003.
Values sent between devices are 32-bit elements; how exact they have to be, the bound alone decides.
No kernel may reach another device: no remote copies, remote signals or barrier semaphores. Data moves between devices by JAX's collectives and lax.ppermute only.
A program may use at most 64 MiB of HBM per device.

v0:
```python
import jax
import jax.numpy as jnp
from jax import lax
from jax.sharding import PartitionSpec as P

LEVELS = 4
STEPS = 3
COARSE_STEPS = 8


LOWER_EDGE = 0.3
UPPER_EDGE = 2.0


def extended(block, sides, width):
    for axis, dim in sides:
        count = lax.axis_size(axis)
        forward = [(i, i + 1) for i in range(count - 1)]
        backward = [(target, source) for source, target in forward]
        low = lax.ppermute(
            lax.slice_in_dim(block, block.shape[dim] - width, None, axis=dim), axis, forward
        )
        high = lax.ppermute(lax.slice_in_dim(block, 0, width, axis=dim), axis, backward)
        block = jnp.concatenate([low, block, high], axis=dim)
    return block


def chebyshev_factors(sweeps):
    centre_value = 0.5 * (UPPER_EDGE + LOWER_EDGE)
    half_width = 0.5 * (UPPER_EDGE - LOWER_EDGE)
    ratio_value = centre_value / half_width
    damping = 1.0 / ratio_value
    factors = [(0.0, 1.0 / centre_value)]
    for sweep_index in range(1, sweeps):
        damping_next = 1.0 / (2.0 * ratio_value - damping)
        factors.append((damping_next * damping, 2.0 * damping_next / half_width))
        damping = damping_next
    return factors


def neighbours(padded):
    return (
        padded[2:, 1:-1, 1:-1],
        padded[:-2, 1:-1, 1:-1],
        padded[1:-1, 2:, 1:-1],
        padded[1:-1, :-2, 1:-1],
        padded[1:-1, 1:-1, 2:],
        padded[1:-1, 1:-1, :-2],
    )


def apply_operator(field_padded, coeff_padded, factor):
    centre_field = field_padded[1:-1, 1:-1, 1:-1]
    centre_coeff = coeff_padded[1:-1, 1:-1, 1:-1]
    summed = jnp.zeros(centre_field.shape, jnp.float32)
    for field_near, coeff_near in zip(neighbours(field_padded), neighbours(coeff_padded)):
        summed = summed + 0.5 * (centre_coeff + coeff_near) * (centre_field - field_near)
    return factor * summed


def diagonal_of(coeff_padded, factor):
    centre_coeff = coeff_padded[1:-1, 1:-1, 1:-1]
    summed = jnp.zeros(centre_coeff.shape, jnp.float32)
    for coeff_near in neighbours(coeff_padded):
        summed = summed + 0.5 * (centre_coeff + coeff_near)
    return factor * summed


def restrict_field(field):
    summed = field[0::2] + field[1::2]
    summed = summed[:, 0::2] + summed[:, 1::2]
    summed = summed[:, :, 0::2] + summed[:, :, 1::2]
    return 0.125 * summed


def prolong_field(padded):
    result = padded
    for axis_index in range(3):
        length = result.shape[axis_index] - 2
        middle = lax.slice_in_dim(result, 1, length + 1, axis=axis_index)
        preceding = lax.slice_in_dim(result, 0, length, axis=axis_index)
        following = lax.slice_in_dim(result, 2, length + 2, axis=axis_index)
        even_cells = 0.75 * middle + 0.25 * preceding
        odd_cells = 0.75 * middle + 0.25 * following
        joined = jnp.stack((even_cells, odd_cells), axis=axis_index + 1)
        new_shape = list(middle.shape)
        new_shape[axis_index] = 2 * length
        result = joined.reshape(new_shape)
    return result


def pad_faces(field):
    return extended(field, (("gx", 0), ("gy", 1), ("gz", 2)), 1)


def pad_correction(field):
    return extended(field, (("gx", 0), ("gy", 1), ("gz", 2)), 1)


def pad_group(field):
    widened = extended(field, (("gx", 0),), 1)
    return jnp.pad(widened, ((0, 0), (1, 1), (1, 1)))


def smooth_field(source, initial, coeff_padded, factor, sweeps, want_residual, padder):
    diagonal = diagonal_of(coeff_padded, factor)
    if initial is None:
        residual = source
    else:
        residual = source - apply_operator(padder(initial), coeff_padded, factor)
    factors = chebyshev_factors(sweeps)
    direction = None
    solution = None
    for sweep_index in range(sweeps):
        keep_factor, push_factor = factors[sweep_index]
        if sweep_index > 0:
            residual = residual - apply_operator(padder(direction), coeff_padded, factor)
            direction = keep_factor * direction + push_factor * (residual / diagonal)
        else:
            direction = push_factor * (residual / diagonal)
        if solution is None and initial is None:
            solution = direction
        elif solution is None:
            solution = initial + direction
        else:
            solution = solution + direction
    if want_residual:
        residual = residual - apply_operator(padder(direction), coeff_padded, factor)
    return (solution, residual)


def assemble_grid(gathered, count_x, count_y, count_z):
    extent = gathered.shape
    blocks = gathered.reshape((count_x, count_y, count_z) + extent[1:])
    arranged = jnp.transpose(blocks, (3, 0, 4, 1, 5, 2, 6))
    return arranged.reshape(
        (extent[1], count_x * extent[2], count_y * extent[3], count_z * extent[4])
    )


def on_device(right_side, conductivity):
    conducts = [conductivity]
    for level_index in range(LEVELS):
        conducts.append(restrict_field(conducts[level_index]))
    local_levels = LEVELS
    coeff_first = pad_faces(conductivity)
    solution, residual = smooth_field(right_side, None, coeff_first, 1.0, STEPS, True, pad_faces)
    padded_coeffs = [coeff_first]
    presmoothed = [solution]
    sources = [right_side, restrict_field(residual)]
    for level_index in range(1, local_levels):
        factor = 0.25**level_index
        coeff_level = pad_faces(conducts[level_index])
        padded_coeffs.append(coeff_level)
        solution, residual = smooth_field(
            sources[level_index], None, coeff_level, factor, STEPS, True, pad_faces
        )
        presmoothed.append(solution)
        sources.append(restrict_field(residual))
    block_x, block_y, block_z = sources[local_levels].shape
    coarse_block = jnp.stack((sources[LEVELS], conducts[LEVELS]))[None]
    gathered = lax.all_gather(coarse_block, ("gy", "gz"), axis=0, tiled=True)
    coarse_grid = assemble_grid(gathered, 1, lax.axis_size("gy"), lax.axis_size("gz"))
    offsets = (jnp.int32(0), lax.axis_index("gy") * block_y, lax.axis_index("gz") * block_z)
    coarse_coeff = pad_group(coarse_grid[1])
    coarse_solution, unused = smooth_field(
        coarse_grid[0], None, coarse_coeff, 0.25**LEVELS, COARSE_STEPS, False, pad_group
    )
    coarse_padded = pad_group(coarse_solution)
    correction_padded = lax.dynamic_slice(
        coarse_padded, offsets, (block_x + 2, block_y + 2, block_z + 2)
    )
    correction = presmoothed[0]
    for level_index in reversed(range(local_levels)):
        initial = presmoothed[level_index] + prolong_field(correction_padded)
        correction, residual = smooth_field(
            sources[level_index],
            initial,
            padded_coeffs[level_index],
            0.25**level_index,
            STEPS,
            level_index == 0,
            pad_faces,
        )
        if level_index > 0:
            correction_padded = pad_correction(correction)
    return (correction, residual)


def solution(mesh):
    in_specs = (P("gx", "gy", "gz"), P("gx", "gy", "gz"))
    out_specs = (P("gx", "gy", "gz"), P("gx", "gy", "gz"))
    return jax.shard_map(
        on_device, mesh=mesh, in_specs=in_specs, out_specs=out_specs, check_vma=False
    )
```

profile of v0, /device:TPU:0, one launch (start us, length us, event | category | flops | bytes accessed | tf_op | source)
XLA Modules:
  0.0 841.5 jit_solution(13354991043988678910)
XLA Ops:
  1.4 4.8 collective-permute-start.1
  23.6 5.5 collective-permute-done.5
  52.5 4.6 collective-permute-start.11
  57.1 8.4 collective-permute-done.10
  83.1 5.0 collective-permute-start.17
  88.1 8.0 collective-permute-done.16
  118.0 5.2 collective-permute-start.23
  123.3 8.7 %collective-permute-done.22 = f32[34,18,1]{2,1,0:T(8,128)S(1)} collective-permute-done((f32[34,18,1]{2,1,0:T(8,128)S(1)}, f32[34,18,1]{2,1,0:T(8,128)S(1)}, u32[]{:S(2)}, u32[]{:S(2)}) %collective-permute-start.22) | collective-permute-done | bytes 2480 | tf_op jit(solution)/shard_map/ppermute | solution.py:23
  135.7 4.8 collective-permute-start.31
  152.4 5.0 collective-permute-start.35
  181.3 5.7 collective-permute-start.41
  206.2 5.0 collective-permute-start.47
  247.6 4.6 collective-permute-start.61
  334.0 4.8 collective-permute-start.89
  354.4 4.8 collective-permute-start.95
  360.9 21.1 %all-gather = f32[16,2,1,8]{3,1,2,0:T(2,128)S(1)} all-gather(f32[2,2,1,8]{3,1,2,0:T(2,128)S(1)} %pad_maximum_fusion.574), channel_id=2, replica_groups=mesh['gx'=4,'gy'=2,'gz'=4] {'gy','gz'}, dimensions={0}, use_global_device_ids=true | all-gather | bytes 1152 | tf_op jit(solution)/shard_map/all_gather | solution.py:162
  472.7 4.8 collective-permute-start.119
  493.1 4.8 collective-permute-start.125
  513.5 4.8 collective-permute-start.131
  577.4 4.9 collective-permute-start.149
  598.1 4.9 collective-permute-start.155
  642.6 4.6 collective-permute-start.167
  664.5 5.0 collective-permute-start.173
  686.8 5.0 collective-permute-start.179
  739.6 4.6 collective-permute-start.191
  744.2 7.7 collective-permute-done.190
  767.9 5.0 collective-permute-start.197
  773.0 8.0 collective-permute-done.196
  797.0 5.0 collective-permute-start.203
  802.1 8.0 collective-permute-done.202
  826.2 5.0 collective-permute-start.209
  832.2 7.0 collective-permute-done.208
  (727 shorter events, 641.8 us)
Async XLA Ops:
  16.4 12.7 %collective-permute-start.5 = (f32[34,18,1]{2,1,0:T(8,128)S(1)}, f32[34,18,1]{2,1,0:T(8,128)S(1)}, u32[]{:S(2)}, u32[]{:S(2)}) collective-permute-start(f32[34,18,1]{2,1,0:T(8,128)S(1)} %get-tuple-element.105), channel_id=1, source_target_pairs={{0,1},{1,2},{2,3},{4,5},{5,6},{6,7},{8,9},{9,10},{10,11},{12,13},{... | collective-permute-start | bytes 7352 | tf_op jit(solution)/shard_map/ppermute | solution.py:20
  19.9 13.3 %collective-permute-start.4 = (f32[34,18,1]{2,1,0:T(8,128)S(1)}, f32[34,18,1]{2,1,0:T(8,128)S(1)}, u32[]{:S(2)}, u32[]{:S(2)}) collective-permute-start(f32[34,18,1]{2,1,0:T(8,128)S(1)} %get-tuple-element.106), channel_id=1, source_target_pairs={{1,0},{2,1},{3,2},{5,4},{6,5},{7,6},{9,8},{10,9},{11,10},{13,12},{... | collective-permute-start | bytes 7352 | tf_op jit(solution)/shard_map/ppermute | solution.py:23
  46.2 10.9 %collective-permute-start.25 = (f32[1,8,64]{2,1,0:T(8,128)S(1)}, f32[1,8,64]{2,1,0:T(8,128)S(1)}, u32[]{:S(2)}, u32[]{:S(2)}) collective-permute-start(f32[1,8,64]{2,1,0:T(8,128)S(1)} %get-tuple-element.207), channel_id=1, source_target_pairs={{0,8},{8,16},{16,24},{1,9},{9,17},{17,25},{2,10},{10,18},{18,26},{... | collective-permute-start | bytes 6152 | tf_op jit(solution)/shard_map/ppermute | solution.py:20
  51.2 14.3 %collective-permute-start.10 = (f32[34,18,1]{2,1,0:T(8,128)S(1)}, f32[34,18,1]{2,1,0:T(8,128)S(1)}, u32[]{:S(2)}, u32[]{:S(2)}) collective-permute-start(f32[34,18,1]{2,1,0:T(8,128)S(1)} %get-tuple-element.103), channel_id=1, source_target_pairs={{1,0},{2,1},{3,2},{5,4},{6,5},{7,6},{9,8},{10,9},{11,10},{13,12},{... | collective-permute-start | bytes 7352 | tf_op jit(solution)/shard_map/ppermute | solution.py:23
  52.5 14.2 %collective-permute-start.11 = (f32[34,18,1]{2,1,0:T(8,128)S(1)}, f32[34,18,1]{2,1,0:T(8,128)S(1)}, u32[]{:S(2)}, u32[]{:S(2)}) collective-permute-start(f32[34,18,1]{2,1,0:T(8,128)S(1)} %get-tuple-element.104), channel_id=1, source_target_pairs={{0,1},{1,2},{2,3},{4,5},{5,6},{6,7},{8,9},{9,10},{10,11},{12,13},{... | collective-permute-start | bytes 7352 | tf_op jit(solution)/shard_map/ppermute | solution.py:20
  67.1 9.9 %collective-permute-start.13 = (f32[1,16,128]{2,1,0:T(8,128)S(1)}, f32[1,16,128]{2,1,0:T(8,128)S(1)}, u32[]{:S(2)}, u32[]{:S(2)}) collective-permute-start(f32[1,16,128]{2,1,0:T(8,128)S(1)} %get-tuple-element.135), channel_id=1, source_target_pairs={{0,8},{8,16},{16,24},{1,9},{9,17},{17,25},{2,10},{10,18},{18,26},{... | collective-permute-start | bytes 24584 | tf_op jit(solution)/shard_map/ppermute | solution.py:20
  72.7 30.9 %collective-permute-start.26 = (f32[18,1,64]{2,1,0:T(1,128)S(1)}, f32[18,1,64]{2,1,0:T(1,128)S(1)}, u32[]{:S(2)}, u32[]{:S(2)}) collective-permute-start(f32[18,1,64]{2,1,0:T(1,128)S(1)} %get-tuple-element.189), channel_id=1, source_target_pairs={{4,0},{5,1},{6,2},{7,3},{12,8},{13,9},{14,10},{15,11},{20,16},{21,... | collective-permute-start | bytes 13832 | tf_op jit(solution)/shard_map/ppermute | solution.py:23
  81.8 14.4 %collective-permute-start.16 = (f32[34,18,1]{2,1,0:T(8,128)S(1)}, f32[34,18,1]{2,1,0:T(8,128)S(1)}, u32[]{:S(2)}, u32[]{:S(2)}) collective-permute-start(f32[34,18,1]{2,1,0:T(8,128)S(1)} %get-tuple-element.101), channel_id=1, source_target_pairs={{1,0},{2,1},{3,2},{5,4},{6,5},{7,6},{9,8},{10,9},{11,10},{13,12},{... | collective-permute-start | bytes 7352 | tf_op jit(solution)/shard_map/ppermute | solution.py:23
  83.1 14.2 %collective-permute-start.17 = (f32[34,18,1]{2,1,0:T(8,128)S(1)}, f32[34,18,1]{2,1,0:T(8,128)S(1)}, u32[]{:S(2)}, u32[]{:S(2)}) collective-permute-start(f32[34,18,1]{2,1,0:T(8,128)S(1)} %get-tuple-element.102), channel_id=1, source_target_pairs={{0,1},{1,2},{2,3},{4,5},{5,6},{6,7},{8,9},{9,10},{10,11},{12,13},{... | collective-permute-start | bytes 7352 | tf_op jit(solution)/shard_map/ppermute | solution.py:20
  110.7 12.5 %collective-permute-start.29 = (f32[18,10,1]{2,0,1:T(8,128)S(1)}, f32[18,10,1]{2,0,1:T(8,128)S(1)}, u32[]{:S(2)}, u32[]{:S(2)}) collective-permute-start(f32[18,10,1]{2,0,1:T(8,128)S(1)} %get-tuple-element.173), channel_id=1, source_target_pairs={{0,1},{1,2},{2,3},{4,5},{5,6},{6,7},{8,9},{9,10},{10,11},{12,13},{... | collective-permute-start | bytes 2168 | tf_op jit(solution)/shard_map/ppermute | solution.py:20
  116.7 15.3 %collective-permute-start.22 = (f32[34,18,1]{2,1,0:T(8,128)S(1)}, f32[34,18,1]{2,1,0:T(8,128)S(1)}, u32[]{:S(2)}, u32[]{:S(2)}) collective-permute-start(f32[34,18,1]{2,1,0:T(8,128)S(1)} %get-tuple-element.99), channel_id=1, source_target_pairs={{1,0},{2,1},{3,2},{5,4},{6,5},{7,6},{9,8},{10,9},{11,10},{13,12},{... | collective-permute-start | bytes 7352 | tf_op jit(solution)/shard_map/ppermute | solution.py:23
  118.0 14.8 %collective-permute-start.23 = (f32[34,18,1]{2,1,0:T(8,128)S(1)}, f32[34,18,1]{2,1,0:T(8,128)S(1)}, u32[]{:S(2)}, u32[]{:S(2)}) collective-permute-start(f32[34,18,1]{2,1,0:T(8,128)S(1)} %get-tuple-element.100), channel_id=1, source_target_pairs={{0,1},{1,2},{2,3},{4,5},{5,6},{6,7},{8,9},{9,10},{10,11},{12,13},{... | collective-permute-start | bytes 7352 | tf_op jit(solution)/shard_map/ppermute | solution.py:20
  169.0 8.5 %collective-permute-start.39 = (f32[18,1,64]{2,1,0:T(1,128)S(1)}, f32[18,1,64]{2,1,0:T(1,128)S(1)}, u32[]{:S(2)}, u32[]{:S(2)}) collective-permute-start(f32[18,1,64]{2,1,0:T(1,128)S(1)} %get-tuple-element.186), channel_id=1, source_target_pairs={{0,4},{1,5},{2,6},{3,7},{8,12},{9,13},{10,14},{11,15},{16,20},{17,... | collective-permute-start | bytes 13832 | tf_op jit(solution)/shard_map/ppermute | solution.py:20
  170.3 25.4 %collective-permute-start.48 = (f32[1,4,32]{2,1,0:T(4,128)S(1)}, f32[1,4,32]{2,1,0:T(4,128)S(1)}, u32[]{:S(2)}, u32[]{:S(2)}) collective-permute-start(f32[1,4,32]{2,1,0:T(4,128)S(1)} %get-tuple-element.267), channel_id=1, source_target_pairs={{8,0},{16,8},{24,16},{9,1},{17,9},{25,17},{10,2},{18,10},{26,18},{... | collective-permute-start | bytes 1544 | tf_op jit(solution)/shard_map/ppermute | solution.py:23
  171.6 24.1 %collective-permute-start.49 = (f32[1,4,32]{2,1,0:T(4,128)S(1)}, f32[1,4,32]{2,1,0:T(4,128)S(1)}, u32[]{:S(2)}, u32[]{:S(2)}) collective-permute-start(f32[1,4,32]{2,1,0:T(4,128)S(1)} %get-tuple-element.268), channel_id=1, source_target_pairs={{0,8},{8,16},{16,24},{1,9},{9,17},{17,25},{2,10},{10,18},{18,26},{... | collective-permute-start | bytes 1544 | tf_op jit(solution)/shard_map/ppermute | solution.py:20
  204.9 11.6 %collective-permute-start.46 = (f32[18,10,1]{2,0,1:T(8,128)S(1)}, f32[18,10,1]{2,0,1:T(8,128)S(1)}, u32[]{:S(2)}, u32[]{:S(2)}) collective-permute-start(f32[18,10,1]{2,0,1:T(8,128)S(1)} %get-tuple-element.161), channel_id=1, source_target_pairs={{1,0},{2,1},{3,2},{5,4},{6,5},{7,6},{9,8},{10,9},{11,10},{13,12},{... | collective-permute-start | bytes 2168 | tf_op jit(solution)/shard_map/ppermute | solution.py:23
  206.2 10.3 %collective-permute-start.47 = (f32[18,10,1]{2,0,1:T(8,128)S(1)}, f32[18,10,1]{2,0,1:T(8,128)S(1)}, u32[]{:S(2)}, u32[]{:S(2)}) collective-permute-start(f32[18,10,1]{2,0,1:T(8,128)S(1)} %get-tuple-element.162), channel_id=1, source_target_pairs={{0,1},{1,2},{2,3},{4,5},{5,6},{6,7},{8,9},{9,10},{10,11},{12,13},{... | collective-permute-start | bytes 2168 | tf_op jit(solution)/shard_map/ppermute | solution.py:20
  235.8 11.7 %collective-permute-start.58 = (f32[10,6,1]{2,1,0:T(8,128)S(1)}, f32[10,6,1]{2,1,0:T(8,128)S(1)}, u32[]{:S(2)}, u32[]{:S(2)}) collective-permute-start(f32[10,6,1]{2,1,0:T(8,128)S(1)} %get-tuple-element.225), channel_id=1, source_target_pairs={{1,0},{2,1},{3,2},{5,4},{6,5},{7,6},{9,8},{10,9},{11,10},{13,12},{... | collective-permute-start | bytes 728 | tf_op jit(solution)/shard_map/ppermute | solution.py:23
  237.0 10.4 %collective-permute-start.59 = (f32[10,6,1]{2,1,0:T(8,128)S(1)}, f32[10,6,1]{2,1,0:T(8,128)S(1)}, u32[]{:S(2)}, u32[]{:S(2)}) collective-permute-start(f32[10,6,1]{2,1,0:T(8,128)S(1)} %get-tuple-element.226), channel_id=1, source_target_pairs={{0,1},{1,2},{2,3},{4,5},{5,6},{6,7},{8,9},{9,10},{10,11},{12,13},{... | collective-permute-start | bytes 728 | tf_op jit(solution)/shard_map/ppermute | solution.py:20
  241.6 12.0 %collective-permute-start.72 = (f32[1,2,16]{2,1,0:T(2,128)S(1)}, f32[1,2,16]{2,1,0:T(2,128)S(1)}, u32[]{:S(2)}, u32[]{:S(2)}) collective-permute-start(f32[1,2,16]{2,1,0:T(2,128)S(1)} %get-tuple-element.323), channel_id=1, source_target_pairs={{8,0},{16,8},{24,16},{9,1},{17,9},{25,17},{10,2},{18,10},{26,18},{... | collective-permute-start | bytes 392 | tf_op jit(solution)/shard_map/ppermute | solution.py:23
  242.9 10.7 %collective-permute-start.73 = (f32[1,2,16]{2,1,0:T(2,128)S(1)}, f32[1,2,16]{2,1,0:T(2,128)S(1)}, u32[]{:S(2)}, u32[]{:S(2)}) collective-permute-start(f32[1,2,16]{2,1,0:T(2,128)S(1)} %get-tuple-element.324), channel_id=1, source_target_pairs={{0,8},{8,16},{16,24},{1,9},{9,17},{17,25},{2,10},{10,18},{18,26},{... | collective-permute-start | bytes 392 | tf_op jit(solution)/shard_map/ppermute | solution.py:20
  262.2 8.7 %collective-permute-start.64 = (f32[10,6,1]{2,1,0:T(8,128)S(1)}, f32[10,6,1]{2,1,0:T(8,128)S(1)}, u32[]{:S(2)}, u32[]{:S(2)}) collective-permute-start(f32[10,6,1]{2,1,0:T(8,128)S(1)} %get-tuple-element.223), channel_id=1, source_target_pairs={{1,0},{2,1},{3,2},{5,4},{6,5},{7,6},{9,8},{10,9},{11,10},{13,12},{... | collective-permute-start | bytes 728 | tf_op jit(solution)/shard_map/ppermute | solution.py:23
  284.2 10.8 %collective-permute-start.70 = (f32[10,6,1]{2,1,0:T(8,128)S(1)}, f32[10,6,1]{2,1,0:T(8,128)S(1)}, u32[]{:S(2)}, u32[]{:S(2)}) collective-permute-start(f32[10,6,1]{2,1,0:T(8,128)S(1)} %get-tuple-element.221), channel_id=1, source_target_pairs={{1,0},{2,1},{3,2},{5,4},{6,5},{7,6},{9,8},{10,9},{11,10},{13,12},{... | collective-permute-start | bytes 728 | tf_op jit(solution)/shard_map/ppermute | solution.py:23
  285.5 9.5 %collective-permute-start.71 = (f32[10,6,1]{2,1,0:T(8,128)S(1)}, f32[10,6,1]{2,1,0:T(8,128)S(1)}, u32[]{:S(2)}, u32[]{:S(2)}) collective-permute-start(f32[10,6,1]{2,1,0:T(8,128)S(1)} %get-tuple-element.222), channel_id=1, source_target_pairs={{0,1},{1,2},{2,3},{4,5},{5,6},{6,7},{8,9},{9,10},{10,11},{12,13},{... | collective-permute-start | bytes 728 | tf_op jit(solution)/shard_map/ppermute | solution.py:20
  738.3 13.6 %collective-permute-start.190 = (f32[34,18,1]{2,1,0:T(8,128)S(1)}, f32[34,18,1]{2,1,0:T(8,128)S(1)}, u32[]{:S(2)}, u32[]{:S(2)}) collective-permute-start(f32[34,18,1]{2,1,0:T(8,128)S(1)} %get-tuple-element.97), channel_id=1, source_target_pairs={{1,0},{2,1},{3,2},{5,4},{6,5},{7,6},{9,8},{10,9},{11,10},{13,12},{... | collective-permute-start | bytes 7352 | tf_op jit(solution)/shard_map/ppermute | solution.py:23
  739.6 13.5 %collective-permute-start.191 = (f32[34,18,1]{2,1,0:T(8,128)S(1)}, f32[34,18,1]{2,1,0:T(8,128)S(1)}, u32[]{:S(2)}, u32[]{:S(2)}) collective-permute-start(f32[34,18,1]{2,1,0:T(8,128)S(1)} %get-tuple-element.98), channel_id=1, source_target_pairs={{0,1},{1,2},{2,3},{4,5},{5,6},{6,7},{8,9},{9,10},{10,11},{12,13},{... | collective-permute-start | bytes 7352 | tf_op jit(solution)/shard_map/ppermute | solution.py:20
  766.6 14.4 %collective-permute-start.196 = (f32[34,18,1]{2,1,0:T(8,128)S(1)}, f32[34,18,1]{2,1,0:T(8,128)S(1)}, u32[]{:S(2)}, u32[]{:S(2)}) collective-permute-start(f32[34,18,1]{2,1,0:T(8,128)S(1)} %get-tuple-element.95), channel_id=1, source_target_pairs={{1,0},{2,1},{3,2},{5,4},{6,5},{7,6},{9,8},{10,9},{11,10},{13,12},{... | collective-permute-start | bytes 7352 | tf_op jit(solution)/shard_map/ppermute | solution.py:23
  767.9 14.2 %collective-permute-start.197 = (f32[34,18,1]{2,1,0:T(8,128)S(1)}, f32[34,18,1]{2,1,0:T(8,128)S(1)}, u32[]{:S(2)}, u32[]{:S(2)}) collective-permute-start(f32[34,18,1]{2,1,0:T(8,128)S(1)} %get-tuple-element.96), channel_id=1, source_target_pairs={{0,1},{1,2},{2,3},{4,5},{5,6},{6,7},{8,9},{9,10},{10,11},{12,13},{... | collective-permute-start | bytes 7352 | tf_op jit(solution)/shard_map/ppermute | solution.py:20
  795.7 14.4 %collective-permute-start.202 = (f32[34,18,1]{2,1,0:T(8,128)S(1)}, f32[34,18,1]{2,1,0:T(8,128)S(1)}, u32[]{:S(2)}, u32[]{:S(2)}) collective-permute-start(f32[34,18,1]{2,1,0:T(8,128)S(1)} %get-tuple-element.93), channel_id=1, source_target_pairs={{1,0},{2,1},{3,2},{5,4},{6,5},{7,6},{9,8},{10,9},{11,10},{13,12},{... | collective-permute-start | bytes 7352 | tf_op jit(solution)/shard_map/ppermute | solution.py:23
  797.0 14.2 %collective-permute-start.203 = (f32[34,18,1]{2,1,0:T(8,128)S(1)}, f32[34,18,1]{2,1,0:T(8,128)S(1)}, u32[]{:S(2)}, u32[]{:S(2)}) collective-permute-start(f32[34,18,1]{2,1,0:T(8,128)S(1)} %get-tuple-element.94), channel_id=1, source_target_pairs={{0,1},{1,2},{2,3},{4,5},{5,6},{6,7},{8,9},{9,10},{10,11},{12,13},{... | collective-permute-start | bytes 7352 | tf_op jit(solution)/shard_map/ppermute | solution.py:20
  824.9 14.4 %collective-permute-start.208 = (f32[34,18,1]{2,1,0:T(8,128)S(1)}, f32[34,18,1]{2,1,0:T(8,128)S(1)}, u32[]{:S(2)}, u32[]{:S(2)}) collective-permute-start(f32[34,18,1]{2,1,0:T(8,128)S(1)} %get-tuple-element.91), channel_id=1, source_target_pairs={{1,0},{2,1},{3,2},{5,4},{6,5},{7,6},{9,8},{10,9},{11,10},{13,12},{... | collective-permute-start | bytes 7352 | tf_op jit(solution)/shard_map/ppermute | solution.py:23
  826.2 14.2 %collective-permute-start.209 = (f32[34,18,1]{2,1,0:T(8,128)S(1)}, f32[34,18,1]{2,1,0:T(8,128)S(1)}, u32[]{:S(2)}, u32[]{:S(2)}) collective-permute-start(f32[34,18,1]{2,1,0:T(8,128)S(1)} %get-tuple-element.92), channel_id=1, source_target_pairs={{0,1},{1,2},{2,3},{4,5},{5,6},{6,7},{8,9},{9,10},{10,11},{12,13},{... | collective-permute-start | bytes 7352 | tf_op jit(solution)/shard_map/ppermute | solution.py:20
  (181 other events, 883.8 us)
where the time goes:
time: 847 us; the launch traced here: 842 us
  starting transfers between devices  462 us (55%)
  waiting for transfers between devices  320 us (38%)
  blocking collectives  21.1 us (2%)
  local copies, waits for them, and re-layouts  17.8 us (2%)
  other arithmetic  15.8 us (2%)
    ppermute x105, starting transfers between devices, extended(): lax.ppermute(lax.slice_in_dim(block, block.shape[dim] - width, None, axis...  327 us
    ppermute x105, waiting for transfers between devices, extended(): lax.ppermute(lax.slice_in_dim(block, 0, width, axis=dim), axis, backward)  285 us
    ppermute x105, starting transfers between devices, extended(): lax.ppermute(lax.slice_in_dim(block, 0, width, axis=dim), axis, backward)  136 us
    ppermute x105, waiting for transfers between devices, extended(): lax.ppermute(lax.slice_in_dim(block, block.shape[dim] - width, None, axis...  34.6 us
    all_gather x1, blocking collectives, on_device(): gathered = lax.all_gather(coarse_block, ('gy', 'gz'), axis=0, tiled=True)  21.1 us
  transfers between devices with their start and end apart: 210, of which 107 were waited for; matrix products, arithmetic and copies ran while one was open for 1% of the time, Pallas kernels for 0%

commit v1 on v0

v1 whole, which is shorter than its diff:
```python
import functools
import jax
import jax.numpy as jnp
from jax import lax
from jax.experimental import pallas as pl
from jax.experimental.pallas import tpu as pltpu
from jax.sharding import PartitionSpec as P

LEVELS = 4
STEPS = 3
COARSE_STEPS = 8
LOWER_EDGE = 0.3
UPPER_EDGE = 2.0

LANES = 128
HALF = 64
REACH_X = 12
REACH_XB = 9
REACH_Z = 20
WIN0 = 4
WIN1 = REACH_X // 2
SLOTS = LANES // REACH_Z
AXES = ("gx", "gy", "gz")


def chebyshev_factors(sweeps):
    centre_value = 0.5 * (UPPER_EDGE + LOWER_EDGE)
    half_width = 0.5 * (UPPER_EDGE - LOWER_EDGE)
    ratio_value = centre_value / half_width
    damping = 1.0 / ratio_value
    factors = [(0.0, 1.0 / centre_value)]
    for _ in range(1, sweeps):
        damping_next = 1.0 / (2.0 * ratio_value - damping)
        factors.append((damping_next * damping, 2.0 * damping_next / half_width))
        damping = damping_next
    return factors


FACTORS = chebyshev_factors(STEPS)
COARSE_FACTORS = chebyshev_factors(COARSE_STEPS)


def chunks(count, body, size, first=1):
    if count == size:
        body(first)
    else:
        def step(i, carry):
            body(first + i * size)
            return carry
        lax.fori_loop(0, count // size, step, 0)


def rows_of(shape):
    return lax.broadcasted_iota(jnp.int32, shape, len(shape) - 2)


def lanes_of(shape):
    return lax.broadcasted_iota(jnp.int32, shape, len(shape) - 1)


class Grid:
    def __init__(self, x, y, z, sy, sz, whole_z, size):
        self.x, self.y, self.z, self.sy, self.sz = x, y, z, sy, sz
        self.whole_z, self.size = whole_z, size

    def up_y(self, v):
        return pltpu.roll(v, self.y - self.sy, v.ndim - 2)

    def down_y(self, v):
        return pltpu.roll(v, self.sy, v.ndim - 2)

    def up_z(self, v):
        return pltpu.roll(v, self.z - self.sz, v.ndim - 1)

    def down_z(self, v):
        return pltpu.roll(v, self.sz, v.ndim - 1)

    def setup(self, k_ref, cx, cy, cz, iv, ds, scale, after=None):
        cx[0] = 0.5 * (k_ref[0] + k_ref[1])

        def body(at):
            here = pl.ds(at, self.size)
            k = k_ref[here]
            row, lane = rows_of(k.shape), lanes_of(k.shape)
            k_next = k_ref[pl.ds(at + 1, self.size)]
            k_prev = k_ref[pl.ds(at - 1, self.size)]
            not_last = row < self.y - self.sy
            k_up = jnp.where(not_last, self.up_y(k), 0.0)
            k_down = jnp.where(row >= self.sy, self.down_y(k), 0.0)
            z_up, z_down = self.up_z(k), self.down_z(k)
            if self.whole_z:
                inner = lane < self.z - self.sz
                z_up = jnp.where(inner, z_up, 0.0)
                z_down = jnp.where(lane >= self.sz, z_down, 0.0)
            total = 3.0 * k + 0.5 * ((k_next + k_prev) + (k_up + k_down) + (z_up + z_down))
            inverse = jnp.where(k > 0.0, 1.0 / total, 0.0)
            cx[here] = 0.5 * (k + k_next)
            cy[here] = jnp.where(not_last, 0.5 * (k + k_up), 0.0)
            across = 0.5 * (k + z_up)
            cz[here] = jnp.where(inner, across, 0.0) if self.whole_z else across
            iv[here] = inverse
            if ds is not None:
                ds[here] = scale * total
            if after is not None:
                after(at, here, inverse)

        chunks(self.x, body, self.size)

    def step(self, coeffs, src, g_in, keep, push, out, first=1, count=None):
        cx, cy, cz, iv = coeffs

        def body(at):
            here, before = pl.ds(at, self.size), pl.ds(at - 1, self.size)
            v = src[here]
            y_coeff, z_coeff = cy[here], cz[here]
            near = cx[here] * src[pl.ds(at + 1, self.size)] + cx[before] * src[before]
            near = near + (y_coeff * self.up_y(v) + self.down_y(y_coeff * v))
            near = near + (z_coeff * self.up_z(v) + self.down_z(z_coeff * v))
            g = g_in[here] - v + iv[here] * near
            out(here, v, g, None if push is None else (keep * v + push * g if keep else push * g))

        chunks(count or self.x, body, self.size, first)


def pair_z(v, shift, lanes):
    even = (lanes_of(v.shape) // shift) % 2 == 0
    return v + jnp.where(even, pltpu.roll(v, lanes - shift, v.ndim - 1), pltpu.roll(v, shift, v.ndim - 1))


def pair_y(v, shift, rows):
    even = (rows_of(v.shape) // shift) % 2 == 0
    return v + jnp.where(even, pltpu.roll(v, rows - shift, v.ndim - 2), pltpu.roll(v, shift, v.ndim - 2))


def spread_z(v, shift, lanes, whole):
    lane = lanes_of(v.shape)
    even = (lane // shift) % 2 == 0
    low, high = pltpu.roll(v, shift, v.ndim - 1), pltpu.roll(v, lanes - shift, v.ndim - 1)
    if whole:
        low = jnp.where(lane >= shift, low, 0.0)
        high = jnp.where(lane < lanes - shift, high, 0.0)
    return 0.75 * v + 0.25 * jnp.where(even, low, high)


def spread_y(v, shift, rows):
    row = rows_of(v.shape)
    even = (row // shift) % 2 == 0
    low = jnp.where(row >= shift, pltpu.roll(v, shift, v.ndim - 2), 0.0)
    high = jnp.where(row < rows - shift, pltpu.roll(v, rows - shift, v.ndim - 2), 0.0)
    return 0.75 * v + 0.25 * jnp.where(even, low, high)


def zero_pads(*refs):
    for ref in refs:
        ref[0] = jnp.zeros(ref.shape[1:], jnp.float32)
        ref[ref.shape[0] - 1] = jnp.zeros(ref.shape[1:], jnp.float32)


def core_of():
    return lax.rem(lax.axis_index("gy"), 2)


def pack_kernel(geo, own_b, own_k, sib_b, sib_k, z_out, dp_out, dm_out):
    core = core_of()
    bx, ye = geo["bx"], geo["ye"]
    base = jnp.where(core == 1, LANES - REACH_Z, 0)
    lane = lanes_of((ye, LANES))

    def pack(out, first_b, count_b, first_k, count_k):
        for refs, half in (((own_b, own_k), core), ((sib_b, sib_k), 1 - core)):
            rows = pl.ds(pl.multiple_of(half * ye, 8), ye)
            planes = [(refs[0], first_b + p) for p in range(count_b)] + [(refs[1], first_k + p) for p in range(count_k)]
            for m in range(out.shape[0]):
                packed = jnp.zeros((ye, LANES), jnp.float32)
                for q, (ref, p) in enumerate(planes[m * SLOTS:(m + 1) * SLOTS]):
                    moved = pltpu.roll(ref[p], lax.rem(REACH_Z * q - base + LANES, LANES), 1)
                    packed = jnp.where((lane >= REACH_Z * q) & (lane < REACH_Z * (q + 1)), moved, packed)
                out[m, rows] = packed

    pack(z_out, 0, bx, 0, bx)
    high_b, high_k = bx - REACH_XB, bx - REACH_X
    pack(dp_out, jnp.where(core == 0, high_b, 0), REACH_XB, jnp.where(core == 0, high_k, 0), REACH_X)
    pack(dm_out, jnp.where(core == 0, 0, high_b), REACH_XB, jnp.where(core == 0, 0, high_k), REACH_X)


def down_kernel(geo, *refs):
    (own_b, own_k, sib_b, sib_k, even_own, odd_own, any_even, any_odd, any_z, any_dp, any_dm,
     packed_out, even_out, odd_out, o_cx, o_cy, o_cz, o_iv, o_g0, o_w, p_cx, p_cy, p_cz, p_iv, p_g0, p_w,
     even_sib, odd_sib, z_in, dp_in, dm_in,
     k0, cx, cy, cz, iv, ds, g0, g, d1, d2,
     k1, ex, ey, ez, ei, es, h0, h, f1, f2, u1, half_y, half_y1, sems, in_sems) = refs
    core = core_of()
    ix, nx = lax.axis_index("gx"), lax.axis_size("gx")
    iz, nz = lax.axis_index("gz"), lax.axis_size("gz")
    bx, ye, yw, xw = geo["bx"], geo["ye"], geo["yw"], geo["xw"]
    z_there = jnp.where(core == 0, iz > 0, iz < nz - 1)
    lo_there, hi_there = ix > 0, ix < nx - 1
    even = lax.rem(ix, 2) == 0

    arrivals = []
    for i, (source, target) in enumerate(
            ((any_even, even_sib), (any_odd, odd_sib), (any_z, z_in), (any_dp, dp_in), (any_dm, dm_in))):
        copy = pltpu.make_async_copy(source, target, in_sems.at[i])
        copy.start()
        arrivals.append(copy)

    lane = lanes_of((yw, LANES))
    halo_lanes = jnp.where(core == 0, lane - (LANES - REACH_Z), REACH_Z - 1 - lane) >= 0
    base = jnp.where(core == 0, LANES - REACH_Z, 0)

    def strip(ref, p):
        return pltpu.roll(ref[p // SLOTS], lax.rem(base - REACH_Z * (p % SLOTS) + LANES, LANES), 1)

    own_rows = pl.ds(pl.multiple_of(core * ye, 8), ye)
    sib_rows = pl.ds(pl.multiple_of((1 - core) * ye, 8), ye)
    zero_pads(k0, d1, d2, k1, f1, f2)
    windows = ((g0, own_b, sib_b, REACH_XB, 0, 0), (k0, own_k, sib_k, REACH_X, REACH_XB, bx))
    for p in range(REACH_X - REACH_XB):
        g0[1 + p] = jnp.zeros((yw, LANES), jnp.float32)
        g0[xw - p] = jnp.zeros((yw, LANES), jnp.float32)

    def halos(from_even, from_odd, rows):
        for window, _, _, width, at, _ in windows:
            e, o = from_even[pl.ds(at, width)], from_odd[pl.ds(at, width)]
            window[pl.ds(1 + REACH_X - width, width), rows] = jnp.where(lo_there, jnp.where(even, o, e), 0.0)
            window[pl.ds(1 + REACH_X + bx, width), rows] = jnp.where(hi_there, jnp.where(even, e, o), 0.0)

    for window, own, sib, _, _, _ in windows:
        window[pl.ds(1 + REACH_X, bx), own_rows] = own[...]
        window[pl.ds(1 + REACH_X, bx), sib_rows] = sib[...]
    halos(even_own, odd_own, own_rows)
    for copy in arrivals:
        copy.wait()
    halos(even_sib, odd_sib, sib_rows)
    for window, _, _, width, at_d, at_z in windows:
        for p in range(bx):
            at = 1 + REACH_X + p
            window[at] = jnp.where(halo_lanes, jnp.where(z_there, strip(z_in, at_z + p), 0.0), window[at])
        for p in range(width):
            plus, minus = strip(dp_in, at_d + p), strip(dm_in, at_d + p)
            low = jnp.where(core == 0, minus, plus)
            high = jnp.where(core == 0, plus, minus)
            at = 1 + REACH_X - width + p
            window[at] = jnp.where(halo_lanes, jnp.where(z_there & lo_there, low, 0.0), window[at])
            at = 1 + REACH_X + bx + p
            window[at] = jnp.where(halo_lanes, jnp.where(z_there & hi_there, high, 0.0), window[at])

    grid = Grid(xw, yw, LANES, 1, 1, False, 8)

    def first(at, here, inverse):
        scaled = g0[here] * inverse
        g0[here] = scaled
        d1[here] = FACTORS[0][1] * scaled

    grid.setup(k0, cx, cy, cz, iv, ds, 1.0, first)
    own0 = 1 + REACH_X - WIN0
    wide0 = bx + 2 * WIN0
    copies = []

    def send(source, start, count, target):
        copy = pltpu.make_async_copy(source.at[pl.ds(start, count)], target, sems.at[len(copies)])
        copy.start()
        copies.append(copy)

    send(cx, own0 - 1, wide0 + 1, o_cx)
    send(cy, own0, wide0, o_cy)
    send(cz, own0, wide0, o_cz)
    send(iv, own0, wide0, o_iv)
    send(g0, own0, wide0, o_g0)

    def restrict(source, target, tmp, x_count, at, y_first, y_rows, shift):
        for i in range(x_count):
            j = i % tmp.shape[0]
            tmp[j] = source[at + 2 * i] + source[at + 2 * i + 1]
            v = tmp[j, pl.ds(y_first, y_rows // 2, stride=2)] + tmp[j, pl.ds(y_first + 1, y_rows // 2, stride=2)]
            target(i, 0.125 * pair_z(v, shift, LANES))

    x1, y1 = xw // 2, yw // 2

    def put_k1(i, v):
        k1[1 + i] = v

    def put_b1(i, v):
        h0[1 + i] = v

    restrict(k0, put_k1, half_y, x1, 1, 0, yw, 1)
    coeffs = (cx, cy, cz, iv)

    def second(here, v, value, direction):
        g[here] = value
        d2[here] = direction

    grid.step(coeffs, d1, g0, *FACTORS[1], second)

    def third(here, v, value, direction):
        g[here] = value
        k0[here] = d1[here] + v + direction
        d1[here] = direction

    grid.step(coeffs, d2, g, *FACTORS[2], third)
    send(k0, own0, wide0, o_w)

    def residual(here, v, value, direction):
        g[here] = value * ds[here]

    grid.step(coeffs, d1, g, 0.0, None, residual)

    restrict(g, put_b1, half_y, x1, 1, 0, yw, 1)
    grid1 = Grid(x1, y1, LANES, 1, 2, False, geo["chunk1"])

    def first1(at, here, inverse):
        scaled = 4.0 * (h0[here] * inverse)
        h0[here] = scaled
        f1[here] = FACTORS[0][1] * scaled

    grid1.setup(k1, ex, ey, ez, ei, es, 0.25, first1)
    own1 = 1 + REACH_X // 2 - WIN1
    wide1 = bx // 2 + 2 * WIN1
    send(ex, own1 - 1, wide1 + 1, p_cx)
    send(ey, own1, wide1, p_cy)
    send(ez, own1, wide1, p_cz)
    send(ei, own1, wide1, p_iv)
    send(h0, own1, wide1, p_g0)
    coeffs1 = (ex, ey, ez, ei)

    def second1(here, v, value, direction):
        h[here] = value
        f2[here] = direction

    grid1.step(coeffs1, f1, h0, *FACTORS[1], second1)

    def third1(here, v, value, direction):
        h[here] = value
        u1[here] = f1[here] + v + direction
        f1[here] = direction

    grid1.step(coeffs1, f2, h, *FACTORS[2], third1)
    send(u1, own1, wide1, p_w)
    mine = 1 + REACH_X // 2
    last = mine + bx // 2
    for source, low, high, at, count in ((u1, mine + 1, last - WIN1, 0, 5), (h0, mine + 3, last - 5, 5, 2)):
        low, high = source[pl.ds(low, count)], source[pl.ds(high, count)]
        even_out[pl.ds(at, count)] = jnp.where(even, high, low)
        odd_out[pl.ds(at, count)] = jnp.where(even, low, high)

    def residual1(here, v, value, direction):
        h[here] = value * es[here]

    grid1.step(coeffs1, f1, h, 0.0, None, residual1)

    place = lax.rem(2 * iz + core, 8)
    x2, y2 = bx // 4, geo["by"] // 2
    row, column = rows_of((LANES, LANES)), lanes_of((LANES, LANES))
    pick = (row == HALF * core + 4 * lax.rem(column, 16)).astype(jnp.float32)
    slot = lanes_of((y2, LANES)) // 16
    for f, source in enumerate((h, k1)):
        boxes = []
        restrict(source, lambda i, v, boxes=boxes: boxes.append(v), half_y1, x2, 1 + REACH_X // 2, geo["oy"] // 2, 2 * y2, 2)
        stacked = jnp.concatenate(boxes, axis=0)
        picked = jnp.dot(stacked, pick, precision=lax.Precision.HIGHEST, preferred_element_type=jnp.float32)
        packed = jnp.zeros((y2, LANES), jnp.float32)
        for p in range(x2):
            packed = jnp.where(slot == lax.rem(p + place, 8), picked[p * y2:(p + 1) * y2], packed)
        packed_out[f] = packed
    for copy in copies:
        copy.wait()


def up_kernel(geo, *refs):
    refs = list(refs)

    def take(count):
        taken = refs[:count]
        del refs[:count]
        return taken

    gathered = take(2 if geo["packed"] else 1)
    from_even, from_odd = take(2)
    in0, in1 = take(6), take(6)
    o_send, o_u, o_r = take(3)
    k2, cx2, cy2, cz2, iv2, ds2, g02, g2, da2, db2, w2, e2 = take(12)
    k3, cx3, cy3, cz3, iv3, ds3, g03, g3, da3, db3, w3, e3 = take(12)
    k4, cx4, cy4, cz4, iv4, g04, g4, da4, db4, e4 = take(10)
    cx1, cy1, cz1, iv1, g01, w1, u1, g1, da1, db1, e1 = take(11)
    cx0, cy0, cz0, iv0, g00, w0, u0, g0, da0, db0 = take(10)
    e2_wide, sems = take(2)
    core = core_of()
    ix, nx = lax.axis_index("gx"), lax.axis_size("gx")
    iz, nz = lax.axis_index("gz"), lax.axis_size("gz")
    yp = lax.axis_index("gy") // 2
    bx, by, yw = geo["bx"], geo["by"], geo["yw"]
    x2, y2, z2 = geo["x2"], geo["y2"], geo["z2"]
    wide0, wide1 = bx + 2 * WIN0, bx // 2 + 2 * WIN1

    copies = []
    for sources, targets, wide in ((in1, (cx1, cy1, cz1, iv1, g01, w1), wide1), (in0, (cx0, cy0, cz0, iv0, g00, w0), wide0)):
        for i, (source, target) in enumerate(zip(sources, targets)):
            there = target.at[pl.ds(0, wide + 1)] if i == 0 else target.at[pl.ds(1, wide)]
            copy = pltpu.make_async_copy(source, there, sems.at[len(copies)])
            copy.start()
            copies.append(copy)

    zero_pads(k2, da2, db2, e2, k3, da3, db3, e3, k4, da4, db4, e4, u1, da1, db1, u0, da0, db0)

    if geo["packed"]:
        slot = lanes_of((y2, LANES)) // 16
        for jx in range(nx):
            gx = lax.bitwise_xor(ix, jx)
            for f, target in ((0, g02), (1, k2)):
                for p in range(8):
                    merged = jnp.zeros((y2, LANES), jnp.float32)
                    for jz in range(nz):
                        gz = lax.bitwise_xor(iz, jz)
                        for source, cc in ((gathered[0], core), (gathered[1], 1 - core)):
                            place = 2 * gz + cc
                            merged = jnp.where(slot == lax.rem(p + place, 8), source[jx, jz, f], merged)
                    target[1 + 8 * gx + p] = pltpu.roll(merged, (LANES - 16 * p) % LANES, 1)
    else:
        g02[pl.ds(1, x2)] = gathered[0][0]
        k2[pl.ds(1, x2)] = gathered[0][1]

    def descend(grid, level, k, cx, cy, cz, iv, ds, g0, first_target):
        def first(at, here, inverse):
            scaled = 4.0**level * (g0[here] * inverse)
            g0[here] = scaled
            first_target[here] = FACTORS[0][1] * scaled

        grid.setup(k, cx, cy, cz, iv, ds, 0.25**level, first)

    def pre(grid, level, k, cx, cy, cz, iv, ds, g0, g, da, db, w):
        descend(grid, level, k, cx, cy, cz, iv, ds, g0, da)
        coeffs = (cx, cy, cz, iv)

        def second(here, v, value, direction):
            g[here] = value
            db[here] = direction

        grid.step(coeffs, da, g0, *FACTORS[1], second)

        def third(here, v, value, direction):
            g[here] = value
            w[here] = da[here] + v + direction
            da[here] = direction

        grid.step(coeffs, db, g, *FACTORS[2], third)

        def residual(here, v, value, direction):
            g[here] = value * ds[here]

        grid.step(coeffs, da, g, 0.0, None, residual)

    def post(grid, coeffs, g0, u, g, da, db, result):
        def one(here, v, value, direction):
            g[here] = value
            da[here] = direction

        grid.step(coeffs, u, g0, *FACTORS[0], one)

        def two(here, v, value, direction):
            g[here] = value
            db[here] = direction

        grid.step(coeffs, da, g, *FACTORS[1], two)

        def three(here, v, value, direction):
            g[here] = value
            result[here] = u[here] + da[here] + v + direction
            da[here] = direction

        grid.step(coeffs, db, g, *FACTORS[2], three)

    def restrict(fine, coarse, count, shift):
        for i in range(count):
            v = fine[1 + 2 * i] + fine[2 + 2 * i]
            coarse[1 + i] = 0.125 * pair_z(pair_y(v, shift, y2), shift, z2)

    def prolong(coarse, w, target, count, shift):
        for i in range(count):
            middle = 0.75 * coarse[1 + i]
            for j, side in ((0, coarse[i]), (1, coarse[2 + i])):
                v = spread_y(middle + 0.25 * side, shift, y2)
                target[1 + 2 * i + j] = w[1 + 2 * i + j] + spread_z(v, shift, z2, True)

    def size_of(x):
        planes = max(1, 32 // ((y2 // 8) * (z2 // LANES)))
        return min(x, planes)

    x3, x4 = x2 // 2, x2 // 4
    grid2 = Grid(x2, y2, z2, 1, 1, True, size_of(x2))
    grid3 = Grid(x3, y2, z2, 2, 2, True, size_of(x3))
    grid4 = Grid(x4, y2, z2, 4, 4, True, size_of(x4))
    pre(grid2, 2, k2, cx2, cy2, cz2, iv2, ds2, g02, g2, da2, db2, w2)
    restrict(k2, k3, x3, 1)
    restrict(g2, g03, x3, 1)
    pre(grid3, 3, k3, cx3, cy3, cz3, iv3, ds3, g03, g3, da3, db3, w3)
    restrict(k3, k4, x4, 2)
    restrict(g3, g04, x4, 2)
    descend(grid4, 4, k4, cx4, cy4, cz4, iv4, None, g04, da4)
    e4[pl.ds(1, x4)] = da4[pl.ds(1, x4)]
    for sweep in range(1, COARSE_STEPS):
        src, dst = (da4, db4) if sweep % 2 else (db4, da4)

        def coarse(here, v, value, direction):
            g4[here] = value
            dst[here] = direction
            e4[here] = e4[here] + direction

        grid4.step((cx4, cy4, cz4, iv4), src, g04 if sweep == 1 else g4, *COARSE_FACTORS[sweep], coarse)
    prolong(e4, w3, e3, x4, 2)
    post(grid3, (cx3, cy3, cz3, iv3), g03, e3, g3, da3, db3, w3)
    e3[pl.ds(1, x3)] = w3[pl.ds(1, x3)]
    prolong(e3, w2, e2, x3, 1)
    post(grid2, (cx2, cy2, cz2, iv2), g02, e2, g2, da2, db2, w2)

    pad_y = geo["pad_y"]
    if pad_y:
        e2_wide[...] = jnp.zeros(e2_wide.shape, jnp.float32)
    else:
        edge = jnp.zeros((4,) + e2_wide.shape[1:], jnp.float32)
        e2_wide[pl.ds(0, 4)] = edge
        e2_wide[pl.ds(x2 + 4, 4)] = edge
    e2_wide[pl.ds(4, x2), pl.ds(pad_y, y2)] = w2[pl.ds(1, x2)]
    x2w, y2w = bx // 4 + 8, yw // 4
    cells, lane = rows_of((z2, LANES)), lanes_of((z2, LANES))
    shifted = jnp.where(core == 0, jnp.where(lane >= 104, -32, 0), jnp.where(lane < 24, 32, 0))
    pick = (cells == 32 * iz + lane // 4 + shifted).astype(jnp.float32)
    start = (bx // 4) * ix
    rows = pl.ds(pl.multiple_of(8 * yp, 8), y2w) if pad_y else pl.ds(0, y2w)
    window = e2_wide[pl.ds(start, x2w), rows].reshape(x2w * y2w, z2)
    window = jnp.dot(window, pick, precision=lax.Precision.HIGHEST, preferred_element_type=jnp.float32)
    window = window.reshape(x2w, y2w, LANES)

    def place_rows(target, plane, v, count):
        row = rows_of(v.shape)
        low = jnp.where(row >= 1, pltpu.roll(v, 1, 0), 0.0)
        high = jnp.where(row < count - 1, pltpu.roll(v, count - 1, 0), 0.0)
        target[plane, pl.ds(0, count, stride=2)] = 0.75 * v + 0.25 * low
        target[plane, pl.ds(1, count, stride=2)] = 0.75 * v + 0.25 * high

    for copy in copies[:6]:
        copy.wait()
    even, last1 = lax.rem(ix, 2) == 0, 1 + WIN1 + bx // 2
    for target, low, high, at, count in ((w1, 1, last1 + 1, 0, 5), (g01, 2, last1 + 3, 5, 2)):
        e, o = from_even[pl.ds(at, count)], from_odd[pl.ds(at, count)]
        low, high = pl.ds(low, count), pl.ds(high, count)
        target[low] = jnp.where(ix > 0, jnp.where(even, o, e), target[low])
        target[high] = jnp.where(ix < nx - 1, jnp.where(even, e, o), target[high])
    for plane in range(wide1):
        j = plane // 2
        v = 0.75 * window[j + 1] + 0.25 * window[j + 2 if plane % 2 else j]
        place_rows(u1, 1 + plane, spread_z(v, 2, LANES, False), y2w)
    grid1 = Grid(wide1, yw // 2, LANES, 1, 2, False, geo["chunk1"])

    def start1(at):
        here = pl.ds(at, grid1.size)
        u1[here] = jnp.where(iv1[here] > 0.0, w1[here] + u1[here], 0.0)

    chunks(wide1, start1, grid1.size)
    post(grid1, (cx1, cy1, cz1, iv1), g01, u1, g1, da1, db1, e1)

    for copy in copies[6:]:
        copy.wait()
    grid0 = Grid(wide0, yw, LANES, 1, 1, False, 8)

    def fill(i, carry):
        at = WIN1 + 1 - WIN0 // 2 + i
        middle = 0.75 * e1[at]
        for j, side in ((0, e1[at - 1]), (1, e1[at + 1])):
            place_rows(u0, 1 + 2 * i + j, spread_z(middle + 0.25 * side, 1, LANES, False), yw // 2)
        return carry

    lax.fori_loop(0, wide0 // 2, fill, 0, unroll=4)

    def start0(at):
        here = pl.ds(at, grid0.size)
        u0[here] = jnp.where(iv0[here] > 0.0, w0[here] + u0[here], 0.0)

    chunks(wide0, start0, grid0.size)
    coeffs0 = (cx0, cy0, cz0, iv0)
    post(grid0, coeffs0, g00, u0, g0, da0, db0, w0)

    def residual(here, v, value, direction):
        g0[here] = value / iv0[here]

    grid0.step(coeffs0, da0, g0, 0.0, None, residual, 1 + WIN0, bx)
    own = pl.ds(1 + WIN0, bx)
    own_rows = pl.ds(pl.multiple_of(geo["oy"] + core * by, 8), by)
    sib_rows = pl.ds(pl.multiple_of(geo["oy"] + (1 - core) * by, 8), by)
    mine = lanes_of((bx, by, LANES)) // HALF == core
    o_send[...] = jnp.where(mine, w0[own, sib_rows], pltpu.roll(g0[own, sib_rows], HALF, 2))
    o_u[...] = w0[own, own_rows]
    o_r[...] = g0[own, own_rows]


def merge_kernel(u_ref, r_ref, other, u_out, r_out):
    v = other[...]
    mine = lanes_of(v.shape) // HALF == core_of()
    u_out[...] = jnp.where(mine, u_ref[...], v)
    r_out[...] = jnp.where(mine, r_ref[...], pltpu.roll(v, HALF, 2))


PARAMS = pltpu.CompilerParams(vmem_limit_bytes=60 * 1024 * 1024)


def array(*shape):
    return jax.ShapeDtypeStruct(shape, jnp.float32)


def on_device(right_side, conductivity):
    bx, by, bz = right_side.shape
    nx, ny, nz = (lax.axis_size(axis) for axis in AXES)
    pairs = ny // 2
    ix, iy, iz = (lax.axis_index(axis) for axis in AXES)
    core = iy % 2

    def index(x, p, c, z):
        return ((x % nx) * ny + (p % pairs) * 2 + c) * nz + z % nz

    every = [(x, p, z) for x in range(nx) for p in range(pairs) for z in range(nz)]

    def sibling(v):
        return lax.ppermute(v, "gy", [(i, i ^ 1) for i in range(ny)])

    def xor(v, axis, k):
        return lax.ppermute(v, axis, [(i, i ^ k) for i in range(lax.axis_size(axis))])

    def paired(v, first):
        perm = [(i, i) for i in range(nx)]
        for i in range(first, nx - 1, 2):
            perm[i], perm[i + 1] = (i, i + 1), (i + 1, i)
        return lax.ppermute(v, "gx", perm)

    def facing(v, dx):
        perm = {}
        for x, p, z in every:
            if z > 0 and 0 <= x + dx < nx:
                a, b = index(x, p, 0, z), index(x + dx, p, 1, z - 1)
                perm[a], perm[b] = b, a
        return lax.ppermute(v, AXES, [(i, perm.get(i, i)) for i in range(nx * ny * nz)])

    own_b, own_k, ye = right_side, conductivity, by
    if ny > 2:
        near = []
        far = []
        for p in range(pairs):
            near += [(2 * p, 2 * ((p - 1) % pairs) + 1), (2 * ((p - 1) % pairs) + 1, 2 * p)]
            far += [(2 * p, 2 * ((p + 1) % pairs)), (2 * p + 1, 2 * ((p - 1) % pairs) + 1)]
        there = jnp.where(core == 0, iy > 0, iy < ny - 1)

        def widened(v):
            one = jnp.where(there, lax.ppermute(v, "gy", near), 0.0)
            two = jnp.where(there, lax.ppermute(v, "gy", far), 0.0)
            return jnp.where(core == 0, jnp.concatenate([two, one, v], 1), jnp.concatenate([v, one, two], 1))

        own_b, own_k = widened(own_b), widened(own_k)
        ye = 3 * by
    yw = 2 * ye
    xw = bx + 2 * REACH_X
    geo = dict(
        bx=bx, by=by, ye=ye, yw=yw, xw=xw, oy=(yw - 2 * by) // 2, chunk1=14 if yw == 32 else 4,
        packed=pairs == 1 and 32 * nz == LANES, x2=bx // 4 * nx, y2=by // 4 * ny, z2=bz // 4 * nz,
        pad_y=(yw // 4 - by // 2) // 2,
    )

    sib_b, sib_k = sibling(own_b), sibling(own_k)
    even = ix % 2 == 0
    high = jnp.concatenate([own_b[bx - REACH_XB:], own_k[bx - REACH_X:]], 0)
    low = jnp.concatenate([own_b[:REACH_XB], own_k[:REACH_X]], 0)
    even_own = paired(jnp.where(even, high, low), 0)
    odd_own = paired(jnp.where(even, low, high), 1)
    m, md = -(-2 * bx // SLOTS), -(-(REACH_X + REACH_XB) // SLOTS)
    z_send, dp_send, dm_send = pl.pallas_call(
        functools.partial(pack_kernel, geo),
        out_shape=[array(m, yw, LANES), array(md, yw, LANES), array(md, yw, LANES)],
        compiler_params=PARAMS, name="pack_z",
        cost_estimate=pl.CostEstimate(flops=4_000_000, bytes_accessed=8_000_000, transcendentals=0),
    )(own_b, own_k, sib_b, sib_k)
    z_in, dp_in, dm_in = facing(z_send, 0), facing(dp_send, 1), facing(dm_send, -1)
    even_sib, odd_sib = sibling(even_own), sibling(odd_own)

    wide0, wide1 = bx + 2 * WIN0, bx // 2 + 2 * WIN1
    x1, y1 = xw // 2, yw // 2
    some0 = pltpu.VMEM((xw + 2, yw, LANES), jnp.float32)
    some1 = pltpu.VMEM((x1 + 2, y1, LANES), jnp.float32)
    passed0 = [array(wide0 + (i == 0), yw, LANES) for i in range(6)]
    passed1 = [array(wide1 + (i == 0), y1, LANES) for i in range(6)]
    vmem, anywhere = pl.BlockSpec(memory_space=pltpu.VMEM), pl.BlockSpec(memory_space=pl.ANY)
    edge = 7
    down = pl.pallas_call(
        functools.partial(down_kernel, geo),
        out_shape=[array(2, by // 2, LANES), array(edge, y1, LANES), array(edge, y1, LANES)] + passed0 + passed1,
        in_specs=[vmem] * 6 + [anywhere] * 5,
        out_specs=[vmem] * 3 + [anywhere] * 12,
        scratch_shapes=[pltpu.VMEM(v.shape, jnp.float32) for v in (even_sib, odd_sib, z_in, dp_in, dm_in)]
        + [some0] * 10 + [some1] * 11
        + [pltpu.VMEM((6, yw, LANES), jnp.float32), pltpu.VMEM((6, y1, LANES), jnp.float32)]
        + [pltpu.SemaphoreType.DMA((12,)), pltpu.SemaphoreType.DMA((5,))],
        compiler_params=PARAMS, name="down",
    )(own_b, own_k, sib_b, sib_k, even_own, odd_own, even_sib, odd_sib, z_in, dp_in, dm_in)
    packed, even_send, odd_send, passed = down[0], down[1], down[2], down[3:]
    from_even, from_odd = paired(even_send, 0), paired(odd_send, 1)

    if geo["packed"]:
        along_z = jnp.stack([packed] + [xor(packed, "gz", j) for j in range(1, nz)])
        along_x = jnp.stack([along_z] + [xor(along_z, "gx", j) for j in range(1, nx)])
        gathered = (along_x, sibling(along_x))
    else:
        pieces = lax.all_gather(packed, AXES).reshape(nx, pairs, 2, nz, 2, by // 2, 8, 16)
        order = (jnp.arange(8) + 2 * jnp.arange(nz)[:, None, None] + jnp.arange(2)[:, None]) % 8
        order = jnp.transpose(order, (1, 0, 2))[None, None, :, :, None, None, :, None]
        pieces = jnp.take_along_axis(pieces, order, axis=6)
        gathered = (jnp.transpose(pieces, (4, 0, 6, 1, 5, 3, 2, 7)).reshape(2, geo["x2"], geo["y2"], geo["z2"]),)

    def level(planes, rows, lanes):
        return pltpu.VMEM((planes + 2, rows, lanes), jnp.float32)

    x2, y2, z2 = geo["x2"], geo["y2"], geo["z2"]
    send, keep_u, keep_r = pl.pallas_call(
        functools.partial(up_kernel, geo),
        out_shape=[array(bx, by, LANES)] * 3,
        in_specs=[vmem] * (len(gathered) + 2) + [anywhere] * 12,
        scratch_shapes=[level(x2, y2, z2)] * 12 + [level(x2 // 2, y2, z2)] * 12 + [level(x2 // 4, y2, z2)] * 10
        + [level(wide1, y1, LANES)] * 11 + [level(wide0, yw, LANES)] * 10
        + [pltpu.VMEM((x2 + 8, y2 + 2 * geo["pad_y"], z2), jnp.float32), pltpu.SemaphoreType.DMA((12,))],
        compiler_params=PARAMS, name="up",
    )(*gathered, from_even, from_odd, *passed)
    return pl.pallas_call(
        merge_kernel, out_shape=[array(bx, by, LANES)] * 2, compiler_params=PARAMS, name="merge",
    )(keep_u, keep_r, sibling(send))


def solution(mesh):
    specs = (P(*AXES), P(*AXES))
    return jax.shard_map(on_device, mesh=mesh, in_specs=specs, out_specs=specs, check_vma=False)
```

time: 847 us -> 76.3 us (0.09)
  the two profiles are of different devices: /device:TPU:0 before, /device:TPU:3 now
where the time goes in v1:
time: 76.3 us; the launch traced here: 75.8 us
  starting transfers between devices  32.8 us (43%)
  Pallas kernels  24.9 us (33%)
  waiting for transfers between devices  12.1 us (16%)
  local copies, waits for them, and re-layouts  5.13 us (7%)
  between operations  0.94 us (1%)
    ppermute x3, starting transfers between devices, facing(): lax.ppermute(v, AXES, [(i, perm.get(i, i)) for i in range(nx * ny * nz)])  12.1 us
    pallas_call x1, Pallas kernels, on_device(): pl.pallas_call(functools.partial(up_kernel, geo), out_shape=[array(bx, by...  10.7 us
    pallas_call x1, Pallas kernels, on_device(): pl.pallas_call(functools.partial(down_kernel, geo), out_shape=[array(2, b...  9.85 us
    ppermute x6, starting transfers between devices, sibling(): return lax.ppermute(v, 'gy', [(i, i ^ 1) for i in range(ny)])  8.28 us
    ppermute x6, starting transfers between devices, xor(): lax.ppermute(v, axis, [(i, i ^ k) for i in range(lax.axis_size(axis))])  6.3 us
    ppermute x4, starting transfers between devices, paired(): return lax.ppermute(v, 'gx', perm)  6.07 us
    ppermute x3, waiting for transfers between devices, facing(): lax.ppermute(v, AXES, [(i, perm.get(i, i)) for i in range(nx * ny * nz)])  4.23 us
    unnamed x36, local copies, waits for them, and re-layouts  4.19 us
  transfers between devices with their start and end apart: 19, of which 9 were waited for; matrix products, arithmetic and copies ran while one was open for 1% of the time, Pallas kernels for 3%

profile of v1, /device:TPU:3, one launch (start us, length us, event | category | flops | bytes accessed | tf_op | source)
XLA Modules:
  0.0 75.8 jit_solution(7433154908697439150)
XLA Ops:
  0.6 0.7 collective-permute-start
  1.4 0.1 collective-permute-start.1
  1.5 0.9 %fusion.3 = (f32[9,16,128]{2,1,0:T(8,128)S(1)}, f32[9,16,128]{2,1,0:T(8,128)S(1)}) fusion(f32[32,16,128]{2,1,0:T(8,128)} %refs_0_.1), kind=kLoop, calls=%fused_computation.7 | loop fusion | bytes 294912 | tf_op jit(solution)/shard_map/slice | solution.py:667
  2.5 3.1 %collective-permute-start.3 = (f32[21,16,128]{2,1,0:T(8,128)S(1)}, f32[21,16,128]{2,1,0:T(8,128)S(1)}, u32[]{:S(2)}, u32[]{:S(2)}) collective-permute-start(f32[21,16,128]{2,1,0:T(8,128)S(1)} %get-tuple-element.44), channel_id=1, source_target_pairs={{0,0},{8,16},{16,8},{24,24},{1,1},{9,17},{17,9},{25,25},{2,2},{10,... | collective-permute-start | bytes 516104 | tf_op jit(solution)/shard_map/ppermute | solution.py:631
  5.7 0.7 copy-done.1
  6.4 0.7 copy-done.2
  7.1 2.4 %pack_z.1 = (f32[11,32,128]{2,1,0:T(8,128)}, f32[4,32,128]{2,1,0:T(8,128)}, f32[4,32,128]{2,1,0:T(8,128)}) custom-call(f32[32,16,128]{2,1,0:T(8,128)} %refs_0_.1, f32[32,16,128]{2,1,0:T(8,128)} %refs_1_.1, f32[32,16,128]{2,1,0:T(8,128)} %copy-done.1, f32[32,16,128]{2,1,0:T(8,128)} %copy-done.2), custom_call_target="tpu_custom_call" | custom-call | flops 4000000 | bytes 8000000 | tf_op jit(solution)/shard_map/pack_z/pallas_call | solution.py:672
  9.5 3.8 %collective-permute-start.6 = (f32[11,32,128]{2,1,0:T(8,128)}, f32[11,32,128]{2,1,0:T(8,128)S(1)}, u32[]{:S(2)}, u32[]{:S(2)}) collective-permute-start(f32[11,32,128]{2,1,0:T(8,128)} %get-tuple-element.23), channel_id=1, source_target_pairs={{0,0},{1,4},{2,5},{3,6},{4,1},{5,2},{6,3},{7,7},{8,8},{9,12},{10,1... | collective-permute-start | bytes 540680 | tf_op jit(solution)/shard_map/ppermute | solution.py:639
  13.4 0.5 collective-permute-start.4
  13.9 5.0 %collective-permute-start.7 = (f32[4,32,128]{2,1,0:T(8,128)}, f32[4,32,128]{2,1,0:T(8,128)S(1)}, u32[]{:S(2)}, u32[]{:S(2)}) collective-permute-start(f32[4,32,128]{2,1,0:T(8,128)} %get-tuple-element.24), channel_id=1, source_target_pairs={{0,0},{1,12},{2,13},{3,14},{4,4},{5,5},{6,6},{7,7},{8,8},{9,20},{1... | collective-permute-start | bytes 196616 | tf_op jit(solution)/shard_map/ppermute | solution.py:639
  18.9 3.3 %collective-permute-start.8 = (f32[4,32,128]{2,1,0:T(8,128)}, f32[4,32,128]{2,1,0:T(8,128)S(1)}, u32[]{:S(2)}, u32[]{:S(2)}) collective-permute-start(f32[4,32,128]{2,1,0:T(8,128)} %get-tuple-element.25), channel_id=1, source_target_pairs={{0,0},{1,1},{2,2},{3,3},{4,9},{5,10},{6,11},{7,7},{8,8},{9,4},{10,... | collective-permute-start | bytes 196616 | tf_op jit(solution)/shard_map/ppermute | solution.py:639
  22.2 4.2 %collective-permute-done.8.refs_10_ = f32[4,32,128]{2,1,0:T(8,128)S(1)} collective-permute-done((f32[4,32,128]{2,1,0:T(8,128)}, f32[4,32,128]{2,1,0:T(8,128)S(1)}, u32[]{:S(2)}, u32[]{:S(2)}) %collective-permute-start.8) | collective-permute-done | bytes 65568 | tf_op jit(solution)/shard_map/ppermute | solution.py:639
  26.5 0.6 copy-done.12
  27.2 0.7 copy-done.5
  27.9 9.8 %down.1 = (f32[2,8,128]{2,1,0:T(8,128)}, f32[7,16,128]{2,1,0:T(8,128)}, f32[7,16,128]{2,1,0:T(8,128)}, f32[41,32,128]{2,1,0:T(8,128)}, f32[40,32,128]{2,1,0:T(8,...) custom-call(f32[32,16,128]{2,1,0:T(8,128)} %refs_0_.1, ...), custom_call_target="tpu_custom_call" | custom-call | tf_op jit(solution)/shard_map/down/pallas_call | solution.py:689
  37.9 2.5 %collective-permute-start.10 = (f32[2,8,128]{2,1,0:T(8,128)}, f32[2,8,128]{2,1,0:T(8,128)S(1)}, u32[]{:S(2)}, u32[]{:S(2)}) collective-permute-start(f32[2,8,128]{2,1,0:T(8,128)} %get-tuple-element.26), channel_id=1, source_target_pairs={{0,2},{1,3},{2,0},{3,1},{4,6},{5,7},{6,4},{7,5},{8,10},{9,11},{10,... | collective-permute-start | bytes 24584 | tf_op jit(solution)/shard_map/ppermute | solution.py:625
  40.3 1.1 %collective-permute-start.9 = (f32[2,8,128]{2,1,0:T(8,128)}, f32[2,8,128]{2,1,0:T(8,128)S(1)}, u32[]{:S(2)}, u32[]{:S(2)}) collective-permute-start(f32[2,8,128]{2,1,0:T(8,128)} %get-tuple-element.26), channel_id=1, source_target_pairs={{0,1},{1,0},{2,3},{3,2},{4,5},{5,4},{6,7},{7,6},{8,9},{9,8},{10,11... | collective-permute-start | bytes 24584 | tf_op jit(solution)/shard_map/ppermute | solution.py:625
  41.4 1.0 %collective-permute-done.11 = f32[2,8,128]{2,1,0:T(8,128)S(1)} collective-permute-done((f32[2,8,128]{2,1,0:T(8,128)}, f32[2,8,128]{2,1,0:T(8,128)S(1)}, u32[]{:S(2)}, u32[]{:S(2)}) %collective-permute-start.11) | collective-permute-done | bytes 8224 | tf_op jit(solution)/shard_map/ppermute | solution.py:625
  42.4 0.9 %collective-permute-done.9 = f32[2,8,128]{2,1,0:T(8,128)S(1)} collective-permute-done((f32[2,8,128]{2,1,0:T(8,128)}, f32[2,8,128]{2,1,0:T(8,128)S(1)}, u32[]{:S(2)}, u32[]{:S(2)}) %collective-permute-start.9) | collective-permute-done | bytes 8224 | tf_op jit(solution)/shard_map/ppermute | solution.py:625
  43.4 2.6 %collective-permute-start.14 = (f32[4,2,8,128]{3,2,1,0:T(8,128)S(1)}, f32[4,2,8,128]{3,2,1,0:T(8,128)S(1)}, u32[]{:S(2)}, u32[]{:S(2)}) collective-permute-start(f32[4,2,8,128]{3,2,1,0:T(8,128)S(1)} %get-tuple-element.51), channel_id=1, source_target_pairs={{0,24},{8,16},{16,8},{24,0},{1,25},{9,17},{17,9},{25,1},{2,26},{10... | collective-permute-start | bytes 98312 | tf_op jit(solution)/shard_map/ppermute | solution.py:625
  46.0 0.1 collective-permute-done.13
  46.2 1.5 %collective-permute-done.14 = f32[4,2,8,128]{3,2,1,0:T(8,128)S(1)} collective-permute-done((f32[4,2,8,128]{3,2,1,0:T(8,128)S(1)}, f32[4,2,8,128]{3,2,1,0:T(8,128)S(1)}, u32[]{:S(2)}, u32[]{:S(2)}) %collective-permute-start.14) | collective-permute-done | bytes 32800 | tf_op jit(solution)/shard_map/ppermute | solution.py:625
  47.7 4.9 %collective-permute-start.15 = (f32[4,4,2,8,128]{4,3,2,1,0:T(8,128)S(1)}, f32[4,4,2,8,128]{4,3,2,1,0:T(8,128)S(1)}, u32[]{:S(2)}, u32[]{:S(2)}) collective-permute-start(f32[4,4,2,8,128]{4,3,2,1,0:T(8,128)S(1)} %pad_maximum_fusion.2.refs_0_), channel_id=1, source_target_pairs={{0,4},{4,0},{1,5},{5,1},{2,6},{6,2},{3,7},{7,3},{8,12},{12,8},{9,1... | collective-permute-start | bytes 393224 | tf_op jit(solution)/shard_map/ppermute | solution.py:622
  52.6 2.9 %collective-permute-start.17 = (f32[7,16,128]{2,1,0:T(8,128)S(1)}, f32[7,16,128]{2,1,0:T(8,128)S(1)}, u32[]{:S(2)}, u32[]{:S(2)}) collective-permute-start(f32[7,16,128]{2,1,0:T(8,128)S(1)} %copy-done.16), channel_id=1, source_target_pairs={{0,0},{8,16},{16,8},{24,24},{1,1},{9,17},{17,9},{25,25},{2,2},{10,... | collective-permute-start | bytes 172040 | tf_op jit(solution)/shard_map/ppermute | solution.py:631
  55.5 0.1 collective-permute-done.16.refs_2_
  55.6 2.8 %collective-permute-done.17.refs_3_ = f32[7,16,128]{2,1,0:T(8,128)S(1)} collective-permute-done((f32[7,16,128]{2,1,0:T(8,128)S(1)}, f32[7,16,128]{2,1,0:T(8,128)S(1)}, u32[]{:S(2)}, u32[]{:S(2)}) %collective-permute-start.17) | collective-permute-done | bytes 57376 | tf_op jit(solution)/shard_map/ppermute | solution.py:631
  58.4 0.6 copy-done.14
  59.1 10.7 %up.1 = (f32[32,16,128]{2,1,0:T(8,128)}, f32[32,16,128]{2,1,0:T(8,128)}, f32[32,16,128]{2,1,0:T(8,128)}) custom-call(f32[4,4,2,8,128]{4,3,2,1,0:T(8,128)} %copy-done.3, f32[4,4,2,8,128]{4,3,2,1,0:T(8,128)} %copy-done.10, f32[7,16,128]{2,1,0:T(8,128)} %copy-done.13, f32[7,16,128]{2,1,0:T(8,128)} %copy-done.14, f32[41,32,128]{2,1,0:T(8,128)} %get-tuple-element.29.refs_4_, ...), custom_call_target="tpu_custom_call" | custom-call | tf_op jit(solution)/shard_map/up/pallas_call | solution.py:718
  69.8 2.0 %collective-permute-start.18 = (f32[32,16,128]{2,1,0:T(8,128)}, f32[32,16,128]{2,1,0:T(8,128)S(1)}, u32[]{:S(2)}, u32[]{:S(2)}) collective-permute-start(f32[32,16,128]{2,1,0:T(8,128)} %get-tuple-element.43), channel_id=1, source_target_pairs={{0,4},{4,0},{1,5},{5,1},{2,6},{6,2},{3,7},{7,3},{8,12},{12,8},{9,1... | collective-permute-start | bytes 786440 | tf_op jit(solution)/shard_map/ppermute | solution.py:622
  71.8 1.4 %collective-permute-done.18.other = f32[32,16,128]{2,1,0:T(8,128)S(1)} collective-permute-done((f32[32,16,128]{2,1,0:T(8,128)}, f32[32,16,128]{2,1,0:T(8,128)S(1)}, u32[]{:S(2)}, u32[]{:S(2)}) %collective-permute-start.18) | collective-permute-done | bytes 262176 | tf_op jit(solution)/shard_map/ppermute | solution.py:622
  73.2 0.7 copy-done.4
  73.9 1.9 %merge.1 = (f32[32,16,128]{2,1,0:T(8,128)}, f32[32,16,128]{2,1,0:T(8,128)}) custom-call(f32[32,16,128]{2,1,0:T(8,128)} %get-tuple-element.41.u_ref, f32[32,16,128]{2,1,0:T(8,128)} %get-tuple-element.42.r_ref, f32[32,16,128]{2,1,0:T(8,128)} %copy-done.4), custom_call_target="tpu_custom_call" | custom-call | tf_op jit(solution)/shard_map/merge/pallas_call | solution.py:727
  (51 shorter events, 0.8 us)
Async XLA Ops:
  0.6 1.8 %copy-start = (f32[32,16,128]{2,1,0:T(8,128)S(1)}, f32[32,16,128]{2,1,0:T(8,128)}, u32[]{:S(2)}) copy-start(f32[32,16,128]{2,1,0:T(8,128)} %refs_1_.1) | copy-start | bytes 786436
  0.6 5.0 %collective-permute-start = (f32[32,16,128]{2,1,0:T(8,128)}, f32[32,16,128]{2,1,0:T(8,128)S(1)}, u32[]{:S(2)}, u32[]{:S(2)}) collective-permute-start(f32[32,16,128]{2,1,0:T(8,128)} %refs_0_.1), channel_id=1, source_target_pairs={{0,4},{4,0},{1,5},{5,1},{2,6},{6,2},{3,7},{7,3},{8,12},{12,8},{9,1... | collective-permute-start | bytes 786440 | tf_op jit(solution)/shard_map/ppermute | solution.py:622
  1.4 4.3 %collective-permute-start.1 = (f32[32,16,128]{2,1,0:T(8,128)}, f32[32,16,128]{2,1,0:T(8,128)S(1)}, u32[]{:S(2)}, u32[]{:S(2)}) collective-permute-start(f32[32,16,128]{2,1,0:T(8,128)} %refs_1_.1), channel_id=1, source_target_pairs={{0,4},{4,0},{1,5},{5,1},{2,6},{6,2},{3,7},{7,3},{8,12},{12,8},{9,1... | collective-permute-start | bytes 786440 | tf_op jit(solution)/shard_map/ppermute | solution.py:622
  2.5 10.8 %collective-permute-start.3 = (f32[21,16,128]{2,1,0:T(8,128)S(1)}, f32[21,16,128]{2,1,0:T(8,128)S(1)}, u32[]{:S(2)}, u32[]{:S(2)}) collective-permute-start(f32[21,16,128]{2,1,0:T(8,128)S(1)} %get-tuple-element.44), channel_id=1, source_target_pairs={{0,0},{8,16},{16,8},{24,24},{1,1},{9,17},{17,9},{25,25},{2,2},{10,... | collective-permute-start | bytes 516104 | tf_op jit(solution)/shard_map/ppermute | solution.py:631
  5.6 7.8 %collective-permute-start.2 = (f32[21,16,128]{2,1,0:T(8,128)S(1)}, f32[21,16,128]{2,1,0:T(8,128)S(1)}, u32[]{:S(2)}, u32[]{:S(2)}) collective-permute-start(f32[21,16,128]{2,1,0:T(8,128)S(1)} %get-tuple-element.45), channel_id=1, source_target_pairs={{0,8},{8,0},{16,24},{24,16},{1,9},{9,1},{17,25},{25,17},{2,10},{10... | collective-permute-start | bytes 516104 | tf_op jit(solution)/shard_map/ppermute | solution.py:631
  5.7 0.7 copy-start.1
  6.4 0.7 copy-start.2
  9.5 17.0 %collective-permute-start.6 = (f32[11,32,128]{2,1,0:T(8,128)}, f32[11,32,128]{2,1,0:T(8,128)S(1)}, u32[]{:S(2)}, u32[]{:S(2)}) collective-permute-start(f32[11,32,128]{2,1,0:T(8,128)} %get-tuple-element.23), channel_id=1, source_target_pairs={{0,0},{1,4},{2,5},{3,6},{4,1},{5,2},{6,3},{7,7},{8,8},{9,12},{10,1... | collective-permute-start | bytes 540680 | tf_op jit(solution)/shard_map/ppermute | solution.py:639
  13.3 13.2 %copy-start.6 = (f32[21,16,128]{2,1,0:T(8,128)}, f32[21,16,128]{2,1,0:T(8,128)S(1)}, u32[]{:S(2)}) copy-start(f32[21,16,128]{2,1,0:T(8,128)S(1)} %collective-permute-done.3.refs_5_) | copy-start | bytes 516100
  13.3 13.2 %collective-permute-start.5 = (f32[21,16,128]{2,1,0:T(8,128)S(1)}, f32[21,16,128]{2,1,0:T(8,128)S(1)}, u32[]{:S(2)}, u32[]{:S(2)}) collective-permute-start(f32[21,16,128]{2,1,0:T(8,128)S(1)} %collective-permute-done.3.refs_5_), channel_id=1, source_target_pairs={{0,4},{4,0},{1,5},{5,1},{2,6},{6,2},{3,7},{7,3},{8,12},{12,8},{9,1... | collective-permute-start | bytes 516104 | tf_op jit(solution)/shard_map/ppermute | solution.py:622
  13.4 13.1 %copy-start.7 = (f32[21,16,128]{2,1,0:T(8,128)}, f32[21,16,128]{2,1,0:T(8,128)S(1)}, u32[]{:S(2)}) copy-start(f32[21,16,128]{2,1,0:T(8,128)S(1)} %collective-permute-done.2.refs_4_) | copy-start | bytes 516100
  13.4 13.1 %collective-permute-start.4 = (f32[21,16,128]{2,1,0:T(8,128)S(1)}, f32[21,16,128]{2,1,0:T(8,128)S(1)}, u32[]{:S(2)}, u32[]{:S(2)}) collective-permute-start(f32[21,16,128]{2,1,0:T(8,128)S(1)} %collective-permute-done.2.refs_4_), channel_id=1, source_target_pairs={{0,4},{4,0},{1,5},{5,1},{2,6},{6,2},{3,7},{7,3},{8,12},{12,8},{9,1... | collective-permute-start | bytes 516104 | tf_op jit(solution)/shard_map/ppermute | solution.py:622
  13.9 8.3 %collective-permute-start.7 = (f32[4,32,128]{2,1,0:T(8,128)}, f32[4,32,128]{2,1,0:T(8,128)S(1)}, u32[]{:S(2)}, u32[]{:S(2)}) collective-permute-start(f32[4,32,128]{2,1,0:T(8,128)} %get-tuple-element.24), channel_id=1, source_target_pairs={{0,0},{1,12},{2,13},{3,14},{4,4},{5,5},{6,6},{7,7},{8,8},{9,20},{1... | collective-permute-start | bytes 196616 | tf_op jit(solution)/shard_map/ppermute | solution.py:639
  18.9 7.6 %collective-permute-start.8 = (f32[4,32,128]{2,1,0:T(8,128)}, f32[4,32,128]{2,1,0:T(8,128)S(1)}, u32[]{:S(2)}, u32[]{:S(2)}) collective-permute-start(f32[4,32,128]{2,1,0:T(8,128)} %get-tuple-element.25), channel_id=1, source_target_pairs={{0,0},{1,1},{2,2},{3,3},{4,9},{5,10},{6,11},{7,7},{8,8},{9,4},{10,... | collective-permute-start | bytes 196616 | tf_op jit(solution)/shard_map/ppermute | solution.py:639
  22.2 4.3 %copy-start.11 = (f32[4,32,128]{2,1,0:T(8,128)}, f32[4,32,128]{2,1,0:T(8,128)S(1)}, u32[]{:S(2)}) copy-start(f32[4,32,128]{2,1,0:T(8,128)S(1)} %collective-permute-done.7.refs_9_) | copy-start | bytes 196612
  26.5 0.7 copy-start.9
  27.2 0.7 copy-start.5
  37.8 5.5 %copy-start.15 = (f32[2,8,128]{2,1,0:T(8,128)S(1)}, f32[2,8,128]{2,1,0:T(8,128)}, u32[]{:S(2)}) copy-start(f32[2,8,128]{2,1,0:T(8,128)} %get-tuple-element.26) | copy-start | bytes 24580
  37.8 4.6 %collective-permute-start.11 = (f32[2,8,128]{2,1,0:T(8,128)}, f32[2,8,128]{2,1,0:T(8,128)S(1)}, u32[]{:S(2)}, u32[]{:S(2)}) collective-permute-start(f32[2,8,128]{2,1,0:T(8,128)} %get-tuple-element.26), channel_id=1, source_target_pairs={{0,3},{1,2},{2,1},{3,0},{4,7},{5,6},{6,5},{7,4},{8,11},{9,10},{10,... | collective-permute-start | bytes 24584 | tf_op jit(solution)/shard_map/ppermute | solution.py:625
  37.9 4.5 %collective-permute-start.10 = (f32[2,8,128]{2,1,0:T(8,128)}, f32[2,8,128]{2,1,0:T(8,128)S(1)}, u32[]{:S(2)}, u32[]{:S(2)}) collective-permute-start(f32[2,8,128]{2,1,0:T(8,128)} %get-tuple-element.26), channel_id=1, source_target_pairs={{0,2},{1,3},{2,0},{3,1},{4,6},{5,7},{6,4},{7,5},{8,10},{9,11},{10,... | collective-permute-start | bytes 24584 | tf_op jit(solution)/shard_map/ppermute | solution.py:625
  40.3 2.9 %collective-permute-start.9 = (f32[2,8,128]{2,1,0:T(8,128)}, f32[2,8,128]{2,1,0:T(8,128)S(1)}, u32[]{:S(2)}, u32[]{:S(2)}) collective-permute-start(f32[2,8,128]{2,1,0:T(8,128)} %get-tuple-element.26), channel_id=1, source_target_pairs={{0,1},{1,0},{2,3},{3,2},{4,5},{5,4},{6,7},{7,6},{8,9},{9,8},{10,11... | collective-permute-start | bytes 24584 | tf_op jit(solution)/shard_map/ppermute | solution.py:625
  43.3 2.8 %collective-permute-start.13 = (f32[4,2,8,128]{3,2,1,0:T(8,128)S(1)}, f32[4,2,8,128]{3,2,1,0:T(8,128)S(1)}, u32[]{:S(2)}, u32[]{:S(2)}) collective-permute-start(f32[4,2,8,128]{3,2,1,0:T(8,128)S(1)} %get-tuple-element.51), channel_id=1, source_target_pairs={{0,16},{8,24},{16,0},{24,8},{1,17},{9,25},{17,1},{25,9},{2,18},{10... | collective-permute-start | bytes 98312 | tf_op jit(solution)/shard_map/ppermute | solution.py:625
  43.4 2.8 %collective-permute-start.12 = (f32[4,2,8,128]{3,2,1,0:T(8,128)S(1)}, f32[4,2,8,128]{3,2,1,0:T(8,128)S(1)}, u32[]{:S(2)}, u32[]{:S(2)}) collective-permute-start(f32[4,2,8,128]{3,2,1,0:T(8,128)S(1)} %get-tuple-element.51), channel_id=1, source_target_pairs={{0,8},{8,0},{16,24},{24,16},{1,9},{9,1},{17,25},{25,17},{2,10},{10... | collective-permute-start | bytes 98312 | tf_op jit(solution)/shard_map/ppermute | solution.py:625
  43.4 4.2 %collective-permute-start.14 = (f32[4,2,8,128]{3,2,1,0:T(8,128)S(1)}, f32[4,2,8,128]{3,2,1,0:T(8,128)S(1)}, u32[]{:S(2)}, u32[]{:S(2)}) collective-permute-start(f32[4,2,8,128]{3,2,1,0:T(8,128)S(1)} %get-tuple-element.51), channel_id=1, source_target_pairs={{0,24},{8,16},{16,8},{24,0},{1,25},{9,17},{17,9},{25,1},{2,26},{10... | collective-permute-start | bytes 98312 | tf_op jit(solution)/shard_map/ppermute | solution.py:625
  47.6 4.9 %copy-start.17 = (f32[7,16,128]{2,1,0:T(8,128)S(1)}, f32[7,16,128]{2,1,0:T(8,128)}, u32[]{:S(2)}) copy-start(f32[7,16,128]{2,1,0:T(8,128)} %get-tuple-element.27) | copy-start | bytes 172036
  47.6 5.0 %copy-start.16 = (f32[7,16,128]{2,1,0:T(8,128)S(1)}, f32[7,16,128]{2,1,0:T(8,128)}, u32[]{:S(2)}) copy-start(f32[7,16,128]{2,1,0:T(8,128)} %get-tuple-element.28) | copy-start | bytes 172036
  47.7 10.8 %copy-start.3 = (f32[4,4,2,8,128]{4,3,2,1,0:T(8,128)}, f32[4,4,2,8,128]{4,3,2,1,0:T(8,128)S(1)}, u32[]{:S(2)}) copy-start(f32[4,4,2,8,128]{4,3,2,1,0:T(8,128)S(1)} %pad_maximum_fusion.2.refs_0_) | copy-start | bytes 393220
  47.7 10.8 %collective-permute-start.15 = (f32[4,4,2,8,128]{4,3,2,1,0:T(8,128)S(1)}, f32[4,4,2,8,128]{4,3,2,1,0:T(8,128)S(1)}, u32[]{:S(2)}, u32[]{:S(2)}) collective-permute-start(f32[4,4,2,8,128]{4,3,2,1,0:T(8,128)S(1)} %pad_maximum_fusion.2.refs_0_), channel_id=1, source_target_pairs={{0,4},{4,0},{1,5},{5,1},{2,6},{6,2},{3,7},{7,3},{8,12},{12,8},{9,1... | collective-permute-start | bytes 393224 | tf_op jit(solution)/shard_map/ppermute | solution.py:622
  52.6 3.0 %collective-permute-start.16 = (f32[7,16,128]{2,1,0:T(8,128)S(1)}, f32[7,16,128]{2,1,0:T(8,128)S(1)}, u32[]{:S(2)}, u32[]{:S(2)}) collective-permute-start(f32[7,16,128]{2,1,0:T(8,128)S(1)} %copy-done.17), channel_id=1, source_target_pairs={{0,8},{8,0},{16,24},{24,16},{1,9},{9,1},{17,25},{25,17},{2,10},{10... | collective-permute-start | bytes 172040 | tf_op jit(solution)/shard_map/ppermute | solution.py:631
  52.6 5.8 %collective-permute-start.17 = (f32[7,16,128]{2,1,0:T(8,128)S(1)}, f32[7,16,128]{2,1,0:T(8,128)S(1)}, u32[]{:S(2)}, u32[]{:S(2)}) collective-permute-start(f32[7,16,128]{2,1,0:T(8,128)S(1)} %copy-done.16), channel_id=1, source_target_pairs={{0,0},{8,16},{16,8},{24,24},{1,1},{9,17},{17,9},{25,25},{2,2},{10,... | collective-permute-start | bytes 172040 | tf_op jit(solution)/shard_map/ppermute | solution.py:631
  55.6 2.8 %copy-start.13 = (f32[7,16,128]{2,1,0:T(8,128)}, f32[7,16,128]{2,1,0:T(8,128)S(1)}, u32[]{:S(2)}) copy-start(f32[7,16,128]{2,1,0:T(8,128)S(1)} %collective-permute-done.16.refs_2_) | copy-start | bytes 172036
  69.8 3.4 %collective-permute-start.18 = (f32[32,16,128]{2,1,0:T(8,128)}, f32[32,16,128]{2,1,0:T(8,128)S(1)}, u32[]{:S(2)}, u32[]{:S(2)}) collective-permute-start(f32[32,16,128]{2,1,0:T(8,128)} %get-tuple-element.43), channel_id=1, source_target_pairs={{0,4},{4,0},{1,5},{5,1},{2,6},{6,2},{3,7},{7,3},{8,12},{12,8},{9,1... | collective-permute-start | bytes 786440 | tf_op jit(solution)/shard_map/ppermute | solution.py:622
  (5 other events, 3.3 us)

commit v2 on v1

--- a/solution.py
+++ b/solution.py
@@ -1,4 +1,5 @@
 import functools
+import math
 import jax
 import jax.numpy as jnp
 from jax import lax
@@ -20,6 +21,8 @@
 WIN0 = 4
 WIN1 = REACH_X // 2
 SLOTS = LANES // REACH_Z
+SLAB = -(-(REACH_X + REACH_XB) // SLOTS)
+VMEM_LIMIT = 48 * 1024 * 1024
 AXES = ("gx", "gy", "gz")
 
 
@@ -160,33 +163,60 @@
     return lax.rem(lax.axis_index("gy"), 2)
 
 
-def pack_kernel(geo, own_b, own_k, sib_b, sib_k, z_out, dp_out, dm_out):
-    core = core_of()
-    bx, ye = geo["bx"], geo["ye"]
+def fetch(pairs, sems, first=0):
+    copies = [pltpu.make_async_copy(source, target, sems.at[first + i]) for i, (source, target) in enumerate(pairs)]
+    for copy in copies:
+        copy.start()
+    return copies
+
+
+def strip_planes(bx):
+    b0, b1, k0, k1 = REACH_XB, bx - REACH_XB, REACH_X, bx - REACH_X
+    parts = ((0, b0, 0, k0), (b0, b1, k0, k1), (b1, bx, k1, bx))
+    slots = []
+    for b_first, b_last, k_first, k_last in parts:
+        slots += [(0, p) for p in range(b_first, b_last)] + [(1, p) for p in range(k_first, k_last)]
+        slots += [None] * (-len(slots) % SLOTS)
+    return slots
+
+
+def pack_kernel(geo, lists, count, *refs):
+    count //= 2
+    arrays, sems, scratch = refs[:2 * count], refs[-1], refs[-1 - 2 * count:-1]
+    z_out, own, sib = refs[-2 - 2 * count], scratch[:count], scratch[count:]
+    core, ye = core_of(), geo["ye"]
+    copies = fetch(list(zip(arrays, own + sib)), sems)
     base = jnp.where(core == 1, LANES - REACH_Z, 0)
     lane = lanes_of((ye, LANES))
-
-    def pack(out, first_b, count_b, first_k, count_k):
-        for refs, half in (((own_b, own_k), core), ((sib_b, sib_k), 1 - core)):
-            rows = pl.ds(pl.multiple_of(half * ye, 8), ye)
-            planes = [(refs[0], first_b + p) for p in range(count_b)] + [(refs[1], first_k + p) for p in range(count_k)]
-            for m in range(out.shape[0]):
-                packed = jnp.zeros((ye, LANES), jnp.float32)
-                for q, (ref, p) in enumerate(planes[m * SLOTS:(m + 1) * SLOTS]):
-                    moved = pltpu.roll(ref[p], lax.rem(REACH_Z * q - base + LANES, LANES), 1)
+    for i, (fields, half) in enumerate(((own, core), (sib, 1 - core))):
+        for copy in copies[i * count:(i + 1) * count]:
+            copy.wait()
+        rows = pl.ds(pl.multiple_of(half * ye, 8), ye)
+        for m in range(len(lists) // SLOTS):
+            packed = jnp.zeros((ye, LANES), jnp.float32)
+            for q, slot in enumerate(lists[m * SLOTS:(m + 1) * SLOTS]):
+                if slot is not None:
+                    moved = pltpu.roll(fields[slot[0]][slot[1]], lax.rem(REACH_Z * q - base + LANES, LANES), 1)
                     packed = jnp.where((lane >= REACH_Z * q) & (lane < REACH_Z * (q + 1)), moved, packed)
-                out[m, rows] = packed
-
-    pack(z_out, 0, bx, 0, bx)
-    high_b, high_k = bx - REACH_XB, bx - REACH_X
-    pack(dp_out, jnp.where(core == 0, high_b, 0), REACH_XB, jnp.where(core == 0, high_k, 0), REACH_X)
-    pack(dm_out, jnp.where(core == 0, 0, high_b), REACH_XB, jnp.where(core == 0, 0, high_k), REACH_X)
+            z_out[m, rows] = packed
+
+
+def passed_views(geo, ref):
+    wide0, wide1, rows = geo["bx"] + 2 * WIN0, geo["bx"] // 2 + 2 * WIN1, geo["yw"] // 2
+    views, at = [], 0
+    for i in range(6):
+        views.append(ref.at[pl.ds(at, wide0 + (i == 0))])
+        at += wide0 + 1
+    for i in range(6):
+        views.append(ref.at[pl.ds(at + i // 2 * (wide1 + 1), wide1 + (i == 0)), pl.ds(i % 2 * rows, rows)])
+    return views
 
 
 def down_kernel(geo, *refs):
-    (own_b, own_k, sib_b, sib_k, even_own, odd_own, any_even, any_odd, any_z, any_dp, any_dm,
-     packed_out, even_out, odd_out, o_cx, o_cy, o_cz, o_iv, o_g0, o_w, p_cx, p_cy, p_cz, p_iv, p_g0, p_w,
-     even_sib, odd_sib, z_in, dp_in, dm_in,
+    ins, refs = refs[:8], refs[8:]
+    (packed_any, even_any, odd_any, passed,
+     own_in, sib_in, even_own, odd_own, even_sib, odd_sib, z_in, zx_in,
+     packed_out, even_out, odd_out,
      k0, cx, cy, cz, iv, ds, g0, g, d1, d2,
      k1, ex, ey, ez, ei, es, h0, h, f1, f2, u1, half_y, half_y1, sems, in_sems) = refs
     core = core_of()
@@ -197,12 +227,8 @@
     lo_there, hi_there = ix > 0, ix < nx - 1
     even = lax.rem(ix, 2) == 0
 
-    arrivals = []
-    for i, (source, target) in enumerate(
-            ((any_even, even_sib), (any_odd, odd_sib), (any_z, z_in), (any_dp, dp_in), (any_dm, dm_in))):
-        copy = pltpu.make_async_copy(source, target, in_sems.at[i])
-        copy.start()
-        arrivals.append(copy)
+    arrivals = fetch(list(zip(ins, (
+        own_in, sib_in, even_own, odd_own, even_sib, odd_sib, z_in, zx_in))), in_sems)
 
     lane = lanes_of((yw, LANES))
     halo_lanes = jnp.where(core == 0, lane - (LANES - REACH_Z), REACH_Z - 1 - lane) >= 0
@@ -214,36 +240,37 @@
     own_rows = pl.ds(pl.multiple_of(core * ye, 8), ye)
     sib_rows = pl.ds(pl.multiple_of((1 - core) * ye, 8), ye)
     zero_pads(k0, d1, d2, k1, f1, f2)
-    windows = ((g0, own_b, sib_b, REACH_XB, 0, 0), (k0, own_k, sib_k, REACH_X, REACH_XB, bx))
+    windows = ((g0, 0, REACH_XB, 0), (k0, bx, REACH_X, REACH_XB))
     for p in range(REACH_X - REACH_XB):
         g0[1 + p] = jnp.zeros((yw, LANES), jnp.float32)
         g0[xw - p] = jnp.zeros((yw, LANES), jnp.float32)
 
     def halos(from_even, from_odd, rows):
-        for window, _, _, width, at, _ in windows:
+        for window, _, width, at in windows:
             e, o = from_even[pl.ds(at, width)], from_odd[pl.ds(at, width)]
             window[pl.ds(1 + REACH_X - width, width), rows] = jnp.where(lo_there, jnp.where(even, o, e), 0.0)
             window[pl.ds(1 + REACH_X + bx, width), rows] = jnp.where(hi_there, jnp.where(even, e, o), 0.0)
 
-    for window, own, sib, _, _, _ in windows:
-        window[pl.ds(1 + REACH_X, bx), own_rows] = own[...]
-        window[pl.ds(1 + REACH_X, bx), sib_rows] = sib[...]
-    halos(even_own, odd_own, own_rows)
     for copy in arrivals:
         copy.wait()
+    for window, at, _, _ in windows:
+        window[pl.ds(1 + REACH_X, bx), own_rows] = own_in[pl.ds(at, bx)]
+        window[pl.ds(1 + REACH_X, bx), sib_rows] = sib_in[pl.ds(at, bx)]
+    halos(even_own, odd_own, own_rows)
     halos(even_sib, odd_sib, sib_rows)
-    for window, _, _, width, at_d, at_z in windows:
-        for p in range(bx):
-            at = 1 + REACH_X + p
-            window[at] = jnp.where(halo_lanes, jnp.where(z_there, strip(z_in, at_z + p), 0.0), window[at])
+    for slot, plane in enumerate(strip_planes(bx)):
+        if plane is not None:
+            window, at = windows[plane[0]][0], 1 + REACH_X + plane[1]
+            window[at] = jnp.where(halo_lanes, jnp.where(z_there, strip(z_in, slot), 0.0), window[at])
+    for window, _, width, slot in windows:
         for p in range(width):
-            plus, minus = strip(dp_in, at_d + p), strip(dm_in, at_d + p)
-            low = jnp.where(core == 0, minus, plus)
-            high = jnp.where(core == 0, plus, minus)
+            e, o = strip(zx_in, slot + p), strip(zx_in, SLAB * SLOTS + slot + p)
             at = 1 + REACH_X - width + p
-            window[at] = jnp.where(halo_lanes, jnp.where(z_there & lo_there, low, 0.0), window[at])
+            low = jnp.where(z_there & lo_there, jnp.where(even, o, e), 0.0)
+            window[at] = jnp.where(halo_lanes, low, window[at])
             at = 1 + REACH_X + bx + p
-            window[at] = jnp.where(halo_lanes, jnp.where(z_there & hi_there, high, 0.0), window[at])
+            high = jnp.where(z_there & hi_there, jnp.where(even, e, o), 0.0)
+            window[at] = jnp.where(halo_lanes, high, window[at])
 
     grid = Grid(xw, yw, LANES, 1, 1, False, 8)
 
@@ -257,16 +284,19 @@
     wide0 = bx + 2 * WIN0
     copies = []
 
-    def send(source, start, count, target):
-        copy = pltpu.make_async_copy(source.at[pl.ds(start, count)], target, sems.at[len(copies)])
+    views = passed_views(geo, passed)
+
+    def send(source, start, count):
+        i = len(copies)
+        copy = pltpu.make_async_copy(source.at[pl.ds(start, count)], views[i], sems.at[i])
         copy.start()
         copies.append(copy)
 
-    send(cx, own0 - 1, wide0 + 1, o_cx)
-    send(cy, own0, wide0, o_cy)
-    send(cz, own0, wide0, o_cz)
-    send(iv, own0, wide0, o_iv)
-    send(g0, own0, wide0, o_g0)
+    send(cx, own0 - 1, wide0 + 1)
+    send(cy, own0, wide0)
+    send(cz, own0, wide0)
+    send(iv, own0, wide0)
+    send(g0, own0, wide0)
 
     def restrict(source, target, tmp, x_count, at, y_first, y_rows, shift):
         for i in range(x_count):
@@ -298,7 +328,7 @@
         d1[here] = direction
 
     grid.step(coeffs, d2, g, *FACTORS[2], third)
-    send(k0, own0, wide0, o_w)
+    send(k0, own0, wide0)
 
     def residual(here, v, value, direction):
         g[here] = value * ds[here]
@@ -316,11 +346,11 @@
     grid1.setup(k1, ex, ey, ez, ei, es, 0.25, first1)
     own1 = 1 + REACH_X // 2 - WIN1
     wide1 = bx // 2 + 2 * WIN1
-    send(ex, own1 - 1, wide1 + 1, p_cx)
-    send(ey, own1, wide1, p_cy)
-    send(ez, own1, wide1, p_cz)
-    send(ei, own1, wide1, p_iv)
-    send(h0, own1, wide1, p_g0)
+    send(ex, own1 - 1, wide1 + 1)
+    send(ey, own1, wide1)
+    send(ez, own1, wide1)
+    send(ei, own1, wide1)
+    send(h0, own1, wide1)
     coeffs1 = (ex, ey, ez, ei)
 
     def second1(here, v, value, direction):
@@ -335,13 +365,14 @@
         f1[here] = direction
 
     grid1.step(coeffs1, f2, h, *FACTORS[2], third1)
-    send(u1, own1, wide1, p_w)
+    send(u1, own1, wide1)
     mine = 1 + REACH_X // 2
     last = mine + bx // 2
     for source, low, high, at, count in ((u1, mine + 1, last - WIN1, 0, 5), (h0, mine + 3, last - 5, 5, 2)):
         low, high = source[pl.ds(low, count)], source[pl.ds(high, count)]
         even_out[pl.ds(at, count)] = jnp.where(even, high, low)
         odd_out[pl.ds(at, count)] = jnp.where(even, low, high)
+    copies += fetch(((even_out, even_any), (odd_out, odd_any)), sems, 12)
 
     def residual1(here, v, value, direction):
         h[here] = value * es[here]
@@ -361,7 +392,9 @@
         packed = jnp.zeros((y2, LANES), jnp.float32)
         for p in range(x2):
             packed = jnp.where(slot == lax.rem(p + place, 8), picked[p * y2:(p + 1) * y2], packed)
-        packed_out[f] = packed
+        for j in range(packed_out.shape[0]):
+            packed_out[j, f] = packed
+    copies += fetch(((packed_out, packed_any),), sems, 14)
     for copy in copies:
         copy.wait()
 
@@ -374,16 +407,16 @@
         del refs[:count]
         return taken
 
-    gathered = take(2 if geo["packed"] else 1)
-    from_even, from_odd = take(2)
-    in0, in1 = take(6), take(6)
-    o_send, o_u, o_r = take(3)
+    any_gathered, any_even, any_odd = take(3)
+    views = passed_views(geo, take(1)[0])
+    in0, in1 = views[:6], views[6:]
+    send_u, send_r, keep_u, keep_r = take(4)
     k2, cx2, cy2, cz2, iv2, ds2, g02, g2, da2, db2, w2, e2 = take(12)
     k3, cx3, cy3, cz3, iv3, ds3, g03, g3, da3, db3, w3, e3 = take(12)
     k4, cx4, cy4, cz4, iv4, g04, g4, da4, db4, e4 = take(10)
     cx1, cy1, cz1, iv1, g01, w1, u1, g1, da1, db1, e1 = take(11)
     cx0, cy0, cz0, iv0, g00, w0, u0, g0, da0, db0 = take(10)
-    e2_wide, sems = take(2)
+    e2_wide, gathered, from_even, from_odd, sems = take(5)
     core = core_of()
     ix, nx = lax.axis_index("gx"), lax.axis_size("gx")
     iz, nz = lax.axis_index("gz"), lax.axis_size("gz")
@@ -392,6 +425,7 @@
     x2, y2, z2 = geo["x2"], geo["y2"], geo["z2"]
     wide0, wide1 = bx + 2 * WIN0, bx // 2 + 2 * WIN1
 
+    arrivals = fetch(((any_gathered, gathered), (any_even, from_even), (any_odd, from_odd)), sems, 12)
     copies = []
     for sources, targets, wide in ((in1, (cx1, cy1, cz1, iv1, g01, w1), wide1), (in0, (cx0, cy0, cz0, iv0, g00, w0), wide0)):
         for i, (source, target) in enumerate(zip(sources, targets)):
@@ -402,22 +436,22 @@
 
     zero_pads(k2, da2, db2, e2, k3, da3, db3, e3, k4, da4, db4, e4, u1, da1, db1, u0, da0, db0)
 
+    for copy in arrivals:
+        copy.wait()
     if geo["packed"]:
         slot = lanes_of((y2, LANES)) // 16
-        for jx in range(nx):
-            gx = lax.bitwise_xor(ix, jx)
+        for gx in range(nx):
             for f, target in ((0, g02), (1, k2)):
                 for p in range(8):
                     merged = jnp.zeros((y2, LANES), jnp.float32)
-                    for jz in range(nz):
-                        gz = lax.bitwise_xor(iz, jz)
-                        for source, cc in ((gathered[0], core), (gathered[1], 1 - core)):
-                            place = 2 * gz + cc
-                            merged = jnp.where(slot == lax.rem(p + place, 8), source[jx, jz, f], merged)
+                    for gz in range(nz):
+                        for cc in range(2):
+                            here = gathered[(2 * gx + cc) * nz + gz, f]
+                            merged = jnp.where(slot == (p + 2 * gz + cc) % 8, here, merged)
                     target[1 + 8 * gx + p] = pltpu.roll(merged, (LANES - 16 * p) % LANES, 1)
     else:
-        g02[pl.ds(1, x2)] = gathered[0][0]
-        k2[pl.ds(1, x2)] = gathered[0][1]
+        g02[pl.ds(1, x2)] = gathered[0]
+        k2[pl.ds(1, x2)] = gathered[1]
 
     def descend(grid, level, k, cx, cy, cz, iv, ds, g0, first_target):
         def first(at, here, inverse):
@@ -586,20 +620,10 @@
     own = pl.ds(1 + WIN0, bx)
     own_rows = pl.ds(pl.multiple_of(geo["oy"] + core * by, 8), by)
     sib_rows = pl.ds(pl.multiple_of(geo["oy"] + (1 - core) * by, 8), by)
-    mine = lanes_of((bx, by, LANES)) // HALF == core
-    o_send[...] = jnp.where(mine, w0[own, sib_rows], pltpu.roll(g0[own, sib_rows], HALF, 2))
-    o_u[...] = w0[own, own_rows]
-    o_r[...] = g0[own, own_rows]
-
-
-def merge_kernel(u_ref, r_ref, other, u_out, r_out):
-    v = other[...]
-    mine = lanes_of(v.shape) // HALF == core_of()
-    u_out[...] = jnp.where(mine, u_ref[...], v)
-    r_out[...] = jnp.where(mine, r_ref[...], pltpu.roll(v, HALF, 2))
-
-
-PARAMS = pltpu.CompilerParams(vmem_limit_bytes=60 * 1024 * 1024)
+    leaving = fetch(((w0.at[own, sib_rows], send_u), (g0.at[own, sib_rows], send_r),
+                     (w0.at[own, own_rows], keep_u), (g0.at[own, own_rows], keep_r)), sems, 15)
+    for copy in leaving:
+        copy.wait()
 
 
 def array(*shape):
@@ -630,11 +654,11 @@
             perm[i], perm[i + 1] = (i, i + 1), (i + 1, i)
         return lax.ppermute(v, "gx", perm)
 
-    def facing(v, dx):
+    def facing(v):
         perm = {}
         for x, p, z in every:
-            if z > 0 and 0 <= x + dx < nx:
-                a, b = index(x, p, 0, z), index(x + dx, p, 1, z - 1)
+            if z > 0:
+                a, b = index(x, p, 0, z), index(x, p, 1, z - 1)
                 perm[a], perm[b] = b, a
         return lax.ppermute(v, AXES, [(i, perm.get(i, i)) for i in range(nx * ny * nz)])
 
@@ -662,71 +686,86 @@
         pad_y=(yw // 4 - by // 2) // 2,
     )
 
-    sib_b, sib_k = sibling(own_b), sibling(own_k)
+    own = lax.optimization_barrier(jnp.concatenate([own_b, own_k], 0))
     even = ix % 2 == 0
-    high = jnp.concatenate([own_b[bx - REACH_XB:], own_k[bx - REACH_X:]], 0)
-    low = jnp.concatenate([own_b[:REACH_XB], own_k[:REACH_X]], 0)
+    high = jnp.concatenate([own[bx - REACH_XB:bx], own[2 * bx - REACH_X:]], 0)
+    low = jnp.concatenate([own[:REACH_XB], own[bx:bx + REACH_X]], 0)
     even_own = paired(jnp.where(even, high, low), 0)
     odd_own = paired(jnp.where(even, low, high), 1)
-    m, md = -(-2 * bx // SLOTS), -(-(REACH_X + REACH_XB) // SLOTS)
-    z_send, dp_send, dm_send = pl.pallas_call(
-        functools.partial(pack_kernel, geo),
-        out_shape=[array(m, yw, LANES), array(md, yw, LANES), array(md, yw, LANES)],
-        compiler_params=PARAMS, name="pack_z",
-        cost_estimate=pl.CostEstimate(flops=4_000_000, bytes_accessed=8_000_000, transcendentals=0),
-    )(own_b, own_k, sib_b, sib_k)
-    z_in, dp_in, dm_in = facing(z_send, 0), facing(dp_send, 1), facing(dm_send, -1)
+    sib = sibling(own)
+    anywhere, hbm = pl.BlockSpec(memory_space=pl.ANY), pl.BlockSpec(memory_space=pltpu.HBM)
+
+    def call(name, kernel, ins, outs, scratch, hbm_ins=0, hbm_outs=0, limit=0):
+        held = sum(4 * math.prod(v.shape) for v in scratch if v.dtype == jnp.float32)
+        return pl.pallas_call(
+            kernel, out_shape=outs, in_specs=[anywhere] * (len(ins) - hbm_ins) + [hbm] * hbm_ins,
+            out_specs=[anywhere] * (len(outs) - hbm_outs) + [hbm] * hbm_outs,
+            scratch_shapes=scratch, name=name,
+            compiler_params=pltpu.CompilerParams(vmem_limit_bytes=max(limit, held + 6 * 1024 * 1024)),
+        )(*ins)
+
+    def vmem(shape):
+        return pltpu.VMEM(shape, jnp.float32)
+
+    def pack(name, lists, ins, later=()):
+        shape = (len(lists) // SLOTS, yw, LANES)
+        return pl.pallas_call(
+            functools.partial(pack_kernel, geo, lists, len(ins)),
+            out_shape=array(*shape), in_specs=[anywhere] * (len(ins) + len(later)),
+            scratch_shapes=[vmem(v.shape) for v in ins] + [pltpu.SemaphoreType.DMA((len(ins),))],
+            compiler_params=pltpu.CompilerParams(vmem_limit_bytes=8 * 1024 * 1024 * max(1, yw // 32)), name=name,
+            cost_estimate=pl.CostEstimate(flops=4_000_000, bytes_accessed=8_000_000, transcendentals=0),
+        )(*ins, *later)
+
+    z_send = pack("pack_box", [p and (0, p[0] * bx + p[1]) for p in strip_planes(bx)], (own, sib))
+    z_in = facing(z_send)
+    even_own, odd_own, z_send = lax.optimization_barrier((even_own, odd_own, z_send))
     even_sib, odd_sib = sibling(even_own), sibling(odd_own)
+    slab = [(0, p) for p in range(REACH_X + REACH_XB)]
+    slab += [None] * (SLAB * SLOTS - len(slab))
+    slabs = slab + [p and (1, p[1]) for p in slab]
+    zx_in = facing(pack("pack_halo", slabs, (even_own, odd_own, even_sib, odd_sib), (z_in,)))
 
     wide0, wide1 = bx + 2 * WIN0, bx // 2 + 2 * WIN1
     x1, y1 = xw // 2, yw // 2
-    some0 = pltpu.VMEM((xw + 2, yw, LANES), jnp.float32)
-    some1 = pltpu.VMEM((x1 + 2, y1, LANES), jnp.float32)
-    passed0 = [array(wide0 + (i == 0), yw, LANES) for i in range(6)]
-    passed1 = [array(wide1 + (i == 0), y1, LANES) for i in range(6)]
-    vmem, anywhere = pl.BlockSpec(memory_space=pltpu.VMEM), pl.BlockSpec(memory_space=pl.ANY)
+    some0 = vmem((xw + 2, yw, LANES))
+    some1 = vmem((x1 + 2, y1, LANES))
+    passed = array(6 * (wide0 + 1) + 3 * (wide1 + 1), yw, LANES)
     edge = 7
-    down = pl.pallas_call(
-        functools.partial(down_kernel, geo),
-        out_shape=[array(2, by // 2, LANES), array(edge, y1, LANES), array(edge, y1, LANES)] + passed0 + passed1,
-        in_specs=[vmem] * 6 + [anywhere] * 5,
-        out_specs=[vmem] * 3 + [anywhere] * 12,
-        scratch_shapes=[pltpu.VMEM(v.shape, jnp.float32) for v in (even_sib, odd_sib, z_in, dp_in, dm_in)]
-        + [some0] * 10 + [some1] * 11
-        + [pltpu.VMEM((6, yw, LANES), jnp.float32), pltpu.VMEM((6, y1, LANES), jnp.float32)]
-        + [pltpu.SemaphoreType.DMA((12,)), pltpu.SemaphoreType.DMA((5,))],
-        compiler_params=PARAMS, name="down",
-    )(own_b, own_k, sib_b, sib_k, even_own, odd_own, even_sib, odd_sib, z_in, dp_in, dm_in)
-    packed, even_send, odd_send, passed = down[0], down[1], down[2], down[3:]
+    ins = (own, sib, even_own, odd_own, even_sib, odd_sib, z_in, zx_in)
+    sends = [array(nx * ny * nz if geo["packed"] else 1, 2, by // 2, LANES), array(edge, y1, LANES), array(edge, y1, LANES)]
+    down = call(
+        "down", functools.partial(down_kernel, geo), ins, sends + [passed],
+        [vmem(v.shape) for v in ins] + [vmem(v.shape) for v in sends] + [some0] * 10 + [some1] * 11
+        + [vmem((6, yw, LANES)), vmem((6, y1, LANES)), pltpu.SemaphoreType.DMA((15,)), pltpu.SemaphoreType.DMA((8,))],
+        hbm_outs=1, limit=VMEM_LIMIT,
+    )
+    packed, even_send, odd_send, passed = down[0], down[1], down[2], down[3]
     from_even, from_odd = paired(even_send, 0), paired(odd_send, 1)
 
     if geo["packed"]:
-        along_z = jnp.stack([packed] + [xor(packed, "gz", j) for j in range(1, nz)])
-        along_x = jnp.stack([along_z] + [xor(along_z, "gx", j) for j in range(1, nx)])
-        gathered = (along_x, sibling(along_x))
+        gathered = lax.all_to_all(packed, AXES, 0, 0, tiled=True)
     else:
         pieces = lax.all_gather(packed, AXES).reshape(nx, pairs, 2, nz, 2, by // 2, 8, 16)
         order = (jnp.arange(8) + 2 * jnp.arange(nz)[:, None, None] + jnp.arange(2)[:, None]) % 8
         order = jnp.transpose(order, (1, 0, 2))[None, None, :, :, None, None, :, None]
         pieces = jnp.take_along_axis(pieces, order, axis=6)
-        gathered = (jnp.transpose(pieces, (4, 0, 6, 1, 5, 3, 2, 7)).reshape(2, geo["x2"], geo["y2"], geo["z2"]),)
+        gathered = jnp.transpose(pieces, (4, 0, 6, 1, 5, 3, 2, 7)).reshape(2, geo["x2"], geo["y2"], geo["z2"])
 
     def level(planes, rows, lanes):
-        return pltpu.VMEM((planes + 2, rows, lanes), jnp.float32)
+        return vmem((planes + 2, rows, lanes))
 
     x2, y2, z2 = geo["x2"], geo["y2"], geo["z2"]
-    send, keep_u, keep_r = pl.pallas_call(
-        functools.partial(up_kernel, geo),
-        out_shape=[array(bx, by, LANES)] * 3,
-        in_specs=[vmem] * (len(gathered) + 2) + [anywhere] * 12,
-        scratch_shapes=[level(x2, y2, z2)] * 12 + [level(x2 // 2, y2, z2)] * 12 + [level(x2 // 4, y2, z2)] * 10
+    send_u, send_r, keep_u, keep_r = call(
+        "up", functools.partial(up_kernel, geo), (gathered, from_even, from_odd, passed), [array(bx, by, LANES)] * 4,
+        [level(x2, y2, z2)] * 12 + [level(x2 // 2, y2, z2)] * 12 + [level(x2 // 4, y2, z2)] * 10
         + [level(wide1, y1, LANES)] * 11 + [level(wide0, yw, LANES)] * 10
-        + [pltpu.VMEM((x2 + 8, y2 + 2 * geo["pad_y"], z2), jnp.float32), pltpu.SemaphoreType.DMA((12,))],
-        compiler_params=PARAMS, name="up",
-    )(*gathered, from_even, from_odd, *passed)
-    return pl.pallas_call(
-        merge_kernel, out_shape=[array(bx, by, LANES)] * 2, compiler_params=PARAMS, name="merge",
-    )(keep_u, keep_r, sibling(send))
+        + [vmem((x2 + 8, y2 + 2 * geo["pad_y"], z2)), vmem(gathered.shape), vmem(from_even.shape), vmem(from_odd.shape)]
+        + [pltpu.SemaphoreType.DMA((19,))],
+        hbm_ins=1, limit=VMEM_LIMIT,
+    )
+    mine = lanes_of((1, 1, LANES)) // HALF == core
+    return jnp.where(mine, keep_u, sibling(send_u)), jnp.where(mine, keep_r, sibling(send_r))
 
 
 def solution(mesh):

time: 76.3 us -> 60.6 us (0.79)
  the two profiles are of different devices: /device:TPU:3 before, /device:TPU:0 now
where the time goes in v2:
time: 60.6 us; the launch traced here: 60.4 us
  starting transfers between devices  21.8 us (36%)
  Pallas kernels  18.4 us (30%)
  waiting for transfers between devices  17.4 us (29%)
  other arithmetic  1.95 us (3%)
  between operations  0.76 us (1%)
    pallas_call x2, Pallas kernels, call(): pl.pallas_call(kernel, out_shape=outs, in_specs=[anywhere] * (len(ins) -...  16.7 us
    ppermute x4, waiting for transfers between devices, paired(): return lax.ppermute(v, 'gx', perm)  10.5 us
    all_to_all x1, starting transfers between devices, on_device(): gathered = lax.all_to_all(packed, AXES, 0, 0, tiled=True)  10.4 us
    ppermute x4, starting transfers between devices, paired(): return lax.ppermute(v, 'gx', perm)  8.45 us
    all_to_all x1, waiting for transfers between devices, on_device(): gathered = lax.all_to_all(packed, AXES, 0, 0, tiled=True)  4.37 us
    ppermute x5, waiting for transfers between devices, sibling(): return lax.ppermute(v, 'gy', [(i, i ^ 1) for i in range(ny)])  2.56 us
    pallas_call x2, Pallas kernels, pack(): pl.pallas_call(functools.partial(pack_kernel, geo, lists, len(ins)), out_...  1.72 us
    ppermute x5, starting transfers between devices, sibling(): return lax.ppermute(v, 'gy', [(i, i ^ 1) for i in range(ny)])  1.6 us
  transfers between devices with their start and end apart: 12, of which 7 were waited for; matrix products, arithmetic and copies ran while one was open for 0% of the time, Pallas kernels for 1%

profile of v2, /device:TPU:0, one launch (start us, length us, event | category | flops | bytes accessed | tf_op | source)
XLA Modules:
  0.0 60.4 jit_solution(8766811253808795590)
XLA Ops:
  0.6 1.1 %pad_maximum_fusion.refs_0_ = f32[64,16,128]{2,1,0:T(8,128)S(1)} fusion(f32[32,16,128]{2,1,0:T(8,128)} %param.3, f32[32,16,128]{2,1,0:T(8,128)} %param.2), kind=kLoop, calls=%fused_computation | loop fusion | flops 131072 | bytes 1048576 | tf_op jit(solution)/shard_map/concatenate | solution.py:689
  1.7 0.5 collective-permute-start
  2.3 0.7 %collective-permute-start.2 = (f32[21,16,128]{2,1,0:T(8,128)S(1)}, f32[21,16,128]{2,1,0:T(8,128)S(1)}, u32[]{:S(2)}, u32[]{:S(2)}) collective-permute-start(f32[21,16,128]{2,1,0:T(8,128)S(1)} %get-tuple-element.26), channel_id=1, source_target_pairs={{0,0},{8,16},{16,8},{24,24},{1,1},{9,17},{17,9},{25,25},{2,2},{10,... | collective-permute-start | bytes 516104 | tf_op jit(solution)/shard_map/ppermute | solution.py:655
  3.0 5.3 %collective-permute-start.1 = (f32[21,16,128]{2,1,0:T(8,128)S(1)}, f32[21,16,128]{2,1,0:T(8,128)S(1)}, u32[]{:S(2)}, u32[]{:S(2)}) collective-permute-start(f32[21,16,128]{2,1,0:T(8,128)S(1)} %get-tuple-element.27), channel_id=1, source_target_pairs={{0,8},{8,0},{16,24},{24,16},{1,9},{9,1},{17,25},{25,17},{2,10},{10... | collective-permute-start | bytes 516104 | tf_op jit(solution)/shard_map/ppermute | solution.py:655
  8.3 0.0 collective-permute-done.refs_1_
  8.3 0.5 pack_box.1
  8.8 0.7 %collective-permute-start.5 = (f32[12,32,128]{2,1,0:T(8,128)S(1)}, f32[12,32,128]{2,1,0:T(8,128)S(1)}, u32[]{:S(2)}, u32[]{:S(2)}) collective-permute-start(f32[12,32,128]{2,1,0:T(8,128)S(1)} %pack_box.1), channel_id=1, source_target_pairs={{0,0},{1,4},{2,5},{3,6},{4,1},{5,2},{6,3},{7,7},{8,8},{9,12},{10,1... | collective-permute-start | bytes 589832 | tf_op jit(solution)/shard_map/ppermute | solution.py:663
  9.5 0.0 collective-permute-done.2.refs_1_.refs_3_
  9.5 7.1 %collective-permute-done.1.refs_0_.refs_2_ = f32[21,16,128]{2,1,0:T(8,128)S(1)} collective-permute-done((f32[21,16,128]{2,1,0:T(8,128)S(1)}, f32[21,16,128]{2,1,0:T(8,128)S(1)}, u32[]{:S(2)}, u32[]{:S(2)}) %collective-permute-start.1) | collective-permute-done | bytes 172064 | tf_op jit(solution)/shard_map/ppermute | solution.py:655
  16.6 0.0 collective-permute-start.3
  16.6 0.5 collective-permute-start.4
  17.1 0.9 %collective-permute-done.3.refs_2_.refs_4_ = f32[21,16,128]{2,1,0:T(8,128)S(1)} collective-permute-done((f32[21,16,128]{2,1,0:T(8,128)S(1)}, f32[21,16,128]{2,1,0:T(8,128)S(1)}, u32[]{:S(2)}, u32[]{:S(2)}) %collective-permute-start.3) | collective-permute-done | bytes 172064 | tf_op jit(solution)/shard_map/ppermute | solution.py:646
  18.0 0.2 collective-permute-done.4.refs_3_.refs_5_
  18.3 0.0 collective-permute-done.5.refs_4_.refs_6_
  18.3 1.2 %pack_halo.1 = f32[8,32,128]{2,1,0:T(8,128)S(1)} custom-call(f32[21,16,128]{2,1,0:T(8,128)S(1)} %collective-permute-done.1.refs_0_.refs_2_, f32[21,16,128]{2,1,0:T(8,128)S(1)} %collective-permute-done.2.refs_1_.refs_3_, f32[21,16,128]{2,1,0:T(8,128)S(1)} %collective-permute-done.3.refs_2_.refs_4_, f32[21,16,128]{2,1,0:T(8,128)S(1)} %collective-permute-done.4.refs_3_.refs_5_, ...), custom_call_target="tpu_custom_call" | custom-call | flops 4000000 | bytes 8000000 | tf_op jit(solution)/shard_map/pack_halo/pallas_call | solution.py:712
  19.5 0.7 %collective-permute-start.6 = (f32[8,32,128]{2,1,0:T(8,128)S(1)}, f32[8,32,128]{2,1,0:T(8,128)S(1)}, u32[]{:S(2)}, u32[]{:S(2)}) collective-permute-start(f32[8,32,128]{2,1,0:T(8,128)S(1)} %pack_halo.1), channel_id=1, source_target_pairs={{0,0},{1,4},{2,5},{3,6},{4,1},{5,2},{6,3},{7,7},{8,8},{9,12},{10,1... | collective-permute-start | bytes 393224 | tf_op jit(solution)/shard_map/ppermute | solution.py:663
  20.2 0.0 collective-permute-done.6.refs_7_
  20.2 9.0 %down.1 = (f32[32,2,8,128]{3,2,1,0:T(8,128)}, f32[7,16,128]{2,1,0:T(8,128)S(1)}, f32[7,16,128]{2,1,0:T(8,128)S(1)}, f32[333,32,128]{2,1,0:T(8,128)}) custom-call(f32[64,16,128]{2,1,0:T(8,128)S(1)} %pad_maximum_fusion.refs_0_, f32[64,16,128]{2,1,0:T(8,128)S(1)} %collective-permute-done.refs_1_, f32[21,16,128]{2,1,0:T(8,128)S(1)} %collective-permute-done.1.refs_0_.refs_2_, ...), custom_call_target="tpu_custom_call" | custom-call | tf_op jit(solution)/shard_map/down/pallas_call | solution.py:700
  29.2 10.4 %all-to-all-start = ((f32[32,2,8,128]{3,2,1,0:T(8,128)}), f32[32,2,8,128]{3,2,1,0:T(8,128)S(1)}, u32[]{:S(2)}, u32[]{:S(2)}) async-start(f32[32,2,8,128]{3,2,1,0:T(8,128)} %get-tuple-element.14), calls=%async_computation | async-start | bytes 524288 | tf_op jit(solution)/shard_map/all_to_all | solution.py:747
  39.7 1.8 %collective-permute-start.7 = (f32[7,16,128]{2,1,0:T(8,128)S(1)}, f32[7,16,128]{2,1,0:T(8,128)S(1)}, u32[]{:S(2)}, u32[]{:S(2)}) collective-permute-start(f32[7,16,128]{2,1,0:T(8,128)S(1)} %get-tuple-element.15), channel_id=1, source_target_pairs={{0,8},{8,0},{16,24},{24,16},{1,9},{9,1},{17,25},{25,17},{2,10},{10... | collective-permute-start | bytes 172040 | tf_op jit(solution)/shard_map/ppermute | solution.py:655
  41.5 0.7 %collective-permute-start.8 = (f32[7,16,128]{2,1,0:T(8,128)S(1)}, f32[7,16,128]{2,1,0:T(8,128)S(1)}, u32[]{:S(2)}, u32[]{:S(2)}) collective-permute-start(f32[7,16,128]{2,1,0:T(8,128)S(1)} %get-tuple-element.16), channel_id=1, source_target_pairs={{0,0},{8,16},{16,8},{24,24},{1,1},{9,17},{17,9},{25,25},{2,2},{10,... | collective-permute-start | bytes 172040 | tf_op jit(solution)/shard_map/ppermute | solution.py:655
  42.2 3.3 %collective-permute-done.7.refs_1_ = f32[7,16,128]{2,1,0:T(8,128)S(1)} collective-permute-done((f32[7,16,128]{2,1,0:T(8,128)S(1)}, f32[7,16,128]{2,1,0:T(8,128)S(1)}, u32[]{:S(2)}, u32[]{:S(2)}) %collective-permute-start.7) | collective-permute-done | bytes 57376 | tf_op jit(solution)/shard_map/ppermute | solution.py:655
  45.5 0.0 collective-permute-done.8.refs_2_
  45.5 4.4 %all-to-all-done.refs_0_ = f32[32,2,8,128]{3,2,1,0:T(8,128)S(1)} async-done(((f32[32,2,8,128]{3,2,1,0:T(8,128)}), f32[32,2,8,128]{3,2,1,0:T(8,128)S(1)}, u32[]{:S(2)}, u32[]{:S(2)}) %all-to-all-start) | async-done | bytes 262176 | tf_op jit(solution)/shard_map/all_to_all | solution.py:747
  49.9 7.7 %up.1 = (f32[32,16,128]{2,1,0:T(8,128)S(1)}, f32[32,16,128]{2,1,0:T(8,128)S(1)}, f32[32,16,128]{2,1,0:T(8,128)S(1)}, f32[32,16,128]{2,1,0:T(8,128)S(1)}) custom-call(f32[32,2,8,128]{3,2,1,0:T(8,128)S(1)} %all-to-all-done.refs_0_, f32[7,16,128]{2,1,0:T(8,128)S(1)} %collective-permute-done.7.refs_1_, f32[7,16,128]{2,1,0:T(8,128)S(1)} %collective-permute-done.8.refs_2_, ...), custom_call_target="tpu_custom_call" | custom-call | tf_op jit(solution)/shard_map/up/pallas_call | solution.py:700
  57.5 0.5 collective-permute-start.9
  58.0 0.1 collective-permute-start.10
  58.1 1.0 %collective-permute-done.9 = f32[32,16,128]{2,1,0:T(8,128)S(1)} collective-permute-done((f32[32,16,128]{2,1,0:T(8,128)S(1)}, f32[32,16,128]{2,1,0:T(8,128)S(1)}, u32[]{:S(2)}, u32[]{:S(2)}) %collective-permute-start.9) | collective-permute-done | bytes 262176 | tf_op jit(solution)/shard_map/ppermute | solution.py:646
  59.1 0.4 collective-permute-done.10
  59.5 0.9 %broadcast_select_fusion = (f32[32,16,128]{2,1,0:T(8,128)}, f32[32,16,128]{2,1,0:T(8,128)}) fusion(f32[32,16,128]{2,1,0:T(8,128)S(1)} %get-tuple-element.20, f32[32,16,128]{2,1,0:T(8,128)S(1)} %collective-permute-done.10, pred[128]{0:T(512)(128)(4,1)S(1)} %fusion.2, f32[32,16,128]{2,1,0:T(8,128)S(1)} %get-tuple-element.18, ...), kind=kLoop, calls=%fused_computation.5 | loop fusion | flops 131072 | bytes 1572992 | tf_op jit(solution)/shard_map/jit(_where)/select_n | solution.py:768
  (4 shorter events, 0.1 us)
Async XLA Ops:
  1.7 6.6 %collective-permute-start = (f32[64,16,128]{2,1,0:T(8,128)S(1)}, f32[64,16,128]{2,1,0:T(8,128)S(1)}, u32[]{:S(2)}, u32[]{:S(2)}) collective-permute-start(f32[64,16,128]{2,1,0:T(8,128)S(1)} %pad_maximum_fusion.refs_0_), channel_id=1, source_target_pairs={{0,4},{4,0},{1,5},{5,1},{2,6},{6,2},{3,7},{7,3},{8,12},{12,8},{9,1... | collective-permute-start | bytes 1572872 | tf_op jit(solution)/shard_map/ppermute | solution.py:646
  2.3 7.2 %collective-permute-start.2 = (f32[21,16,128]{2,1,0:T(8,128)S(1)}, f32[21,16,128]{2,1,0:T(8,128)S(1)}, u32[]{:S(2)}, u32[]{:S(2)}) collective-permute-start(f32[21,16,128]{2,1,0:T(8,128)S(1)} %get-tuple-element.26), channel_id=1, source_target_pairs={{0,0},{8,16},{16,8},{24,24},{1,1},{9,17},{17,9},{25,25},{2,2},{10,... | collective-permute-start | bytes 516104 | tf_op jit(solution)/shard_map/ppermute | solution.py:655
  3.0 13.6 %collective-permute-start.1 = (f32[21,16,128]{2,1,0:T(8,128)S(1)}, f32[21,16,128]{2,1,0:T(8,128)S(1)}, u32[]{:S(2)}, u32[]{:S(2)}) collective-permute-start(f32[21,16,128]{2,1,0:T(8,128)S(1)} %get-tuple-element.27), channel_id=1, source_target_pairs={{0,8},{8,0},{16,24},{24,16},{1,9},{9,1},{17,25},{25,17},{2,10},{10... | collective-permute-start | bytes 516104 | tf_op jit(solution)/shard_map/ppermute | solution.py:655
  8.8 9.5 %collective-permute-start.5 = (f32[12,32,128]{2,1,0:T(8,128)S(1)}, f32[12,32,128]{2,1,0:T(8,128)S(1)}, u32[]{:S(2)}, u32[]{:S(2)}) collective-permute-start(f32[12,32,128]{2,1,0:T(8,128)S(1)} %pack_box.1), channel_id=1, source_target_pairs={{0,0},{1,4},{2,5},{3,6},{4,1},{5,2},{6,3},{7,7},{8,8},{9,12},{10,1... | collective-permute-start | bytes 589832 | tf_op jit(solution)/shard_map/ppermute | solution.py:663
  16.6 1.4 %collective-permute-start.3 = (f32[21,16,128]{2,1,0:T(8,128)S(1)}, f32[21,16,128]{2,1,0:T(8,128)S(1)}, u32[]{:S(2)}, u32[]{:S(2)}) collective-permute-start(f32[21,16,128]{2,1,0:T(8,128)S(1)} %collective-permute-done.1.refs_0_.refs_2_), channel_id=1, source_target_pairs={{0,4},{4,0},{1,5},{5,1},{2,6},{6,2},{3,7},{7,3},{8,12},{12,8},{9,1... | collective-permute-start | bytes 516104 | tf_op jit(solution)/shard_map/ppermute | solution.py:646
  16.6 1.6 %collective-permute-start.4 = (f32[21,16,128]{2,1,0:T(8,128)S(1)}, f32[21,16,128]{2,1,0:T(8,128)S(1)}, u32[]{:S(2)}, u32[]{:S(2)}) collective-permute-start(f32[21,16,128]{2,1,0:T(8,128)S(1)} %collective-permute-done.2.refs_1_.refs_3_), channel_id=1, source_target_pairs={{0,4},{4,0},{1,5},{5,1},{2,6},{6,2},{3,7},{7,3},{8,12},{12,8},{9,1... | collective-permute-start | bytes 516104 | tf_op jit(solution)/shard_map/ppermute | solution.py:646
  19.5 0.7 %collective-permute-start.6 = (f32[8,32,128]{2,1,0:T(8,128)S(1)}, f32[8,32,128]{2,1,0:T(8,128)S(1)}, u32[]{:S(2)}, u32[]{:S(2)}) collective-permute-start(f32[8,32,128]{2,1,0:T(8,128)S(1)} %pack_halo.1), channel_id=1, source_target_pairs={{0,0},{1,4},{2,5},{3,6},{4,1},{5,2},{6,3},{7,7},{8,8},{9,12},{10,1... | collective-permute-start | bytes 393224 | tf_op jit(solution)/shard_map/ppermute | solution.py:663
  29.2 20.6 %all-to-all-start = ((f32[32,2,8,128]{3,2,1,0:T(8,128)}), f32[32,2,8,128]{3,2,1,0:T(8,128)S(1)}, u32[]{:S(2)}, u32[]{:S(2)}) async-start(f32[32,2,8,128]{3,2,1,0:T(8,128)} %get-tuple-element.14), calls=%async_computation | async-start | bytes 524288 | tf_op jit(solution)/shard_map/all_to_all | solution.py:747
  39.7 5.8 %collective-permute-start.7 = (f32[7,16,128]{2,1,0:T(8,128)S(1)}, f32[7,16,128]{2,1,0:T(8,128)S(1)}, u32[]{:S(2)}, u32[]{:S(2)}) collective-permute-start(f32[7,16,128]{2,1,0:T(8,128)S(1)} %get-tuple-element.15), channel_id=1, source_target_pairs={{0,8},{8,0},{16,24},{24,16},{1,9},{9,1},{17,25},{25,17},{2,10},{10... | collective-permute-start | bytes 172040 | tf_op jit(solution)/shard_map/ppermute | solution.py:655
  41.5 4.0 %collective-permute-start.8 = (f32[7,16,128]{2,1,0:T(8,128)S(1)}, f32[7,16,128]{2,1,0:T(8,128)S(1)}, u32[]{:S(2)}, u32[]{:S(2)}) collective-permute-start(f32[7,16,128]{2,1,0:T(8,128)S(1)} %get-tuple-element.16), channel_id=1, source_target_pairs={{0,0},{8,16},{16,8},{24,24},{1,1},{9,17},{17,9},{25,25},{2,2},{10,... | collective-permute-start | bytes 172040 | tf_op jit(solution)/shard_map/ppermute | solution.py:655
  57.5 1.6 %collective-permute-start.9 = (f32[32,16,128]{2,1,0:T(8,128)S(1)}, f32[32,16,128]{2,1,0:T(8,128)S(1)}, u32[]{:S(2)}, u32[]{:S(2)}) collective-permute-start(f32[32,16,128]{2,1,0:T(8,128)S(1)} %get-tuple-element.19), channel_id=1, source_target_pairs={{0,4},{4,0},{1,5},{5,1},{2,6},{6,2},{3,7},{7,3},{8,12},{12,8},{9,1... | collective-permute-start | bytes 786440 | tf_op jit(solution)/shard_map/ppermute | solution.py:646
  58.0 1.5 %collective-permute-start.10 = (f32[32,16,128]{2,1,0:T(8,128)S(1)}, f32[32,16,128]{2,1,0:T(8,128)S(1)}, u32[]{:S(2)}, u32[]{:S(2)}) collective-permute-start(f32[32,16,128]{2,1,0:T(8,128)S(1)} %get-tuple-element.21), channel_id=1, source_target_pairs={{0,4},{4,0},{1,5},{5,1},{2,6},{6,2},{3,7},{7,3},{8,12},{12,8},{9,1... | collective-permute-start | bytes 786440 | tf_op jit(solution)/shard_map/ppermute | solution.py:646

commit v3 on v2

--- a/solution.py
+++ b/solution.py
@@ -20,8 +20,6 @@
 REACH_Z = 20
 WIN0 = 4
 WIN1 = REACH_X // 2
-SLOTS = LANES // REACH_Z
-SLAB = -(-(REACH_X + REACH_XB) // SLOTS)
 VMEM_LIMIT = 48 * 1024 * 1024
 AXES = ("gx", "gy", "gz")
 
@@ -113,10 +111,11 @@
         cx, cy, cz, iv = coeffs
 
         def body(at):
-            here, before = pl.ds(at, self.size), pl.ds(at - 1, self.size)
-            v = src[here]
+            here = pl.ds(at, self.size)
+            planes, x_coeff = src[pl.ds(at - 1, self.size + 2)], cx[pl.ds(at - 1, self.size + 1)]
+            v = planes[1:-1]
             y_coeff, z_coeff = cy[here], cz[here]
-            near = cx[here] * src[pl.ds(at + 1, self.size)] + cx[before] * src[before]
+            near = x_coeff[1:] * planes[2:] + x_coeff[:-1] * planes[:-2]
             near = near + (y_coeff * self.up_y(v) + self.down_y(y_coeff * v))
             near = near + (z_coeff * self.up_z(v) + self.down_z(z_coeff * v))
             g = g_in[here] - v + iv[here] * near
@@ -153,6 +152,16 @@
     return 0.75 * v + 0.25 * jnp.where(even, low, high)
 
 
+def picked_lanes(v, pick):
+    pick, total = pick.astype(jnp.bfloat16), None
+    for _ in range(3):
+        part = v.astype(jnp.bfloat16)
+        v = v - part.astype(jnp.float32)
+        product = jnp.dot(part, pick, preferred_element_type=jnp.float32)
+        total = product if total is None else total + product
+    return total
+
+
 def zero_pads(*refs):
     for ref in refs:
         ref[0] = jnp.zeros(ref.shape[1:], jnp.float32)
@@ -163,41 +172,64 @@
     return lax.rem(lax.axis_index("gy"), 2)
 
 
-def fetch(pairs, sems, first=0):
-    copies = [pltpu.make_async_copy(source, target, sems.at[first + i]) for i, (source, target) in enumerate(pairs)]
-    for copy in copies:
-        copy.start()
-    return copies
-
-
-def strip_planes(bx):
-    b0, b1, k0, k1 = REACH_XB, bx - REACH_XB, REACH_X, bx - REACH_X
-    parts = ((0, b0, 0, k0), (b0, b1, k0, k1), (b1, bx, k1, bx))
-    slots = []
-    for b_first, b_last, k_first, k_last in parts:
-        slots += [(0, p) for p in range(b_first, b_last)] + [(1, p) for p in range(k_first, k_last)]
-        slots += [None] * (-len(slots) % SLOTS)
-    return slots
-
-
-def pack_kernel(geo, lists, count, *refs):
-    count //= 2
-    arrays, sems, scratch = refs[:2 * count], refs[-1], refs[-1 - 2 * count:-1]
-    z_out, own, sib = refs[-2 - 2 * count], scratch[:count], scratch[count:]
+def reaches():
+    source1 = {0: WIN1 + 2, 1: WIN1 + 1, 2: WIN1, 3: 0}
+    coeff1 = {a: max(source1.get(a, -1) + 1, source1.get(a - 1, -1), source1.get(a + 1, -1), min(WIN1, 7 - a)) for a in range(7)}
+    residual0 = {0: 2 * source1[0]}
+    coeff0 = {0: 2 * coeff1[0]}
+    for a in range(1, 7):
+        for x in (2 * a - 1, 2 * a):
+            coeff0[x] = 2 * coeff1[a]
+            if a in source1:
+                residual0[x] = 2 * source1[a]
+
+    def grown(steps, x):
+        return max([z + steps - abs(x - at) for at, z in residual0.items() if abs(x - at) <= steps], default=0)
+
+    source = [grown(3, x) for x in range(REACH_XB + 1)]
+    coeff = [max(grown(4, x), coeff0[x]) for x in range(REACH_X + 1)]
+    assert max(source + coeff) <= REACH_Z
+    return source, coeff
+
+
+def slots_of(items):
+    rows, used = [], LANES
+    for item, width in items:
+        if width:
+            if used + width > LANES:
+                rows.append([])
+                used = 0
+            rows[-1].append((item, used, width))
+            used += width
+    return rows
+
+
+def box_slots(bx):
+    source, coeff = reaches()
+    return slots_of([((0, p), source[0]) for p in range(bx)] + [((1, p), coeff[0]) for p in range(bx)])
+
+
+def halo_slots():
+    source, coeff = reaches()
+    items = []
+    for pair in range(2):
+        items += [((pair, 0, x), source[x]) for x in range(1, REACH_XB + 1)]
+        items += [((pair, 1, x), coeff[x]) for x in range(1, REACH_X + 1)]
+    return slots_of(items)
+
+
+def pack_kernel(geo, slots, plane_of, count, *refs):
+    own, sib, z_out = refs[:count // 2], refs[count // 2:count], refs[-1]
     core, ye = core_of(), geo["ye"]
-    copies = fetch(list(zip(arrays, own + sib)), sems)
-    base = jnp.where(core == 1, LANES - REACH_Z, 0)
     lane = lanes_of((ye, LANES))
-    for i, (fields, half) in enumerate(((own, core), (sib, 1 - core))):
-        for copy in copies[i * count:(i + 1) * count]:
-            copy.wait()
+    for fields, half in ((own, core), (sib, 1 - core)):
         rows = pl.ds(pl.multiple_of(half * ye, 8), ye)
-        for m in range(len(lists) // SLOTS):
+        for m, row in enumerate(slots):
             packed = jnp.zeros((ye, LANES), jnp.float32)
-            for q, slot in enumerate(lists[m * SLOTS:(m + 1) * SLOTS]):
-                if slot is not None:
-                    moved = pltpu.roll(fields[slot[0]][slot[1]], lax.rem(REACH_Z * q - base + LANES, LANES), 1)
-                    packed = jnp.where((lane >= REACH_Z * q) & (lane < REACH_Z * (q + 1)), moved, packed)
+            for item, at, width in row:
+                shift = jnp.where(core == 1, (at + width) % LANES, at)
+                field, plane = plane_of(item)
+                packed = jnp.where((lane >= at) & (lane < at + width), pltpu.roll(fields[field][plane], shift, 1), packed)
             z_out[m, rows] = packed
 
 
@@ -213,12 +245,10 @@
 
 
 def down_kernel(geo, *refs):
-    ins, refs = refs[:8], refs[8:]
-    (packed_any, even_any, odd_any, passed,
-     own_in, sib_in, even_own, odd_own, even_sib, odd_sib, z_in, zx_in,
+    (own_in, sib_in, even_own, odd_own, even_sib, odd_sib, z_in, zx_in, packed_any, even_any, odd_any, passed,
      packed_out, even_out, odd_out,
      k0, cx, cy, cz, iv, ds, g0, g, d1, d2,
-     k1, ex, ey, ez, ei, es, h0, h, f1, f2, u1, half_y, half_y1, sems, in_sems) = refs
+     k1, ex, ey, ez, ei, es, h0, h, f1, f2, u1, half_y, half_y1, sems) = refs
     core = core_of()
     ix, nx = lax.axis_index("gx"), lax.axis_size("gx")
     iz, nz = lax.axis_index("gz"), lax.axis_size("gz")
@@ -227,15 +257,15 @@
     lo_there, hi_there = ix > 0, ix < nx - 1
     even = lax.rem(ix, 2) == 0
 
-    arrivals = fetch(list(zip(ins, (
-        own_in, sib_in, even_own, odd_own, even_sib, odd_sib, z_in, zx_in))), in_sems)
-
     lane = lanes_of((yw, LANES))
-    halo_lanes = jnp.where(core == 0, lane - (LANES - REACH_Z), REACH_Z - 1 - lane) >= 0
-    base = jnp.where(core == 0, LANES - REACH_Z, 0)
-
-    def strip(ref, p):
-        return pltpu.roll(ref[p // SLOTS], lax.rem(base - REACH_Z * (p % SLOTS) + LANES, LANES), 1)
+
+    def strip(ref, m, at, width):
+        shift = jnp.where(core == 0, (2 * LANES - width - at) % LANES, (LANES - at) % LANES)
+        return pltpu.roll(ref[m], shift, 1)
+
+    def merge(window, at, width, there, moved):
+        halo = jnp.where(core == 0, lane - (LANES - width), width - 1 - lane) >= 0
+        window[at] = jnp.where(halo, jnp.where(there, moved, 0.0), window[at])
 
     own_rows = pl.ds(pl.multiple_of(core * ye, 8), ye)
     sib_rows = pl.ds(pl.multiple_of((1 - core) * ye, 8), ye)
@@ -251,28 +281,28 @@
             window[pl.ds(1 + REACH_X - width, width), rows] = jnp.where(lo_there, jnp.where(even, o, e), 0.0)
             window[pl.ds(1 + REACH_X + bx, width), rows] = jnp.where(hi_there, jnp.where(even, e, o), 0.0)
 
-    for copy in arrivals:
-        copy.wait()
     for window, at, _, _ in windows:
         window[pl.ds(1 + REACH_X, bx), own_rows] = own_in[pl.ds(at, bx)]
         window[pl.ds(1 + REACH_X, bx), sib_rows] = sib_in[pl.ds(at, bx)]
     halos(even_own, odd_own, own_rows)
     halos(even_sib, odd_sib, sib_rows)
-    for slot, plane in enumerate(strip_planes(bx)):
-        if plane is not None:
-            window, at = windows[plane[0]][0], 1 + REACH_X + plane[1]
-            window[at] = jnp.where(halo_lanes, jnp.where(z_there, strip(z_in, slot), 0.0), window[at])
-    for window, _, width, slot in windows:
-        for p in range(width):
-            e, o = strip(zx_in, slot + p), strip(zx_in, SLAB * SLOTS + slot + p)
-            at = 1 + REACH_X - width + p
-            low = jnp.where(z_there & lo_there, jnp.where(even, o, e), 0.0)
-            window[at] = jnp.where(halo_lanes, low, window[at])
-            at = 1 + REACH_X + bx + p
-            high = jnp.where(z_there & hi_there, jnp.where(even, e, o), 0.0)
-            window[at] = jnp.where(halo_lanes, high, window[at])
-
-    grid = Grid(xw, yw, LANES, 1, 1, False, 8)
+    for m, row in enumerate(box_slots(bx)):
+        for (f, p), at, width in row:
+            merge(windows[f][0], 1 + REACH_X + p, width, z_there, strip(z_in, m, at, width))
+    places = {item: (m, at, width) for m, row in enumerate(halo_slots()) for item, at, width in row}
+    for (pair, f, x), place in places.items():
+        if pair == 0:
+            window, width = windows[f][0], place[2]
+            e, o = strip(zx_in, *place), strip(zx_in, *places[1, f, x])
+            merge(window, 1 + REACH_X - x, width, z_there & lo_there, jnp.where(even, o, e))
+            merge(window, REACH_X + bx + x, width, z_there & hi_there, jnp.where(even, e, o))
+
+    grid = Grid(xw, yw, LANES, 1, 1, False, geo["chunk0"])
+    inner = Grid(xw - 8, yw, LANES, 1, 1, False, geo["chunk0_inner"])
+    nothing = jnp.zeros((4, yw, LANES), jnp.float32)
+    for ref in (g, d2):
+        ref[pl.ds(1, 4)] = nothing
+        ref[pl.ds(xw - 3, 4)] = nothing
 
     def first(at, here, inverse):
         scaled = g0[here] * inverse
@@ -320,20 +350,20 @@
         g[here] = value
         d2[here] = direction
 
-    grid.step(coeffs, d1, g0, *FACTORS[1], second)
+    inner.step(coeffs, d1, g0, *FACTORS[1], second, 5)
 
     def third(here, v, value, direction):
         g[here] = value
         k0[here] = d1[here] + v + direction
         d1[here] = direction
 
-    grid.step(coeffs, d2, g, *FACTORS[2], third)
+    inner.step(coeffs, d2, g, *FACTORS[2], third, 5)
     send(k0, own0, wide0)
 
     def residual(here, v, value, direction):
         g[here] = value * ds[here]
 
-    grid.step(coeffs, d1, g, 0.0, None, residual)
+    inner.step(coeffs, d1, g, 0.0, None, residual, 5)
 
     restrict(g, put_b1, half_y, x1, 1, 0, yw, 1)
     grid1 = Grid(x1, y1, LANES, 1, 2, False, geo["chunk1"])
@@ -368,11 +398,18 @@
     send(u1, own1, wide1)
     mine = 1 + REACH_X // 2
     last = mine + bx // 2
-    for source, low, high, at, count in ((u1, mine + 1, last - WIN1, 0, 5), (h0, mine + 3, last - 5, 5, 2)):
+    for source, low, high, at, count in ((u1, mine, last - WIN1, 0, 6), (h0, mine + 2, last - 5, 6, 3)):
         low, high = source[pl.ds(low, count)], source[pl.ds(high, count)]
         even_out[pl.ds(at, count)] = jnp.where(even, high, low)
         odd_out[pl.ds(at, count)] = jnp.where(even, low, high)
-    copies += fetch(((even_out, even_any), (odd_out, odd_any)), sems, 12)
+
+    def leave(source, target):
+        copy = pltpu.make_async_copy(source, target, sems.at[len(copies)])
+        copy.start()
+        copies.append(copy)
+
+    leave(even_out, even_any)
+    leave(odd_out, odd_any)
 
     def residual1(here, v, value, direction):
         h[here] = value * es[here]
@@ -388,13 +425,13 @@
         boxes = []
         restrict(source, lambda i, v, boxes=boxes: boxes.append(v), half_y1, x2, 1 + REACH_X // 2, geo["oy"] // 2, 2 * y2, 2)
         stacked = jnp.concatenate(boxes, axis=0)
-        picked = jnp.dot(stacked, pick, precision=lax.Precision.HIGHEST, preferred_element_type=jnp.float32)
+        picked = picked_lanes(stacked, pick)
         packed = jnp.zeros((y2, LANES), jnp.float32)
         for p in range(x2):
             packed = jnp.where(slot == lax.rem(p + place, 8), picked[p * y2:(p + 1) * y2], packed)
         for j in range(packed_out.shape[0]):
             packed_out[j, f] = packed
-    copies += fetch(((packed_out, packed_any),), sems, 14)
+    leave(packed_out, packed_any)
     for copy in copies:
         copy.wait()
 
@@ -407,7 +444,7 @@
         del refs[:count]
         return taken
 
-    any_gathered, any_even, any_odd = take(3)
+    arriving = take(3)
     views = passed_views(geo, take(1)[0])
     in0, in1 = views[:6], views[6:]
     send_u, send_r, keep_u, keep_r = take(4)
@@ -425,7 +462,10 @@
     x2, y2, z2 = geo["x2"], geo["y2"], geo["z2"]
     wide0, wide1 = bx + 2 * WIN0, bx // 2 + 2 * WIN1
 
-    arrivals = fetch(((any_gathered, gathered), (any_even, from_even), (any_odd, from_odd)), sems, 12)
+    arrivals = []
+    for source, target in zip(arriving, (gathered, from_even, from_odd)):
+        arrivals.append(pltpu.make_async_copy(source, target, sems.at[16 + len(arrivals)]))
+        arrivals[-1].start()
     copies = []
     for sources, targets, wide in ((in1, (cx1, cy1, cz1, iv1, g01, w1), wide1), (in0, (cx0, cy0, cz0, iv0, g00, w0), wide0)):
         for i, (source, target) in enumerate(zip(sources, targets)):
@@ -483,25 +523,31 @@
 
         grid.step(coeffs, da, g, 0.0, None, residual)
 
-    def post(grid, coeffs, g0, u, g, da, db, result):
+    def post(grid, coeffs, g0, u, g, da, db, result, shrink=0):
+        def step(i, *args):
+            part = Grid(grid.x - 2 * i * shrink, grid.y, grid.z, grid.sy, grid.sz, grid.whole_z, grid.size)
+            if shrink:
+                part.size = part.x if grid.size == grid.x else 2
+            part.step(coeffs, *args, 1 + i * shrink)
+
         def one(here, v, value, direction):
             g[here] = value
             da[here] = direction
 
-        grid.step(coeffs, u, g0, *FACTORS[0], one)
+        step(1, u, g0, *FACTORS[0], one)
 
         def two(here, v, value, direction):
             g[here] = value
             db[here] = direction
 
-        grid.step(coeffs, da, g, *FACTORS[1], two)
+        step(2, da, g, *FACTORS[1], two)
 
         def three(here, v, value, direction):
             g[here] = value
             result[here] = u[here] + da[here] + v + direction
             da[here] = direction
 
-        grid.step(coeffs, db, g, *FACTORS[2], three)
+        step(3, db, g, *FACTORS[2], three)
 
     def restrict(fine, coarse, count, shift):
         for i in range(count):
@@ -561,7 +607,7 @@
     start = (bx // 4) * ix
     rows = pl.ds(pl.multiple_of(8 * yp, 8), y2w) if pad_y else pl.ds(0, y2w)
     window = e2_wide[pl.ds(start, x2w), rows].reshape(x2w * y2w, z2)
-    window = jnp.dot(window, pick, precision=lax.Precision.HIGHEST, preferred_element_type=jnp.float32)
+    window = picked_lanes(window, pick)
     window = window.reshape(x2w, y2w, LANES)
 
     def place_rows(target, plane, v, count):
@@ -574,7 +620,7 @@
     for copy in copies[:6]:
         copy.wait()
     even, last1 = lax.rem(ix, 2) == 0, 1 + WIN1 + bx // 2
-    for target, low, high, at, count in ((w1, 1, last1 + 1, 0, 5), (g01, 2, last1 + 3, 5, 2)):
+    for target, low, high, at, count in ((w1, 1, last1, 0, 6), (g01, 2, last1 + 2, 6, 3)):
         e, o = from_even[pl.ds(at, count)], from_odd[pl.ds(at, count)]
         low, high = pl.ds(low, count), pl.ds(high, count)
         target[low] = jnp.where(ix > 0, jnp.where(even, o, e), target[low])
@@ -590,11 +636,11 @@
         u1[here] = jnp.where(iv1[here] > 0.0, w1[here] + u1[here], 0.0)
 
     chunks(wide1, start1, grid1.size)
-    post(grid1, (cx1, cy1, cz1, iv1), g01, u1, g1, da1, db1, e1)
+    post(grid1, (cx1, cy1, cz1, iv1), g01, u1, g1, da1, db1, e1, 1)
 
     for copy in copies[6:]:
         copy.wait()
-    grid0 = Grid(wide0, yw, LANES, 1, 1, False, 8)
+    grid0 = Grid(wide0, yw, LANES, 1, 1, False, geo["chunk_up"])
 
     def fill(i, carry):
         at = WIN1 + 1 - WIN0 // 2 + i
@@ -611,17 +657,27 @@
 
     chunks(wide0, start0, grid0.size)
     coeffs0 = (cx0, cy0, cz0, iv0)
-    post(grid0, coeffs0, g00, u0, g0, da0, db0, w0)
-
-    def residual(here, v, value, direction):
-        g0[here] = value / iv0[here]
-
-    grid0.step(coeffs0, da0, g0, 0.0, None, residual, 1 + WIN0, bx)
+    post(grid0, coeffs0, g00, u0, g0, da0, db0, w0, 1)
+
     own = pl.ds(1 + WIN0, bx)
     own_rows = pl.ds(pl.multiple_of(geo["oy"] + core * by, 8), by)
     sib_rows = pl.ds(pl.multiple_of(geo["oy"] + (1 - core) * by, 8), by)
-    leaving = fetch(((w0.at[own, sib_rows], send_u), (g0.at[own, sib_rows], send_r),
-                     (w0.at[own, own_rows], keep_u), (g0.at[own, own_rows], keep_r)), sems, 15)
+    leaving = []
+
+    def leave(source, rows, target):
+        copy = pltpu.make_async_copy(source.at[own, rows], target, sems.at[12 + len(leaving)])
+        copy.start()
+        leaving.append(copy)
+
+    leave(w0, sib_rows, send_u)
+    leave(w0, own_rows, keep_u)
+
+    def residual(here, v, value, direction):
+        g0[here] = value / iv0[here]
+
+    Grid(bx, yw, LANES, 1, 1, False, geo["chunk_last"]).step(coeffs0, da0, g0, 0.0, None, residual, 1 + WIN0)
+    leave(g0, sib_rows, send_r)
+    leave(g0, own_rows, keep_r)
     for copy in leaving:
         copy.wait()
 
@@ -681,7 +737,8 @@
     yw = 2 * ye
     xw = bx + 2 * REACH_X
     geo = dict(
-        bx=bx, by=by, ye=ye, yw=yw, xw=xw, oy=(yw - 2 * by) // 2, chunk1=14 if yw == 32 else 4,
+        bx=bx, by=by, ye=ye, yw=yw, xw=xw, oy=(yw - 2 * by) // 2, chunk0=56 if yw == 32 else 4, chunk0_inner=48 if yw == 32 else 4,
+        chunk_up=40 if yw == 32 else 4, chunk_last=32 if yw == 32 else 4, chunk1=28 if yw == 32 else 4,
         packed=pairs == 1 and 32 * nz == LANES, x2=bx // 4 * nx, y2=by // 4 * ny, z2=bz // 4 * nz,
         pad_y=(yw // 4 - by // 2) // 2,
     )
@@ -691,54 +748,53 @@
     high = jnp.concatenate([own[bx - REACH_XB:bx], own[2 * bx - REACH_X:]], 0)
     low = jnp.concatenate([own[:REACH_XB], own[bx:bx + REACH_X]], 0)
     even_own = paired(jnp.where(even, high, low), 0)
-    odd_own = paired(jnp.where(even, low, high), 1)
-    sib = sibling(own)
-    anywhere, hbm = pl.BlockSpec(memory_space=pl.ANY), pl.BlockSpec(memory_space=pltpu.HBM)
-
-    def call(name, kernel, ins, outs, scratch, hbm_ins=0, hbm_outs=0, limit=0):
-        held = sum(4 * math.prod(v.shape) for v in scratch if v.dtype == jnp.float32)
+    sib, odd_send = lax.optimization_barrier((sibling(own), jnp.where(even, low, high)))
+    odd_own = paired(odd_send, 1)
+    inside, hbm, anywhere = (pl.BlockSpec(memory_space=space) for space in (pltpu.VMEM, pltpu.HBM, pl.ANY))
+
+    def call(name, kernel, ins, outs, scratch, hbm_ins=0, hbm_outs=0, limit=0, operand=inside, result=inside):
+        held = sum(4 * math.prod(v.shape) for v in (*ins, *outs, *scratch) if v.dtype == jnp.float32)
         return pl.pallas_call(
-            kernel, out_shape=outs, in_specs=[anywhere] * (len(ins) - hbm_ins) + [hbm] * hbm_ins,
-            out_specs=[anywhere] * (len(outs) - hbm_outs) + [hbm] * hbm_outs,
+            kernel, out_shape=outs, in_specs=[operand] * (len(ins) - hbm_ins) + [hbm] * hbm_ins,
+            out_specs=[result] * (len(outs) - hbm_outs) + [hbm] * hbm_outs,
             scratch_shapes=scratch, name=name,
             compiler_params=pltpu.CompilerParams(vmem_limit_bytes=max(limit, held + 6 * 1024 * 1024)),
+            cost_estimate=pl.CostEstimate(flops=4_000_000, bytes_accessed=8_000_000, transcendentals=0),
         )(*ins)
 
     def vmem(shape):
         return pltpu.VMEM(shape, jnp.float32)
 
-    def pack(name, lists, ins, later=()):
-        shape = (len(lists) // SLOTS, yw, LANES)
-        return pl.pallas_call(
-            functools.partial(pack_kernel, geo, lists, len(ins)),
-            out_shape=array(*shape), in_specs=[anywhere] * (len(ins) + len(later)),
-            scratch_shapes=[vmem(v.shape) for v in ins] + [pltpu.SemaphoreType.DMA((len(ins),))],
-            compiler_params=pltpu.CompilerParams(vmem_limit_bytes=8 * 1024 * 1024 * max(1, yw // 32)), name=name,
-            cost_estimate=pl.CostEstimate(flops=4_000_000, bytes_accessed=8_000_000, transcendentals=0),
-        )(*ins, *later)
-
-    z_send = pack("pack_box", [p and (0, p[0] * bx + p[1]) for p in strip_planes(bx)], (own, sib))
+    def pack(name, slots, plane_of, ins, later=()):
+        kernel = functools.partial(pack_kernel, geo, slots, plane_of, len(ins))
+        return call(name, kernel, (*ins, *later), [array(len(slots), yw, LANES)], [], len(later))[0]
+
+    z_send = pack("pack_box", box_slots(bx), lambda item: (0, item[0] * bx + item[1]), (own, sib))
     z_in = facing(z_send)
     even_own, odd_own, z_send = lax.optimization_barrier((even_own, odd_own, z_send))
     even_sib, odd_sib = sibling(even_own), sibling(odd_own)
-    slab = [(0, p) for p in range(REACH_X + REACH_XB)]
-    slab += [None] * (SLAB * SLOTS - len(slab))
-    slabs = slab + [p and (1, p[1]) for p in slab]
-    zx_in = facing(pack("pack_halo", slabs, (even_own, odd_own, even_sib, odd_sib), (z_in,)))
+
+    def halo_plane(item):
+        pair, field, x = item
+        first, count = (0, REACH_XB) if field == 0 else (REACH_XB, REACH_X)
+        from_above = (lax.rem(lax.axis_index("gx"), 2) == 0) == (pair == 0)
+        return pair, first + jnp.where(from_above, x - 1, count - x)
+
+    zx_in = facing(pack("pack_halo", halo_slots(), halo_plane, (even_own, odd_own, even_sib, odd_sib), (z_in,)))
 
     wide0, wide1 = bx + 2 * WIN0, bx // 2 + 2 * WIN1
     x1, y1 = xw // 2, yw // 2
     some0 = vmem((xw + 2, yw, LANES))
     some1 = vmem((x1 + 2, y1, LANES))
     passed = array(6 * (wide0 + 1) + 3 * (wide1 + 1), yw, LANES)
-    edge = 7
+    edge = 9
     ins = (own, sib, even_own, odd_own, even_sib, odd_sib, z_in, zx_in)
     sends = [array(nx * ny * nz if geo["packed"] else 1, 2, by // 2, LANES), array(edge, y1, LANES), array(edge, y1, LANES)]
     down = call(
         "down", functools.partial(down_kernel, geo), ins, sends + [passed],
-        [vmem(v.shape) for v in ins] + [vmem(v.shape) for v in sends] + [some0] * 10 + [some1] * 11
-        + [vmem((6, yw, LANES)), vmem((6, y1, LANES)), pltpu.SemaphoreType.DMA((15,)), pltpu.SemaphoreType.DMA((8,))],
-        hbm_outs=1, limit=VMEM_LIMIT,
+        [vmem(v.shape) for v in sends] + [some0] * 10 + [some1] * 11
+        + [vmem((6, yw, LANES)), vmem((6, y1, LANES)), pltpu.SemaphoreType.DMA((15,))],
+        hbm_outs=1, limit=VMEM_LIMIT, result=anywhere,
     )
     packed, even_send, odd_send, passed = down[0], down[1], down[2], down[3]
     from_even, from_odd = paired(even_send, 0), paired(odd_send, 1)
@@ -762,7 +818,7 @@
         + [level(wide1, y1, LANES)] * 11 + [level(wide0, yw, LANES)] * 10
         + [vmem((x2 + 8, y2 + 2 * geo["pad_y"], z2)), vmem(gathered.shape), vmem(from_even.shape), vmem(from_odd.shape)]
         + [pltpu.SemaphoreType.DMA((19,))],
-        hbm_ins=1, limit=VMEM_LIMIT,
+        hbm_ins=1, limit=VMEM_LIMIT, operand=anywhere, result=anywhere,
     )
     mine = lanes_of((1, 1, LANES)) // HALF == core
     return jnp.where(mine, keep_u, sibling(send_u)), jnp.where(mine, keep_r, sibling(send_r))

time: 60.6 us -> 52.7 us (0.87)
  Pallas kernels: 18.4 us -> 12.8 us
  waiting for transfers between devices: 17.4 us -> 13.6 us
  starting transfers between devices: 21.8 us -> 23.4 us
    pallas_call x4, Pallas kernels: 18.4 us -> 12.8 us  [call(): pl.pallas_call(kernel, out_shape=outs, in_specs=[operand] * (len(ins) - h...]
    all_to_all x1, starting transfers between devices: 10.4 us -> 14.7 us  [on_device(): gathered = lax.all_to_all(packed, AXES, 0, 0, tiled=True)]
    ppermute x4, waiting for transfers between devices: 10.5 us -> 7.11 us  [paired(): return lax.ppermute(v, 'gx', perm)]
    ppermute x4, starting transfers between devices: 8.45 us -> 5.73 us  [paired(): return lax.ppermute(v, 'gx', perm)]
where the time goes in v3:
time: 52.7 us; the launch traced here: 52.4 us
  starting transfers between devices  23.4 us (44%)
  waiting for transfers between devices  13.6 us (26%)
  Pallas kernels  12.8 us (24%)
  other arithmetic  1.95 us (4%)
  between operations  0.73 us (1%)
    all_to_all x1, starting transfers between devices, on_device(): gathered = lax.all_to_all(packed, AXES, 0, 0, tiled=True)  14.7 us
    pallas_call x4, Pallas kernels, call(): pl.pallas_call(kernel, out_shape=outs, in_specs=[operand] * (len(ins) - h...  12.8 us
    ppermute x4, waiting for transfers between devices, paired(): return lax.ppermute(v, 'gx', perm)  7.11 us
    ppermute x4, starting transfers between devices, paired(): return lax.ppermute(v, 'gx', perm)  5.73 us
    all_to_all x1, waiting for transfers between devices, on_device(): gathered = lax.all_to_all(packed, AXES, 0, 0, tiled=True)  3.91 us
    ppermute x5, waiting for transfers between devices, sibling(): return lax.ppermute(v, 'gy', [(i, i ^ 1) for i in range(ny)])  2.55 us
    ppermute x5, starting transfers between devices, sibling(): return lax.ppermute(v, 'gy', [(i, i ^ 1) for i in range(ny)])  1.6 us
    ppermute x2, starting transfers between devices, facing(): lax.ppermute(v, AXES, [(i, perm.get(i, i)) for i in range(nx * ny * nz)])  1.34 us
  transfers between devices with their start and end apart: 12, of which 7 were waited for; matrix products, arithmetic and copies ran while one was open for 0% of the time, Pallas kernels for 1%

profile of v3, /device:TPU:0, one launch (start us, length us, event | category | flops | bytes accessed | tf_op | source)
XLA Modules:
  0.0 52.4 jit_solution(13682038236934008617)
XLA Ops:
  0.6 1.1 %pad_maximum_fusion.refs_0_ = f32[64,16,128]{2,1,0:T(8,128)S(1)} fusion(f32[32,16,128]{2,1,0:T(8,128)} %param.3, f32[32,16,128]{2,1,0:T(8,128)} %param.2), kind=kLoop, calls=%fused_computation | loop fusion | flops 131072 | bytes 1048576 | tf_op jit(solution)/shard_map/concatenate | solution.py:746
  1.7 0.5 collective-permute-start
  2.3 2.6 %collective-permute-start.1 = (f32[21,16,128]{2,1,0:T(8,128)S(1)}, f32[21,16,128]{2,1,0:T(8,128)S(1)}, u32[]{:S(2)}, u32[]{:S(2)}) collective-permute-start(f32[21,16,128]{2,1,0:T(8,128)S(1)} %get-tuple-element.30), channel_id=1, source_target_pairs={{0,8},{8,0},{16,24},{24,16},{1,9},{9,1},{17,25},{25,17},{2,10},{10... | collective-permute-start | bytes 516104 | tf_op jit(solution)/shard_map/ppermute | solution.py:711
  4.9 0.0 collective-permute-done.refs_1_
  4.9 0.7 %collective-permute-start.2 = (f32[21,16,128]{2,1,0:T(8,128)S(1)}, f32[21,16,128]{2,1,0:T(8,128)S(1)}, u32[]{:S(2)}, u32[]{:S(2)}) collective-permute-start(f32[21,16,128]{2,1,0:T(8,128)S(1)} %get-tuple-element.15), channel_id=1, source_target_pairs={{0,0},{8,16},{16,8},{24,24},{1,1},{9,17},{17,9},{25,25},{2,2},{10,... | collective-permute-start | bytes 516104 | tf_op jit(solution)/shard_map/ppermute | solution.py:711
  5.5 0.3 pack_box.1
  5.9 0.7 %collective-permute-start.5 = (f32[11,32,128]{2,1,0:T(8,128)S(1)}, f32[11,32,128]{2,1,0:T(8,128)S(1)}, u32[]{:S(2)}, u32[]{:S(2)}) collective-permute-start(f32[11,32,128]{2,1,0:T(8,128)S(1)} %pack_box.1), channel_id=1, source_target_pairs={{0,0},{1,4},{2,5},{3,6},{4,1},{5,2},{6,3},{7,7},{8,8},{9,12},{10,1... | collective-permute-start | bytes 540680 | tf_op jit(solution)/shard_map/ppermute | solution.py:719
  6.6 3.3 %collective-permute-done.1.refs_0_.refs_2_ = f32[21,16,128]{2,1,0:T(8,128)S(1)} collective-permute-done((f32[21,16,128]{2,1,0:T(8,128)S(1)}, f32[21,16,128]{2,1,0:T(8,128)S(1)}, u32[]{:S(2)}, u32[]{:S(2)}) %collective-permute-start.1) | collective-permute-done | bytes 172064 | tf_op jit(solution)/shard_map/ppermute | solution.py:711
  9.9 0.0 collective-permute-done.2.refs_1_.refs_3_
  9.9 0.0 collective-permute-start.3
  9.9 0.5 collective-permute-start.4
  10.4 0.0 collective-permute-done.5.refs_4_.refs_6_
  10.4 0.9 %collective-permute-done.3.refs_2_.refs_4_ = f32[21,16,128]{2,1,0:T(8,128)S(1)} collective-permute-done((f32[21,16,128]{2,1,0:T(8,128)S(1)}, f32[21,16,128]{2,1,0:T(8,128)S(1)}, u32[]{:S(2)}, u32[]{:S(2)}) %collective-permute-start.3) | collective-permute-done | bytes 172064 | tf_op jit(solution)/shard_map/ppermute | solution.py:702
  11.3 0.2 collective-permute-done.4.refs_3_.refs_5_
  11.5 0.2 pack_halo.1
  11.8 0.7 %collective-permute-start.6 = (f32[4,32,128]{2,1,0:T(8,128)S(1)}, f32[4,32,128]{2,1,0:T(8,128)S(1)}, u32[]{:S(2)}, u32[]{:S(2)}) collective-permute-start(f32[4,32,128]{2,1,0:T(8,128)S(1)} %pack_halo.1), channel_id=1, source_target_pairs={{0,0},{1,4},{2,5},{3,6},{4,1},{5,2},{6,3},{7,7},{8,8},{9,12},{10,1... | collective-permute-start | bytes 196616 | tf_op jit(solution)/shard_map/ppermute | solution.py:719
  12.5 0.0 collective-permute-done.6.refs_7_
  12.5 5.7 %down.1 = (f32[32,2,8,128]{3,2,1,0:T(8,128)}, f32[9,16,128]{2,1,0:T(8,128)S(1)}, f32[9,16,128]{2,1,0:T(8,128)S(1)}, f32[333,32,128]{2,1,0:T(8,128)}) custom-call(f32[64,16,128]{2,1,0:T(8,128)S(1)} %pad_maximum_fusion.refs_0_, f32[64,16,128]{2,1,0:T(8,128)S(1)} %collective-permute-done.refs_1_, f32[21,16,128]{2,1,0:T(8,128)S(1)} %collective-permute-done.1.refs_0_.refs_2_, ...), custom_call_target="tpu_custom_call" | custom-call | flops 4000000 | bytes 8000000 | tf_op jit(solution)/shard_map/down/pallas_call | solution.py:757
  18.2 14.7 %all-to-all-start = ((f32[32,2,8,128]{3,2,1,0:T(8,128)}), f32[32,2,8,128]{3,2,1,0:T(8,128)S(1)}, u32[]{:S(2)}, u32[]{:S(2)}) async-start(f32[32,2,8,128]{3,2,1,0:T(8,128)} %get-tuple-element.18), calls=%async_computation | async-start | bytes 524288 | tf_op jit(solution)/shard_map/all_to_all | solution.py:803
  32.9 1.8 %collective-permute-start.7 = (f32[9,16,128]{2,1,0:T(8,128)S(1)}, f32[9,16,128]{2,1,0:T(8,128)S(1)}, u32[]{:S(2)}, u32[]{:S(2)}) collective-permute-start(f32[9,16,128]{2,1,0:T(8,128)S(1)} %get-tuple-element.19), channel_id=1, source_target_pairs={{0,8},{8,0},{16,24},{24,16},{1,9},{9,1},{17,25},{25,17},{2,10},{10... | collective-permute-start | bytes 221192 | tf_op jit(solution)/shard_map/ppermute | solution.py:711
  34.7 0.7 %collective-permute-start.8 = (f32[9,16,128]{2,1,0:T(8,128)S(1)}, f32[9,16,128]{2,1,0:T(8,128)S(1)}, u32[]{:S(2)}, u32[]{:S(2)}) collective-permute-start(f32[9,16,128]{2,1,0:T(8,128)S(1)} %get-tuple-element.20), channel_id=1, source_target_pairs={{0,0},{8,16},{16,8},{24,24},{1,1},{9,17},{17,9},{25,25},{2,2},{10,... | collective-permute-start | bytes 221192 | tf_op jit(solution)/shard_map/ppermute | solution.py:711
  35.4 3.8 %collective-permute-done.7.refs_1_ = f32[9,16,128]{2,1,0:T(8,128)S(1)} collective-permute-done((f32[9,16,128]{2,1,0:T(8,128)S(1)}, f32[9,16,128]{2,1,0:T(8,128)S(1)}, u32[]{:S(2)}, u32[]{:S(2)}) %collective-permute-start.7) | collective-permute-done | bytes 73760 | tf_op jit(solution)/shard_map/ppermute | solution.py:711
  39.2 0.0 collective-permute-done.8.refs_2_
  39.2 3.9 %all-to-all-done.refs_0_ = f32[32,2,8,128]{3,2,1,0:T(8,128)S(1)} async-done(((f32[32,2,8,128]{3,2,1,0:T(8,128)}), f32[32,2,8,128]{3,2,1,0:T(8,128)S(1)}, u32[]{:S(2)}, u32[]{:S(2)}) %all-to-all-start) | async-done | bytes 262176 | tf_op jit(solution)/shard_map/all_to_all | solution.py:803
  43.1 6.5 %up.1 = (f32[32,16,128]{2,1,0:T(8,128)S(1)}, f32[32,16,128]{2,1,0:T(8,128)S(1)}, f32[32,16,128]{2,1,0:T(8,128)S(1)}, f32[32,16,128]{2,1,0:T(8,128)S(1)}) custom-call(f32[32,2,8,128]{3,2,1,0:T(8,128)S(1)} %all-to-all-done.refs_0_, f32[9,16,128]{2,1,0:T(8,128)S(1)} %collective-permute-done.7.refs_1_, f32[9,16,128]{2,1,0:T(8,128)S(1)} %collective-permute-done.8.refs_2_, ...), custom_call_target="tpu_custom_call" | custom-call | flops 4000000 | bytes 8000000 | tf_op jit(solution)/shard_map/up/pallas_call | solution.py:757
  49.6 0.5 collective-permute-start.9
  50.0 0.1 collective-permute-start.10
  50.2 1.0 %collective-permute-done.9 = f32[32,16,128]{2,1,0:T(8,128)S(1)} collective-permute-done((f32[32,16,128]{2,1,0:T(8,128)S(1)}, f32[32,16,128]{2,1,0:T(8,128)S(1)}, u32[]{:S(2)}, u32[]{:S(2)}) %collective-permute-start.9) | collective-permute-done | bytes 262176 | tf_op jit(solution)/shard_map/ppermute | solution.py:702
  51.2 0.4 collective-permute-done.10
  51.6 0.9 %broadcast_select_fusion = (f32[32,16,128]{2,1,0:T(8,128)}, f32[32,16,128]{2,1,0:T(8,128)}) fusion(f32[32,16,128]{2,1,0:T(8,128)S(1)} %get-tuple-element.24, f32[32,16,128]{2,1,0:T(8,128)S(1)} %collective-permute-done.10, pred[128]{0:T(512)(128)(4,1)S(1)} %fusion.2, f32[32,16,128]{2,1,0:T(8,128)S(1)} %get-tuple-element.22, ...), kind=kLoop, calls=%fused_computation.5 | loop fusion | flops 131072 | bytes 1572992 | tf_op jit(solution)/shard_map/jit(_where)/select_n | solution.py:824
  (4 shorter events, 0.1 us)
Async XLA Ops:
  1.7 3.2 %collective-permute-start = (f32[64,16,128]{2,1,0:T(8,128)S(1)}, f32[64,16,128]{2,1,0:T(8,128)S(1)}, u32[]{:S(2)}, u32[]{:S(2)}) collective-permute-start(f32[64,16,128]{2,1,0:T(8,128)S(1)} %pad_maximum_fusion.refs_0_), channel_id=1, source_target_pairs={{0,4},{4,0},{1,5},{5,1},{2,6},{6,2},{3,7},{7,3},{8,12},{12,8},{9,1... | collective-permute-start | bytes 1572872 | tf_op jit(solution)/shard_map/ppermute | solution.py:702
  2.3 7.6 %collective-permute-start.1 = (f32[21,16,128]{2,1,0:T(8,128)S(1)}, f32[21,16,128]{2,1,0:T(8,128)S(1)}, u32[]{:S(2)}, u32[]{:S(2)}) collective-permute-start(f32[21,16,128]{2,1,0:T(8,128)S(1)} %get-tuple-element.30), channel_id=1, source_target_pairs={{0,8},{8,0},{16,24},{24,16},{1,9},{9,1},{17,25},{25,17},{2,10},{10... | collective-permute-start | bytes 516104 | tf_op jit(solution)/shard_map/ppermute | solution.py:711
  4.9 5.0 %collective-permute-start.2 = (f32[21,16,128]{2,1,0:T(8,128)S(1)}, f32[21,16,128]{2,1,0:T(8,128)S(1)}, u32[]{:S(2)}, u32[]{:S(2)}) collective-permute-start(f32[21,16,128]{2,1,0:T(8,128)S(1)} %get-tuple-element.15), channel_id=1, source_target_pairs={{0,0},{8,16},{16,8},{24,24},{1,1},{9,17},{17,9},{25,25},{2,2},{10,... | collective-permute-start | bytes 516104 | tf_op jit(solution)/shard_map/ppermute | solution.py:711
  5.9 4.5 %collective-permute-start.5 = (f32[11,32,128]{2,1,0:T(8,128)S(1)}, f32[11,32,128]{2,1,0:T(8,128)S(1)}, u32[]{:S(2)}, u32[]{:S(2)}) collective-permute-start(f32[11,32,128]{2,1,0:T(8,128)S(1)} %pack_box.1), channel_id=1, source_target_pairs={{0,0},{1,4},{2,5},{3,6},{4,1},{5,2},{6,3},{7,7},{8,8},{9,12},{10,1... | collective-permute-start | bytes 540680 | tf_op jit(solution)/shard_map/ppermute | solution.py:719
  9.9 1.4 %collective-permute-start.3 = (f32[21,16,128]{2,1,0:T(8,128)S(1)}, f32[21,16,128]{2,1,0:T(8,128)S(1)}, u32[]{:S(2)}, u32[]{:S(2)}) collective-permute-start(f32[21,16,128]{2,1,0:T(8,128)S(1)} %collective-permute-done.1.refs_0_.refs_2_), channel_id=1, source_target_pairs={{0,4},{4,0},{1,5},{5,1},{2,6},{6,2},{3,7},{7,3},{8,12},{12,8},{9,1... | collective-permute-start | bytes 516104 | tf_op jit(solution)/shard_map/ppermute | solution.py:702
  9.9 1.7 %collective-permute-start.4 = (f32[21,16,128]{2,1,0:T(8,128)S(1)}, f32[21,16,128]{2,1,0:T(8,128)S(1)}, u32[]{:S(2)}, u32[]{:S(2)}) collective-permute-start(f32[21,16,128]{2,1,0:T(8,128)S(1)} %collective-permute-done.2.refs_1_.refs_3_), channel_id=1, source_target_pairs={{0,4},{4,0},{1,5},{5,1},{2,6},{6,2},{3,7},{7,3},{8,12},{12,8},{9,1... | collective-permute-start | bytes 516104 | tf_op jit(solution)/shard_map/ppermute | solution.py:702
  11.8 0.7 %collective-permute-start.6 = (f32[4,32,128]{2,1,0:T(8,128)S(1)}, f32[4,32,128]{2,1,0:T(8,128)S(1)}, u32[]{:S(2)}, u32[]{:S(2)}) collective-permute-start(f32[4,32,128]{2,1,0:T(8,128)S(1)} %pack_halo.1), channel_id=1, source_target_pairs={{0,0},{1,4},{2,5},{3,6},{4,1},{5,2},{6,3},{7,7},{8,8},{9,12},{10,1... | collective-permute-start | bytes 196616 | tf_op jit(solution)/shard_map/ppermute | solution.py:719
  18.2 24.9 %all-to-all-start = ((f32[32,2,8,128]{3,2,1,0:T(8,128)}), f32[32,2,8,128]{3,2,1,0:T(8,128)S(1)}, u32[]{:S(2)}, u32[]{:S(2)}) async-start(f32[32,2,8,128]{3,2,1,0:T(8,128)} %get-tuple-element.18), calls=%async_computation | async-start | bytes 524288 | tf_op jit(solution)/shard_map/all_to_all | solution.py:803
  32.9 6.3 %collective-permute-start.7 = (f32[9,16,128]{2,1,0:T(8,128)S(1)}, f32[9,16,128]{2,1,0:T(8,128)S(1)}, u32[]{:S(2)}, u32[]{:S(2)}) collective-permute-start(f32[9,16,128]{2,1,0:T(8,128)S(1)} %get-tuple-element.19), channel_id=1, source_target_pairs={{0,8},{8,0},{16,24},{24,16},{1,9},{9,1},{17,25},{25,17},{2,10},{10... | collective-permute-start | bytes 221192 | tf_op jit(solution)/shard_map/ppermute | solution.py:711
  34.7 4.5 %collective-permute-start.8 = (f32[9,16,128]{2,1,0:T(8,128)S(1)}, f32[9,16,128]{2,1,0:T(8,128)S(1)}, u32[]{:S(2)}, u32[]{:S(2)}) collective-permute-start(f32[9,16,128]{2,1,0:T(8,128)S(1)} %get-tuple-element.20), channel_id=1, source_target_pairs={{0,0},{8,16},{16,8},{24,24},{1,1},{9,17},{17,9},{25,25},{2,2},{10,... | collective-permute-start | bytes 221192 | tf_op jit(solution)/shard_map/ppermute | solution.py:711
  49.6 1.6 %collective-permute-start.9 = (f32[32,16,128]{2,1,0:T(8,128)S(1)}, f32[32,16,128]{2,1,0:T(8,128)S(1)}, u32[]{:S(2)}, u32[]{:S(2)}) collective-permute-start(f32[32,16,128]{2,1,0:T(8,128)S(1)} %get-tuple-element.23), channel_id=1, source_target_pairs={{0,4},{4,0},{1,5},{5,1},{2,6},{6,2},{3,7},{7,3},{8,12},{12,8},{9,1... | collective-permute-start | bytes 786440 | tf_op jit(solution)/shard_map/ppermute | solution.py:702
  50.0 1.5 %collective-permute-start.10 = (f32[32,16,128]{2,1,0:T(8,128)S(1)}, f32[32,16,128]{2,1,0:T(8,128)S(1)}, u32[]{:S(2)}, u32[]{:S(2)}) collective-permute-start(f32[32,16,128]{2,1,0:T(8,128)S(1)} %get-tuple-element.25), channel_id=1, source_target_pairs={{0,4},{4,0},{1,5},{5,1},{2,6},{6,2},{3,7},{7,3},{8,12},{12,8},{9,1... | collective-permute-start | bytes 786440 | tf_op jit(solution)/shard_map/ppermute | solution.py:702

commit v4 on v3

--- a/solution.py
+++ b/solution.py
@@ -429,8 +429,12 @@
         packed = jnp.zeros((y2, LANES), jnp.float32)
         for p in range(x2):
             packed = jnp.where(slot == lax.rem(p + place, 8), picked[p * y2:(p + 1) * y2], packed)
-        for j in range(packed_out.shape[0]):
-            packed_out[j, f] = packed
+        if geo["packed"]:
+            for j in range(packed_out.shape[0]):
+                if (j // nz) % 2 == f:
+                    packed_out[j] = packed
+        else:
+            packed_out[f] = packed
     leave(packed_out, packed_any)
     for copy in copies:
         copy.wait()
@@ -444,7 +448,8 @@
         del refs[:count]
         return taken
 
-    arriving = take(3)
+    count = 2 if geo["packed"] else 1
+    arriving = take(count + 2)
     views = passed_views(geo, take(1)[0])
     in0, in1 = views[:6], views[6:]
     send_u, send_r, keep_u, keep_r = take(4)
@@ -453,7 +458,9 @@
     k4, cx4, cy4, cz4, iv4, g04, g4, da4, db4, e4 = take(10)
     cx1, cy1, cz1, iv1, g01, w1, u1, g1, da1, db1, e1 = take(11)
     cx0, cy0, cz0, iv0, g00, w0, u0, g0, da0, db0 = take(10)
-    e2_wide, gathered, from_even, from_odd, sems = take(5)
+    e2_wide, = take(1)
+    gathered = take(count)
+    from_even, from_odd, sems = take(3)
     core = core_of()
     ix, nx = lax.axis_index("gx"), lax.axis_size("gx")
     iz, nz = lax.axis_index("gz"), lax.axis_size("gz")
@@ -463,7 +470,7 @@
     wide0, wide1 = bx + 2 * WIN0, bx // 2 + 2 * WIN1
 
     arrivals = []
-    for source, target in zip(arriving, (gathered, from_even, from_odd)):
+    for source, target in zip(arriving, (*gathered, from_even, from_odd)):
         arrivals.append(pltpu.make_async_copy(source, target, sems.at[16 + len(arrivals)]))
         arrivals[-1].start()
     copies = []
@@ -486,12 +493,13 @@
                     merged = jnp.zeros((y2, LANES), jnp.float32)
                     for gz in range(nz):
                         for cc in range(2):
-                            here = gathered[(2 * gx + cc) * nz + gz, f]
+                            at = (2 * gx + cc) * nz + gz
+                            here = jnp.where(core == f, gathered[0][at], gathered[1][at])
                             merged = jnp.where(slot == (p + 2 * gz + cc) % 8, here, merged)
                     target[1 + 8 * gx + p] = pltpu.roll(merged, (LANES - 16 * p) % LANES, 1)
     else:
-        g02[pl.ds(1, x2)] = gathered[0]
-        k2[pl.ds(1, x2)] = gathered[1]
+        g02[pl.ds(1, x2)] = gathered[0][0]
+        k2[pl.ds(1, x2)] = gathered[0][1]
 
     def descend(grid, level, k, cx, cy, cz, iv, ds, g0, first_target):
         def first(at, here, inverse):
@@ -649,7 +657,7 @@
             place_rows(u0, 1 + 2 * i + j, spread_z(middle + 0.25 * side, 1, LANES, False), yw // 2)
         return carry
 
-    lax.fori_loop(0, wide0 // 2, fill, 0, unroll=4)
+    lax.fori_loop(0, wide0 // 2, fill, 0, unroll=10)
 
     def start0(at):
         here = pl.ds(at, grid0.size)
@@ -771,7 +779,8 @@
 
     z_send = pack("pack_box", box_slots(bx), lambda item: (0, item[0] * bx + item[1]), (own, sib))
     z_in = facing(z_send)
-    even_own, odd_own, z_send = lax.optimization_barrier((even_own, odd_own, z_send))
+    even_own, _ = lax.optimization_barrier((even_own, z_send))
+    odd_own, _ = lax.optimization_barrier((odd_own, z_send))
     even_sib, odd_sib = sibling(even_own), sibling(odd_own)
 
     def halo_plane(item):
@@ -789,7 +798,7 @@
     passed = array(6 * (wide0 + 1) + 3 * (wide1 + 1), yw, LANES)
     edge = 9
     ins = (own, sib, even_own, odd_own, even_sib, odd_sib, z_in, zx_in)
-    sends = [array(nx * ny * nz if geo["packed"] else 1, 2, by // 2, LANES), array(edge, y1, LANES), array(edge, y1, LANES)]
+    sends = [array(nx * ny * nz if geo["packed"] else 2, by // 2, LANES), array(edge, y1, LANES), array(edge, y1, LANES)]
     down = call(
         "down", functools.partial(down_kernel, geo), ins, sends + [passed],
         [vmem(v.shape) for v in sends] + [some0] * 10 + [some1] * 11
@@ -800,24 +809,26 @@
     from_even, from_odd = paired(even_send, 0), paired(odd_send, 1)
 
     if geo["packed"]:
-        gathered = lax.all_to_all(packed, AXES, 0, 0, tiled=True)
+        half = lax.all_to_all(packed, AXES, 0, 0, tiled=True)
+        half, from_even, from_odd = lax.optimization_barrier((half, from_even, from_odd))
+        gathered = (half, sibling(half))
     else:
         pieces = lax.all_gather(packed, AXES).reshape(nx, pairs, 2, nz, 2, by // 2, 8, 16)
         order = (jnp.arange(8) + 2 * jnp.arange(nz)[:, None, None] + jnp.arange(2)[:, None]) % 8
         order = jnp.transpose(order, (1, 0, 2))[None, None, :, :, None, None, :, None]
         pieces = jnp.take_along_axis(pieces, order, axis=6)
-        gathered = jnp.transpose(pieces, (4, 0, 6, 1, 5, 3, 2, 7)).reshape(2, geo["x2"], geo["y2"], geo["z2"])
+        gathered = (jnp.transpose(pieces, (4, 0, 6, 1, 5, 3, 2, 7)).reshape(2, geo["x2"], geo["y2"], geo["z2"]),)
 
     def level(planes, rows, lanes):
         return vmem((planes + 2, rows, lanes))
 
     x2, y2, z2 = geo["x2"], geo["y2"], geo["z2"]
     send_u, send_r, keep_u, keep_r = call(
-        "up", functools.partial(up_kernel, geo), (gathered, from_even, from_odd, passed), [array(bx, by, LANES)] * 4,
+        "up", functools.partial(up_kernel, geo), (*gathered, from_even, from_odd, passed), [array(bx, by, LANES)] * 4,
         [level(x2, y2, z2)] * 12 + [level(x2 // 2, y2, z2)] * 12 + [level(x2 // 4, y2, z2)] * 10
         + [level(wide1, y1, LANES)] * 11 + [level(wide0, yw, LANES)] * 10
-        + [vmem((x2 + 8, y2 + 2 * geo["pad_y"], z2)), vmem(gathered.shape), vmem(from_even.shape), vmem(from_odd.shape)]
-        + [pltpu.SemaphoreType.DMA((19,))],
+        + [vmem((x2 + 8, y2 + 2 * geo["pad_y"], z2)), *(vmem(v.shape) for v in gathered), vmem(from_even.shape), vmem(from_odd.shape)]
+        + [pltpu.SemaphoreType.DMA((20,))],
         hbm_ins=1, limit=VMEM_LIMIT, operand=anywhere, result=anywhere,
     )
     mine = lanes_of((1, 1, LANES)) // HALF == core

time: 52.7 us -> 52 us (0.987)
    ppermute x5 -> x6, waiting for transfers between devices: 2.55 us -> 3.87 us  [sibling(): return lax.ppermute(v, 'gy', [(i, i ^ 1) for i in range(ny)])]
    ppermute x4, waiting for transfers between devices: 7.11 us -> 6.18 us  [paired(): return lax.ppermute(v, 'gx', perm)]
    all_to_all x1, waiting for transfers between devices: 3.91 us -> 3.04 us  [on_device(): half = lax.all_to_all(packed, AXES, 0, 0, tiled=True)]
    ppermute x5 -> x6, starting transfers between devices: 1.6 us -> 1.61 us  [sibling(): return lax.ppermute(v, 'gy', [(i, i ^ 1) for i in range(ny)])]
  transfers between devices with their start and end apart: 12 -> 13, of which waited for: 7 -> 8; matrix products, arithmetic and copies ran while one was open for 0% -> 0% of each run, Pallas kernels for 1% -> 1%
where the time goes in v4:
time: 52 us; the launch traced here: 51.7 us
  starting transfers between devices  23.1 us (44%)
  waiting for transfers between devices  13.1 us (25%)
  Pallas kernels  12.8 us (25%)
  other arithmetic  1.95 us (4%)
  between operations  0.73 us (1%)
    all_to_all x1, starting transfers between devices, on_device(): half = lax.all_to_all(packed, AXES, 0, 0, tiled=True)  14.4 us
    pallas_call x4, Pallas kernels, call(): pl.pallas_call(kernel, out_shape=outs, in_specs=[operand] * (len(ins) - h...  12.8 us
    ppermute x4, waiting for transfers between devices, paired(): return lax.ppermute(v, 'gx', perm)  6.18 us
    ppermute x4, starting transfers between devices, paired(): return lax.ppermute(v, 'gx', perm)  5.73 us
    ppermute x6, waiting for transfers between devices, sibling(): return lax.ppermute(v, 'gy', [(i, i ^ 1) for i in range(ny)])  3.87 us
    all_to_all x1, waiting for transfers between devices, on_device(): half = lax.all_to_all(packed, AXES, 0, 0, tiled=True)  3.04 us
    ppermute x6, starting transfers between devices, sibling(): return lax.ppermute(v, 'gy', [(i, i ^ 1) for i in range(ny)])  1.61 us
    ppermute x2, starting transfers between devices, facing(): lax.ppermute(v, AXES, [(i, perm.get(i, i)) for i in range(nx * ny * nz)])  1.34 us
  transfers between devices with their start and end apart: 13, of which 8 were waited for; matrix products, arithmetic and copies ran while one was open for 0% of the time, Pallas kernels for 1%

profile of v4, /device:TPU:0, one launch (start us, length us, event | category | flops | bytes accessed | tf_op | source)
XLA Modules:
  0.0 51.7 jit_solution(16028058627405148321)
XLA Ops:
  0.6 1.1 %pad_maximum_fusion.refs_0_ = f32[64,16,128]{2,1,0:T(8,128)S(1)} fusion(f32[32,16,128]{2,1,0:T(8,128)} %param.3, f32[32,16,128]{2,1,0:T(8,128)} %param.2), kind=kLoop, calls=%fused_computation | loop fusion | flops 131072 | bytes 1048576 | tf_op jit(solution)/shard_map/concatenate | solution.py:754
  1.7 0.5 %collective-permute-start = (f32[64,16,128]{2,1,0:T(8,128)S(1)}, f32[64,16,128]{2,1,0:T(8,128)S(1)}, u32[]{:S(2)}, u32[]{:S(2)}) collective-permute-start(f32[64,16,128]{2,1,0:T(8,128)S(1)} %pad_maximum_fusion.refs_0_), channel_id=1, source_target_pairs={{0,4},{4,0},{1,5},{5,1},{2,6},{6,2},{3,7},{7,3},{8,12},{12,8},{9,1... | collective-permute-start | bytes 1572872 | tf_op jit(solution)/shard_map/ppermute | solution.py:710
  2.3 2.6 %collective-permute-start.1 = (f32[21,16,128]{2,1,0:T(8,128)S(1)}, f32[21,16,128]{2,1,0:T(8,128)S(1)}, u32[]{:S(2)}, u32[]{:S(2)}) collective-permute-start(f32[21,16,128]{2,1,0:T(8,128)S(1)} %get-tuple-element.36), channel_id=1, source_target_pairs={{0,8},{8,0},{16,24},{24,16},{1,9},{9,1},{17,25},{25,17},{2,10},{10... | collective-permute-start | bytes 516104 | tf_op jit(solution)/shard_map/ppermute | solution.py:719
  4.9 0.0 collective-permute-done.refs_1_
  4.9 0.7 %collective-permute-start.2 = (f32[21,16,128]{2,1,0:T(8,128)S(1)}, f32[21,16,128]{2,1,0:T(8,128)S(1)}, u32[]{:S(2)}, u32[]{:S(2)}) collective-permute-start(f32[21,16,128]{2,1,0:T(8,128)S(1)} %get-tuple-element.19), channel_id=1, source_target_pairs={{0,0},{8,16},{16,8},{24,24},{1,1},{9,17},{17,9},{25,25},{2,2},{10,... | collective-permute-start | bytes 516104 | tf_op jit(solution)/shard_map/ppermute | solution.py:719
  5.5 0.3 pack_box.1
  5.9 0.7 %collective-permute-start.5 = (f32[11,32,128]{2,1,0:T(8,128)S(1)}, f32[11,32,128]{2,1,0:T(8,128)S(1)}, u32[]{:S(2)}, u32[]{:S(2)}) collective-permute-start(f32[11,32,128]{2,1,0:T(8,128)S(1)} %pack_box.1), channel_id=1, source_target_pairs={{0,0},{1,4},{2,5},{3,6},{4,1},{5,2},{6,3},{7,7},{8,8},{9,12},{10,1... | collective-permute-start | bytes 540680 | tf_op jit(solution)/shard_map/ppermute | solution.py:727
  6.6 3.3 %collective-permute-done.1.refs_0_.refs_2_ = f32[21,16,128]{2,1,0:T(8,128)S(1)} collective-permute-done((f32[21,16,128]{2,1,0:T(8,128)S(1)}, f32[21,16,128]{2,1,0:T(8,128)S(1)}, u32[]{:S(2)}, u32[]{:S(2)}) %collective-permute-start.1) | collective-permute-done | bytes 172064 | tf_op jit(solution)/shard_map/ppermute | solution.py:719
  9.9 0.0 collective-permute-start.3
  9.9 0.0 collective-permute-done.2.refs_1_.refs_3_
  9.9 0.5 collective-permute-start.4
  10.4 0.9 %collective-permute-done.3.refs_2_.refs_4_ = f32[21,16,128]{2,1,0:T(8,128)S(1)} collective-permute-done((f32[21,16,128]{2,1,0:T(8,128)S(1)}, f32[21,16,128]{2,1,0:T(8,128)S(1)}, u32[]{:S(2)}, u32[]{:S(2)}) %collective-permute-start.3) | collective-permute-done | bytes 172064 | tf_op jit(solution)/shard_map/ppermute | solution.py:710
  11.3 0.0 collective-permute-done.5.refs_4_.refs_6_
  11.3 0.2 collective-permute-done.4.refs_3_.refs_5_
  11.5 0.2 pack_halo.1
  11.8 0.7 %collective-permute-start.6 = (f32[4,32,128]{2,1,0:T(8,128)S(1)}, f32[4,32,128]{2,1,0:T(8,128)S(1)}, u32[]{:S(2)}, u32[]{:S(2)}) collective-permute-start(f32[4,32,128]{2,1,0:T(8,128)S(1)} %pack_halo.1), channel_id=1, source_target_pairs={{0,0},{1,4},{2,5},{3,6},{4,1},{5,2},{6,3},{7,7},{8,8},{9,12},{10,1... | collective-permute-start | bytes 196616 | tf_op jit(solution)/shard_map/ppermute | solution.py:727
  12.5 0.0 collective-permute-done.6.refs_7_
  12.5 5.7 %down.1 = (f32[32,8,128]{2,1,0:T(8,128)}, f32[9,16,128]{2,1,0:T(8,128)S(1)}, f32[9,16,128]{2,1,0:T(8,128)S(1)}, f32[333,32,128]{2,1,0:T(8,128)}) custom-call(f32[64,16,128]{2,1,0:T(8,128)S(1)} %pad_maximum_fusion.refs_0_, f32[64,16,128]{2,1,0:T(8,128)S(1)} %collective-permute-done.refs_1_, f32[21,16,128]{2,1,0:T(8,128)S(1)} %collective-permute-done.1.refs_0_.refs_2_, ...), custom_call_target="tpu_custom_call" | custom-call | flops 4000000 | bytes 8000000 | tf_op jit(solution)/shard_map/down/pallas_call | solution.py:765
  18.1 14.4 %all-to-all-start = ((f32[32,8,128]{2,1,0:T(8,128)}), f32[32,8,128]{2,1,0:T(8,128)S(1)}, u32[]{:S(2)}, u32[]{:S(2)}) async-start(f32[32,8,128]{2,1,0:T(8,128)} %get-tuple-element.21), calls=%async_computation | async-start | bytes 262144 | tf_op jit(solution)/shard_map/all_to_all | solution.py:812
  32.6 1.8 %collective-permute-start.7 = (f32[9,16,128]{2,1,0:T(8,128)S(1)}, f32[9,16,128]{2,1,0:T(8,128)S(1)}, u32[]{:S(2)}, u32[]{:S(2)}) collective-permute-start(f32[9,16,128]{2,1,0:T(8,128)S(1)} %get-tuple-element.22), channel_id=1, source_target_pairs={{0,8},{8,0},{16,24},{24,16},{1,9},{9,1},{17,25},{25,17},{2,10},{10... | collective-permute-start | bytes 221192 | tf_op jit(solution)/shard_map/ppermute | solution.py:719
  34.4 0.7 %collective-permute-start.8 = (f32[9,16,128]{2,1,0:T(8,128)S(1)}, f32[9,16,128]{2,1,0:T(8,128)S(1)}, u32[]{:S(2)}, u32[]{:S(2)}) collective-permute-start(f32[9,16,128]{2,1,0:T(8,128)S(1)} %get-tuple-element.23), channel_id=1, source_target_pairs={{0,0},{8,16},{16,8},{24,24},{1,1},{9,17},{17,9},{25,25},{2,2},{10,... | collective-permute-start | bytes 221192 | tf_op jit(solution)/shard_map/ppermute | solution.py:719
  35.1 2.9 %collective-permute-done.7.refs_2_ = f32[9,16,128]{2,1,0:T(8,128)S(1)} collective-permute-done((f32[9,16,128]{2,1,0:T(8,128)S(1)}, f32[9,16,128]{2,1,0:T(8,128)S(1)}, u32[]{:S(2)}, u32[]{:S(2)}) %collective-permute-start.7) | collective-permute-done | bytes 73760 | tf_op jit(solution)/shard_map/ppermute | solution.py:719
  38.0 0.0 collective-permute-done.8.refs_3_
  38.0 3.0 %all-to-all-done.refs_0_ = f32[32,8,128]{2,1,0:T(8,128)S(1)} async-done(((f32[32,8,128]{2,1,0:T(8,128)}), f32[32,8,128]{2,1,0:T(8,128)S(1)}, u32[]{:S(2)}, u32[]{:S(2)}) %all-to-all-start) | async-done | bytes 131104 | tf_op jit(solution)/shard_map/all_to_all | solution.py:812
  41.0 0.0 collective-permute-start.9
  41.0 1.3 %collective-permute-done.9.refs_1_ = f32[32,8,128]{2,1,0:T(8,128)S(1)} collective-permute-done((f32[32,8,128]{2,1,0:T(8,128)S(1)}, f32[32,8,128]{2,1,0:T(8,128)S(1)}, u32[]{:S(2)}, u32[]{:S(2)}) %collective-permute-start.9) | collective-permute-done | bytes 131104 | tf_op jit(solution)/shard_map/ppermute | solution.py:710
  42.3 6.6 %up.1 = (f32[32,16,128]{2,1,0:T(8,128)S(1)}, f32[32,16,128]{2,1,0:T(8,128)S(1)}, f32[32,16,128]{2,1,0:T(8,128)S(1)}, f32[32,16,128]{2,1,0:T(8,128)S(1)}) custom-call(f32[32,8,128]{2,1,0:T(8,128)S(1)} %all-to-all-done.refs_0_, f32[32,8,128]{2,1,0:T(8,128)S(1)} %collective-permute-done.9.refs_1_, f32[9,16,128]{2,1,0:T(8,128)S(1)} %collective-permute-done.7.refs_2_, ...), custom_call_target="tpu_custom_call" | custom-call | flops 4000000 | bytes 8000000 | tf_op jit(solution)/shard_map/up/pallas_call | solution.py:765
  48.9 0.2 collective-permute-start.10
  49.1 0.4 collective-permute-start.11
  49.5 1.0 %collective-permute-done.10 = f32[32,16,128]{2,1,0:T(8,128)S(1)} collective-permute-done((f32[32,16,128]{2,1,0:T(8,128)S(1)}, f32[32,16,128]{2,1,0:T(8,128)S(1)}, u32[]{:S(2)}, u32[]{:S(2)}) %collective-permute-start.10) | collective-permute-done | bytes 262176 | tf_op jit(solution)/shard_map/ppermute | solution.py:710
  50.5 0.4 collective-permute-done.11
  50.9 0.9 %broadcast_select_fusion = (f32[32,16,128]{2,1,0:T(8,128)}, f32[32,16,128]{2,1,0:T(8,128)}) fusion(f32[32,16,128]{2,1,0:T(8,128)S(1)} %get-tuple-element.30, f32[32,16,128]{2,1,0:T(8,128)S(1)} %collective-permute-done.11, pred[128]{0:T(512)(128)(4,1)S(1)} %fusion.2, f32[32,16,128]{2,1,0:T(8,128)S(1)} %get-tuple-element.28, ...), kind=kLoop, calls=%fused_computation.5 | loop fusion | flops 131072 | bytes 1572992 | tf_op jit(solution)/shard_map/jit(_where)/select_n | solution.py:835
  (4 shorter events, 0.1 us)
Async XLA Ops:
  1.7 3.2 %collective-permute-start = (f32[64,16,128]{2,1,0:T(8,128)S(1)}, f32[64,16,128]{2,1,0:T(8,128)S(1)}, u32[]{:S(2)}, u32[]{:S(2)}) collective-permute-start(f32[64,16,128]{2,1,0:T(8,128)S(1)} %pad_maximum_fusion.refs_0_), channel_id=1, source_target_pairs={{0,4},{4,0},{1,5},{5,1},{2,6},{6,2},{3,7},{7,3},{8,12},{12,8},{9,1... | collective-permute-start | bytes 1572872 | tf_op jit(solution)/shard_map/ppermute | solution.py:710
  2.3 7.6 %collective-permute-start.1 = (f32[21,16,128]{2,1,0:T(8,128)S(1)}, f32[21,16,128]{2,1,0:T(8,128)S(1)}, u32[]{:S(2)}, u32[]{:S(2)}) collective-permute-start(f32[21,16,128]{2,1,0:T(8,128)S(1)} %get-tuple-element.36), channel_id=1, source_target_pairs={{0,8},{8,0},{16,24},{24,16},{1,9},{9,1},{17,25},{25,17},{2,10},{10... | collective-permute-start | bytes 516104 | tf_op jit(solution)/shard_map/ppermute | solution.py:719
  4.9 5.0 %collective-permute-start.2 = (f32[21,16,128]{2,1,0:T(8,128)S(1)}, f32[21,16,128]{2,1,0:T(8,128)S(1)}, u32[]{:S(2)}, u32[]{:S(2)}) collective-permute-start(f32[21,16,128]{2,1,0:T(8,128)S(1)} %get-tuple-element.19), channel_id=1, source_target_pairs={{0,0},{8,16},{16,8},{24,24},{1,1},{9,17},{17,9},{25,25},{2,2},{10,... | collective-permute-start | bytes 516104 | tf_op jit(solution)/shard_map/ppermute | solution.py:719
  5.9 5.4 %collective-permute-start.5 = (f32[11,32,128]{2,1,0:T(8,128)S(1)}, f32[11,32,128]{2,1,0:T(8,128)S(1)}, u32[]{:S(2)}, u32[]{:S(2)}) collective-permute-start(f32[11,32,128]{2,1,0:T(8,128)S(1)} %pack_box.1), channel_id=1, source_target_pairs={{0,0},{1,4},{2,5},{3,6},{4,1},{5,2},{6,3},{7,7},{8,8},{9,12},{10,1... | collective-permute-start | bytes 540680 | tf_op jit(solution)/shard_map/ppermute | solution.py:727
  9.9 1.4 %collective-permute-start.3 = (f32[21,16,128]{2,1,0:T(8,128)S(1)}, f32[21,16,128]{2,1,0:T(8,128)S(1)}, u32[]{:S(2)}, u32[]{:S(2)}) collective-permute-start(f32[21,16,128]{2,1,0:T(8,128)S(1)} %collective-permute-done.1.refs_0_.refs_2_), channel_id=1, source_target_pairs={{0,4},{4,0},{1,5},{5,1},{2,6},{6,2},{3,7},{7,3},{8,12},{12,8},{9,1... | collective-permute-start | bytes 516104 | tf_op jit(solution)/shard_map/ppermute | solution.py:710
  9.9 1.6 %collective-permute-start.4 = (f32[21,16,128]{2,1,0:T(8,128)S(1)}, f32[21,16,128]{2,1,0:T(8,128)S(1)}, u32[]{:S(2)}, u32[]{:S(2)}) collective-permute-start(f32[21,16,128]{2,1,0:T(8,128)S(1)} %collective-permute-done.2.refs_1_.refs_3_), channel_id=1, source_target_pairs={{0,4},{4,0},{1,5},{5,1},{2,6},{6,2},{3,7},{7,3},{8,12},{12,8},{9,1... | collective-permute-start | bytes 516104 | tf_op jit(solution)/shard_map/ppermute | solution.py:710
  11.8 0.7 %collective-permute-start.6 = (f32[4,32,128]{2,1,0:T(8,128)S(1)}, f32[4,32,128]{2,1,0:T(8,128)S(1)}, u32[]{:S(2)}, u32[]{:S(2)}) collective-permute-start(f32[4,32,128]{2,1,0:T(8,128)S(1)} %pack_halo.1), channel_id=1, source_target_pairs={{0,0},{1,4},{2,5},{3,6},{4,1},{5,2},{6,3},{7,7},{8,8},{9,12},{10,1... | collective-permute-start | bytes 196616 | tf_op jit(solution)/shard_map/ppermute | solution.py:727
  18.1 22.9 %all-to-all-start = ((f32[32,8,128]{2,1,0:T(8,128)}), f32[32,8,128]{2,1,0:T(8,128)S(1)}, u32[]{:S(2)}, u32[]{:S(2)}) async-start(f32[32,8,128]{2,1,0:T(8,128)} %get-tuple-element.21), calls=%async_computation | async-start | bytes 262144 | tf_op jit(solution)/shard_map/all_to_all | solution.py:812
  32.6 5.4 %collective-permute-start.7 = (f32[9,16,128]{2,1,0:T(8,128)S(1)}, f32[9,16,128]{2,1,0:T(8,128)S(1)}, u32[]{:S(2)}, u32[]{:S(2)}) collective-permute-start(f32[9,16,128]{2,1,0:T(8,128)S(1)} %get-tuple-element.22), channel_id=1, source_target_pairs={{0,8},{8,0},{16,24},{24,16},{1,9},{9,1},{17,25},{25,17},{2,10},{10... | collective-permute-start | bytes 221192 | tf_op jit(solution)/shard_map/ppermute | solution.py:719
  34.4 3.5 %collective-permute-start.8 = (f32[9,16,128]{2,1,0:T(8,128)S(1)}, f32[9,16,128]{2,1,0:T(8,128)S(1)}, u32[]{:S(2)}, u32[]{:S(2)}) collective-permute-start(f32[9,16,128]{2,1,0:T(8,128)S(1)} %get-tuple-element.23), channel_id=1, source_target_pairs={{0,0},{8,16},{16,8},{24,24},{1,1},{9,17},{17,9},{25,25},{2,2},{10,... | collective-permute-start | bytes 221192 | tf_op jit(solution)/shard_map/ppermute | solution.py:719
  41.0 1.3 %collective-permute-start.9 = (f32[32,8,128]{2,1,0:T(8,128)S(1)}, f32[32,8,128]{2,1,0:T(8,128)S(1)}, u32[]{:S(2)}, u32[]{:S(2)}) collective-permute-start(f32[32,8,128]{2,1,0:T(8,128)S(1)} %all-to-all-done.refs_0_), channel_id=1, source_target_pairs={{0,4},{4,0},{1,5},{5,1},{2,6},{6,2},{3,7},{7,3},{8,12},{12,8},{9,1... | collective-permute-start | bytes 393224 | tf_op jit(solution)/shard_map/ppermute | solution.py:710
  48.9 1.6 %collective-permute-start.10 = (f32[32,16,128]{2,1,0:T(8,128)S(1)}, f32[32,16,128]{2,1,0:T(8,128)S(1)}, u32[]{:S(2)}, u32[]{:S(2)}) collective-permute-start(f32[32,16,128]{2,1,0:T(8,128)S(1)} %get-tuple-element.29), channel_id=1, source_target_pairs={{0,4},{4,0},{1,5},{5,1},{2,6},{6,2},{3,7},{7,3},{8,12},{12,8},{9,1... | collective-permute-start | bytes 786440 | tf_op jit(solution)/shard_map/ppermute | solution.py:710
  49.1 1.8 %collective-permute-start.11 = (f32[32,16,128]{2,1,0:T(8,128)S(1)}, f32[32,16,128]{2,1,0:T(8,128)S(1)}, u32[]{:S(2)}, u32[]{:S(2)}) collective-permute-start(f32[32,16,128]{2,1,0:T(8,128)S(1)} %get-tuple-element.31), channel_id=1, source_target_pairs={{0,4},{4,0},{1,5},{5,1},{2,6},{6,2},{3,7},{7,3},{8,12},{12,8},{9,1... | collective-permute-start | bytes 786440 | tf_op jit(solution)/shard_map/ppermute | solution.py:710

commit v5 on v4

--- a/solution.py
+++ b/solution.py
@@ -331,8 +331,9 @@
     def restrict(source, target, tmp, x_count, at, y_first, y_rows, shift):
         for i in range(x_count):
             j = i % tmp.shape[0]
-            tmp[j] = source[at + 2 * i] + source[at + 2 * i + 1]
-            v = tmp[j, pl.ds(y_first, y_rows // 2, stride=2)] + tmp[j, pl.ds(y_first + 1, y_rows // 2, stride=2)]
+            v = source[at + 2 * i] + source[at + 2 * i + 1]
+            tmp[j] = v + pltpu.roll(v, v.shape[0] - 1, 0)
+            v = tmp[j, pl.ds(y_first, y_rows // 2, stride=2)]
             target(i, 0.125 * pair_z(v, shift, LANES))
 
     x1, y1 = xw // 2, yw // 2
@@ -458,7 +459,7 @@
     k4, cx4, cy4, cz4, iv4, g04, g4, da4, db4, e4 = take(10)
     cx1, cy1, cz1, iv1, g01, w1, u1, g1, da1, db1, e1 = take(11)
     cx0, cy0, cz0, iv0, g00, w0, u0, g0, da0, db0 = take(10)
-    e2_wide, = take(1)
+    e2_wide, spread1, spread0 = take(3)
     gathered = take(count)
     from_even, from_odd, sems = take(3)
     core = core_of()
@@ -636,12 +637,12 @@
     for plane in range(wide1):
         j = plane // 2
         v = 0.75 * window[j + 1] + 0.25 * window[j + 2 if plane % 2 else j]
-        place_rows(u1, 1 + plane, spread_z(v, 2, LANES, False), y2w)
+        place_rows(spread1, 1 + plane, spread_z(v, 2, LANES, False), y2w)
     grid1 = Grid(wide1, yw // 2, LANES, 1, 2, False, geo["chunk1"])
 
     def start1(at):
         here = pl.ds(at, grid1.size)
-        u1[here] = jnp.where(iv1[here] > 0.0, w1[here] + u1[here], 0.0)
+        u1[here] = jnp.where(iv1[here] > 0.0, w1[here] + spread1[here, pl.ds(0, yw // 2)], 0.0)
 
     chunks(wide1, start1, grid1.size)
     post(grid1, (cx1, cy1, cz1, iv1), g01, u1, g1, da1, db1, e1, 1)
@@ -654,14 +655,14 @@
         at = WIN1 + 1 - WIN0 // 2 + i
         middle = 0.75 * e1[at]
         for j, side in ((0, e1[at - 1]), (1, e1[at + 1])):
-            place_rows(u0, 1 + 2 * i + j, spread_z(middle + 0.25 * side, 1, LANES, False), yw // 2)
+            place_rows(spread0, 1 + 2 * i + j, spread_z(middle + 0.25 * side, 1, LANES, False), yw // 2)
         return carry
 
     lax.fori_loop(0, wide0 // 2, fill, 0, unroll=10)
 
     def start0(at):
         here = pl.ds(at, grid0.size)
-        u0[here] = jnp.where(iv0[here] > 0.0, w0[here] + u0[here], 0.0)
+        u0[here] = jnp.where(iv0[here] > 0.0, w0[here] + spread0[here, pl.ds(0, yw)], 0.0)
 
     chunks(wide0, start0, grid0.size)
     coeffs0 = (cx0, cy0, cz0, iv0)
@@ -827,7 +828,7 @@
         "up", functools.partial(up_kernel, geo), (*gathered, from_even, from_odd, passed), [array(bx, by, LANES)] * 4,
         [level(x2, y2, z2)] * 12 + [level(x2 // 2, y2, z2)] * 12 + [level(x2 // 4, y2, z2)] * 10
         + [level(wide1, y1, LANES)] * 11 + [level(wide0, yw, LANES)] * 10
-        + [vmem((x2 + 8, y2 + 2 * geo["pad_y"], z2)), *(vmem(v.shape) for v in gathered), vmem(from_even.shape), vmem(from_odd.shape)]
+        + [vmem((x2 + 8, y2 + 2 * geo["pad_y"], z2)), level(wide1, y1 + 8, LANES), level(wide0, yw + 8, LANES), *(vmem(v.shape) for v in gathered), vmem(from_even.shape), vmem(from_odd.shape)]
         + [pltpu.SemaphoreType.DMA((20,))],
         hbm_ins=1, limit=VMEM_LIMIT, operand=anywhere, result=anywhere,
     )

time: 52 us -> 52 us (level)
  no operation moved by 1% of the time
where the time goes in v5:
time: 52 us; the launch traced here: 51.7 us
  starting transfers between devices  23.1 us (44%)
  waiting for transfers between devices  13.1 us (25%)
  Pallas kernels  12.8 us (25%)
  other arithmetic  1.95 us (4%)
  between operations  0.73 us (1%)
    all_to_all x1, starting transfers between devices, on_device(): half = lax.all_to_all(packed, AXES, 0, 0, tiled=True)  14.4 us
    pallas_call x4, Pallas kernels, call(): pl.pallas_call(kernel, out_shape=outs, in_specs=[operand] * (len(ins) - h...  12.8 us
    ppermute x4, waiting for transfers between devices, paired(): return lax.ppermute(v, 'gx', perm)  6.18 us
    ppermute x4, starting transfers between devices, paired(): return lax.ppermute(v, 'gx', perm)  5.73 us
    ppermute x6, waiting for transfers between devices, sibling(): return lax.ppermute(v, 'gy', [(i, i ^ 1) for i in range(ny)])  3.87 us
    all_to_all x1, waiting for transfers between devices, on_device(): half = lax.all_to_all(packed, AXES, 0, 0, tiled=True)  3.04 us
    ppermute x6, starting transfers between devices, sibling(): return lax.ppermute(v, 'gy', [(i, i ^ 1) for i in range(ny)])  1.61 us
    ppermute x2, starting transfers between devices, facing(): lax.ppermute(v, AXES, [(i, perm.get(i, i)) for i in range(nx * ny * nz)])  1.34 us
  transfers between devices with their start and end apart: 13, of which 8 were waited for; matrix products, arithmetic and copies ran while one was open for 0% of the time, Pallas kernels for 1%

profile of v5, /device:TPU:0, one launch (start us, length us, event | category | flops | bytes accessed | tf_op | source)
XLA Modules:
  0.0 51.7 jit_solution(4928306061982588696)
XLA Ops:
  0.6 1.1 %pad_maximum_fusion.refs_0_ = f32[64,16,128]{2,1,0:T(8,128)S(1)} fusion(f32[32,16,128]{2,1,0:T(8,128)} %param.3, f32[32,16,128]{2,1,0:T(8,128)} %param.2), kind=kLoop, calls=%fused_computation | loop fusion | flops 131072 | bytes 1048576 | tf_op jit(solution)/shard_map/concatenate | solution.py:755
  1.7 0.5 %collective-permute-start = (f32[64,16,128]{2,1,0:T(8,128)S(1)}, f32[64,16,128]{2,1,0:T(8,128)S(1)}, u32[]{:S(2)}, u32[]{:S(2)}) collective-permute-start(f32[64,16,128]{2,1,0:T(8,128)S(1)} %pad_maximum_fusion.refs_0_), channel_id=1, source_target_pairs={{0,4},{4,0},{1,5},{5,1},{2,6},{6,2},{3,7},{7,3},{8,12},{12,8},{9,1... | collective-permute-start | bytes 1572872 | tf_op jit(solution)/shard_map/ppermute | solution.py:711
  2.3 2.6 %collective-permute-start.1 = (f32[21,16,128]{2,1,0:T(8,128)S(1)}, f32[21,16,128]{2,1,0:T(8,128)S(1)}, u32[]{:S(2)}, u32[]{:S(2)}) collective-permute-start(f32[21,16,128]{2,1,0:T(8,128)S(1)} %get-tuple-element.36), channel_id=1, source_target_pairs={{0,8},{8,0},{16,24},{24,16},{1,9},{9,1},{17,25},{25,17},{2,10},{10... | collective-permute-start | bytes 516104 | tf_op jit(solution)/shard_map/ppermute | solution.py:720
  4.9 0.0 collective-permute-done.refs_1_
  4.9 0.7 %collective-permute-start.2 = (f32[21,16,128]{2,1,0:T(8,128)S(1)}, f32[21,16,128]{2,1,0:T(8,128)S(1)}, u32[]{:S(2)}, u32[]{:S(2)}) collective-permute-start(f32[21,16,128]{2,1,0:T(8,128)S(1)} %get-tuple-element.19), channel_id=1, source_target_pairs={{0,0},{8,16},{16,8},{24,24},{1,1},{9,17},{17,9},{25,25},{2,2},{10,... | collective-permute-start | bytes 516104 | tf_op jit(solution)/shard_map/ppermute | solution.py:720
  5.5 0.3 pack_box.1
  5.9 0.7 %collective-permute-start.5 = (f32[11,32,128]{2,1,0:T(8,128)S(1)}, f32[11,32,128]{2,1,0:T(8,128)S(1)}, u32[]{:S(2)}, u32[]{:S(2)}) collective-permute-start(f32[11,32,128]{2,1,0:T(8,128)S(1)} %pack_box.1), channel_id=1, source_target_pairs={{0,0},{1,4},{2,5},{3,6},{4,1},{5,2},{6,3},{7,7},{8,8},{9,12},{10,1... | collective-permute-start | bytes 540680 | tf_op jit(solution)/shard_map/ppermute | solution.py:728
  6.6 3.3 %collective-permute-done.1.refs_0_.refs_2_ = f32[21,16,128]{2,1,0:T(8,128)S(1)} collective-permute-done((f32[21,16,128]{2,1,0:T(8,128)S(1)}, f32[21,16,128]{2,1,0:T(8,128)S(1)}, u32[]{:S(2)}, u32[]{:S(2)}) %collective-permute-start.1) | collective-permute-done | bytes 172064 | tf_op jit(solution)/shard_map/ppermute | solution.py:720
  9.9 0.0 collective-permute-start.3
  9.9 0.0 collective-permute-done.2.refs_1_.refs_3_
  9.9 0.5 collective-permute-start.4
  10.4 0.9 %collective-permute-done.3.refs_2_.refs_4_ = f32[21,16,128]{2,1,0:T(8,128)S(1)} collective-permute-done((f32[21,16,128]{2,1,0:T(8,128)S(1)}, f32[21,16,128]{2,1,0:T(8,128)S(1)}, u32[]{:S(2)}, u32[]{:S(2)}) %collective-permute-start.3) | collective-permute-done | bytes 172064 | tf_op jit(solution)/shard_map/ppermute | solution.py:711
  11.3 0.0 collective-permute-done.5.refs_4_.refs_6_
  11.3 0.2 collective-permute-done.4.refs_3_.refs_5_
  11.5 0.2 pack_halo.1
  11.8 0.7 %collective-permute-start.6 = (f32[4,32,128]{2,1,0:T(8,128)S(1)}, f32[4,32,128]{2,1,0:T(8,128)S(1)}, u32[]{:S(2)}, u32[]{:S(2)}) collective-permute-start(f32[4,32,128]{2,1,0:T(8,128)S(1)} %pack_halo.1), channel_id=1, source_target_pairs={{0,0},{1,4},{2,5},{3,6},{4,1},{5,2},{6,3},{7,7},{8,8},{9,12},{10,1... | collective-permute-start | bytes 196616 | tf_op jit(solution)/shard_map/ppermute | solution.py:728
  12.5 0.0 collective-permute-done.6.refs_7_
  12.5 5.7 %down.1 = (f32[32,8,128]{2,1,0:T(8,128)}, f32[9,16,128]{2,1,0:T(8,128)S(1)}, f32[9,16,128]{2,1,0:T(8,128)S(1)}, f32[333,32,128]{2,1,0:T(8,128)}) custom-call(f32[64,16,128]{2,1,0:T(8,128)S(1)} %pad_maximum_fusion.refs_0_, f32[64,16,128]{2,1,0:T(8,128)S(1)} %collective-permute-done.refs_1_, f32[21,16,128]{2,1,0:T(8,128)S(1)} %collective-permute-done.1.refs_0_.refs_2_, ...), custom_call_target="tpu_custom_call" | custom-call | flops 4000000 | bytes 8000000 | tf_op jit(solution)/shard_map/down/pallas_call | solution.py:766
  18.1 14.4 %all-to-all-start = ((f32[32,8,128]{2,1,0:T(8,128)}), f32[32,8,128]{2,1,0:T(8,128)S(1)}, u32[]{:S(2)}, u32[]{:S(2)}) async-start(f32[32,8,128]{2,1,0:T(8,128)} %get-tuple-element.21), calls=%async_computation | async-start | bytes 262144 | tf_op jit(solution)/shard_map/all_to_all | solution.py:813
  32.6 1.8 %collective-permute-start.7 = (f32[9,16,128]{2,1,0:T(8,128)S(1)}, f32[9,16,128]{2,1,0:T(8,128)S(1)}, u32[]{:S(2)}, u32[]{:S(2)}) collective-permute-start(f32[9,16,128]{2,1,0:T(8,128)S(1)} %get-tuple-element.22), channel_id=1, source_target_pairs={{0,8},{8,0},{16,24},{24,16},{1,9},{9,1},{17,25},{25,17},{2,10},{10... | collective-permute-start | bytes 221192 | tf_op jit(solution)/shard_map/ppermute | solution.py:720
  34.4 0.7 %collective-permute-start.8 = (f32[9,16,128]{2,1,0:T(8,128)S(1)}, f32[9,16,128]{2,1,0:T(8,128)S(1)}, u32[]{:S(2)}, u32[]{:S(2)}) collective-permute-start(f32[9,16,128]{2,1,0:T(8,128)S(1)} %get-tuple-element.23), channel_id=1, source_target_pairs={{0,0},{8,16},{16,8},{24,24},{1,1},{9,17},{17,9},{25,25},{2,2},{10,... | collective-permute-start | bytes 221192 | tf_op jit(solution)/shard_map/ppermute | solution.py:720
  35.1 2.9 %collective-permute-done.7.refs_2_ = f32[9,16,128]{2,1,0:T(8,128)S(1)} collective-permute-done((f32[9,16,128]{2,1,0:T(8,128)S(1)}, f32[9,16,128]{2,1,0:T(8,128)S(1)}, u32[]{:S(2)}, u32[]{:S(2)}) %collective-permute-start.7) | collective-permute-done | bytes 73760 | tf_op jit(solution)/shard_map/ppermute | solution.py:720
  37.9 0.0 collective-permute-done.8.refs_3_
  37.9 3.0 %all-to-all-done.refs_0_ = f32[32,8,128]{2,1,0:T(8,128)S(1)} async-done(((f32[32,8,128]{2,1,0:T(8,128)}), f32[32,8,128]{2,1,0:T(8,128)S(1)}, u32[]{:S(2)}, u32[]{:S(2)}) %all-to-all-start) | async-done | bytes 131104 | tf_op jit(solution)/shard_map/all_to_all | solution.py:813
  41.0 0.0 collective-permute-start.9
  41.0 1.3 %collective-permute-done.9.refs_1_ = f32[32,8,128]{2,1,0:T(8,128)S(1)} collective-permute-done((f32[32,8,128]{2,1,0:T(8,128)S(1)}, f32[32,8,128]{2,1,0:T(8,128)S(1)}, u32[]{:S(2)}, u32[]{:S(2)}) %collective-permute-start.9) | collective-permute-done | bytes 131104 | tf_op jit(solution)/shard_map/ppermute | solution.py:711
  42.3 6.6 %up.1 = (f32[32,16,128]{2,1,0:T(8,128)S(1)}, f32[32,16,128]{2,1,0:T(8,128)S(1)}, f32[32,16,128]{2,1,0:T(8,128)S(1)}, f32[32,16,128]{2,1,0:T(8,128)S(1)}) custom-call(f32[32,8,128]{2,1,0:T(8,128)S(1)} %all-to-all-done.refs_0_, f32[32,8,128]{2,1,0:T(8,128)S(1)} %collective-permute-done.9.refs_1_, f32[9,16,128]{2,1,0:T(8,128)S(1)} %collective-permute-done.7.refs_2_, ...), custom_call_target="tpu_custom_call" | custom-call | flops 4000000 | bytes 8000000 | tf_op jit(solution)/shard_map/up/pallas_call | solution.py:766
  48.9 0.2 collective-permute-start.10
  49.1 0.4 collective-permute-start.11
  49.5 1.0 %collective-permute-done.10 = f32[32,16,128]{2,1,0:T(8,128)S(1)} collective-permute-done((f32[32,16,128]{2,1,0:T(8,128)S(1)}, f32[32,16,128]{2,1,0:T(8,128)S(1)}, u32[]{:S(2)}, u32[]{:S(2)}) %collective-permute-start.10) | collective-permute-done | bytes 262176 | tf_op jit(solution)/shard_map/ppermute | solution.py:711
  50.5 0.4 collective-permute-done.11
  50.9 0.9 %broadcast_select_fusion = (f32[32,16,128]{2,1,0:T(8,128)}, f32[32,16,128]{2,1,0:T(8,128)}) fusion(f32[32,16,128]{2,1,0:T(8,128)S(1)} %get-tuple-element.30, f32[32,16,128]{2,1,0:T(8,128)S(1)} %collective-permute-done.11, pred[128]{0:T(512)(128)(4,1)S(1)} %fusion.2, f32[32,16,128]{2,1,0:T(8,128)S(1)} %get-tuple-element.28, ...), kind=kLoop, calls=%fused_computation.5 | loop fusion | flops 131072 | bytes 1572992 | tf_op jit(solution)/shard_map/jit(_where)/select_n | solution.py:836
  (4 shorter events, 0.1 us)
Async XLA Ops:
  1.7 3.2 %collective-permute-start = (f32[64,16,128]{2,1,0:T(8,128)S(1)}, f32[64,16,128]{2,1,0:T(8,128)S(1)}, u32[]{:S(2)}, u32[]{:S(2)}) collective-permute-start(f32[64,16,128]{2,1,0:T(8,128)S(1)} %pad_maximum_fusion.refs_0_), channel_id=1, source_target_pairs={{0,4},{4,0},{1,5},{5,1},{2,6},{6,2},{3,7},{7,3},{8,12},{12,8},{9,1... | collective-permute-start | bytes 1572872 | tf_op jit(solution)/shard_map/ppermute | solution.py:711
  2.3 7.6 %collective-permute-start.1 = (f32[21,16,128]{2,1,0:T(8,128)S(1)}, f32[21,16,128]{2,1,0:T(8,128)S(1)}, u32[]{:S(2)}, u32[]{:S(2)}) collective-permute-start(f32[21,16,128]{2,1,0:T(8,128)S(1)} %get-tuple-element.36), channel_id=1, source_target_pairs={{0,8},{8,0},{16,24},{24,16},{1,9},{9,1},{17,25},{25,17},{2,10},{10... | collective-permute-start | bytes 516104 | tf_op jit(solution)/shard_map/ppermute | solution.py:720
  4.9 5.0 %collective-permute-start.2 = (f32[21,16,128]{2,1,0:T(8,128)S(1)}, f32[21,16,128]{2,1,0:T(8,128)S(1)}, u32[]{:S(2)}, u32[]{:S(2)}) collective-permute-start(f32[21,16,128]{2,1,0:T(8,128)S(1)} %get-tuple-element.19), channel_id=1, source_target_pairs={{0,0},{8,16},{16,8},{24,24},{1,1},{9,17},{17,9},{25,25},{2,2},{10,... | collective-permute-start | bytes 516104 | tf_op jit(solution)/shard_map/ppermute | solution.py:720
  5.9 5.4 %collective-permute-start.5 = (f32[11,32,128]{2,1,0:T(8,128)S(1)}, f32[11,32,128]{2,1,0:T(8,128)S(1)}, u32[]{:S(2)}, u32[]{:S(2)}) collective-permute-start(f32[11,32,128]{2,1,0:T(8,128)S(1)} %pack_box.1), channel_id=1, source_target_pairs={{0,0},{1,4},{2,5},{3,6},{4,1},{5,2},{6,3},{7,7},{8,8},{9,12},{10,1... | collective-permute-start | bytes 540680 | tf_op jit(solution)/shard_map/ppermute | solution.py:728
  9.9 1.4 %collective-permute-start.3 = (f32[21,16,128]{2,1,0:T(8,128)S(1)}, f32[21,16,128]{2,1,0:T(8,128)S(1)}, u32[]{:S(2)}, u32[]{:S(2)}) collective-permute-start(f32[21,16,128]{2,1,0:T(8,128)S(1)} %collective-permute-done.1.refs_0_.refs_2_), channel_id=1, source_target_pairs={{0,4},{4,0},{1,5},{5,1},{2,6},{6,2},{3,7},{7,3},{8,12},{12,8},{9,1... | collective-permute-start | bytes 516104 | tf_op jit(solution)/shard_map/ppermute | solution.py:711
  9.9 1.6 %collective-permute-start.4 = (f32[21,16,128]{2,1,0:T(8,128)S(1)}, f32[21,16,128]{2,1,0:T(8,128)S(1)}, u32[]{:S(2)}, u32[]{:S(2)}) collective-permute-start(f32[21,16,128]{2,1,0:T(8,128)S(1)} %collective-permute-done.2.refs_1_.refs_3_), channel_id=1, source_target_pairs={{0,4},{4,0},{1,5},{5,1},{2,6},{6,2},{3,7},{7,3},{8,12},{12,8},{9,1... | collective-permute-start | bytes 516104 | tf_op jit(solution)/shard_map/ppermute | solution.py:711
  11.8 0.7 %collective-permute-start.6 = (f32[4,32,128]{2,1,0:T(8,128)S(1)}, f32[4,32,128]{2,1,0:T(8,128)S(1)}, u32[]{:S(2)}, u32[]{:S(2)}) collective-permute-start(f32[4,32,128]{2,1,0:T(8,128)S(1)} %pack_halo.1), channel_id=1, source_target_pairs={{0,0},{1,4},{2,5},{3,6},{4,1},{5,2},{6,3},{7,7},{8,8},{9,12},{10,1... | collective-permute-start | bytes 196616 | tf_op jit(solution)/shard_map/ppermute | solution.py:728
  18.1 22.9 %all-to-all-start = ((f32[32,8,128]{2,1,0:T(8,128)}), f32[32,8,128]{2,1,0:T(8,128)S(1)}, u32[]{:S(2)}, u32[]{:S(2)}) async-start(f32[32,8,128]{2,1,0:T(8,128)} %get-tuple-element.21), calls=%async_computation | async-start | bytes 262144 | tf_op jit(solution)/shard_map/all_to_all | solution.py:813
  32.6 5.4 %collective-permute-start.7 = (f32[9,16,128]{2,1,0:T(8,128)S(1)}, f32[9,16,128]{2,1,0:T(8,128)S(1)}, u32[]{:S(2)}, u32[]{:S(2)}) collective-permute-start(f32[9,16,128]{2,1,0:T(8,128)S(1)} %get-tuple-element.22), channel_id=1, source_target_pairs={{0,8},{8,0},{16,24},{24,16},{1,9},{9,1},{17,25},{25,17},{2,10},{10... | collective-permute-start | bytes 221192 | tf_op jit(solution)/shard_map/ppermute | solution.py:720
  34.4 3.5 %collective-permute-start.8 = (f32[9,16,128]{2,1,0:T(8,128)S(1)}, f32[9,16,128]{2,1,0:T(8,128)S(1)}, u32[]{:S(2)}, u32[]{:S(2)}) collective-permute-start(f32[9,16,128]{2,1,0:T(8,128)S(1)} %get-tuple-element.23), channel_id=1, source_target_pairs={{0,0},{8,16},{16,8},{24,24},{1,1},{9,17},{17,9},{25,25},{2,2},{10,... | collective-permute-start | bytes 221192 | tf_op jit(solution)/shard_map/ppermute | solution.py:720
  41.0 1.3 %collective-permute-start.9 = (f32[32,8,128]{2,1,0:T(8,128)S(1)}, f32[32,8,128]{2,1,0:T(8,128)S(1)}, u32[]{:S(2)}, u32[]{:S(2)}) collective-permute-start(f32[32,8,128]{2,1,0:T(8,128)S(1)} %all-to-all-done.refs_0_), channel_id=1, source_target_pairs={{0,4},{4,0},{1,5},{5,1},{2,6},{6,2},{3,7},{7,3},{8,12},{12,8},{9,1... | collective-permute-start | bytes 393224 | tf_op jit(solution)/shard_map/ppermute | solution.py:711
  48.9 1.6 %collective-permute-start.10 = (f32[32,16,128]{2,1,0:T(8,128)S(1)}, f32[32,16,128]{2,1,0:T(8,128)S(1)}, u32[]{:S(2)}, u32[]{:S(2)}) collective-permute-start(f32[32,16,128]{2,1,0:T(8,128)S(1)} %get-tuple-element.29), channel_id=1, source_target_pairs={{0,4},{4,0},{1,5},{5,1},{2,6},{6,2},{3,7},{7,3},{8,12},{12,8},{9,1... | collective-permute-start | bytes 786440 | tf_op jit(solution)/shard_map/ppermute | solution.py:711
  49.1 1.8 %collective-permute-start.11 = (f32[32,16,128]{2,1,0:T(8,128)S(1)}, f32[32,16,128]{2,1,0:T(8,128)S(1)}, u32[]{:S(2)}, u32[]{:S(2)}) collective-permute-start(f32[32,16,128]{2,1,0:T(8,128)S(1)} %get-tuple-element.31), channel_id=1, source_target_pairs={{0,4},{4,0},{1,5},{5,1},{2,6},{6,2},{3,7},{7,3},{8,12},{12,8},{9,1... | collective-permute-start | bytes 786440 | tf_op jit(solution)/shard_map/ppermute | solution.py:711

commit v6 on v5

--- a/solution.py
+++ b/solution.py
@@ -63,6 +63,10 @@
     def __init__(self, x, y, z, sy, sz, whole_z, size):
         self.x, self.y, self.z, self.sy, self.sz = x, y, z, sy, sz
         self.whole_z, self.size = whole_z, size
+
+    def part(self, less):
+        x = self.x - 2 * less
+        return Grid(x, self.y, self.z, self.sy, self.sz, self.whole_z, x if self.size == self.x else 2)
 
     def up_y(self, v):
         return pltpu.roll(v, self.y - self.sy, v.ndim - 2)
@@ -358,13 +362,13 @@
         k0[here] = d1[here] + v + direction
         d1[here] = direction
 
-    inner.step(coeffs, d2, g, *FACTORS[2], third, 5)
+    inner.part(1).step(coeffs, d2, g, *FACTORS[2], third, 6)
     send(k0, own0, wide0)
 
     def residual(here, v, value, direction):
         g[here] = value * ds[here]
 
-    inner.step(coeffs, d1, g, 0.0, None, residual, 5)
+    inner.part(2).step(coeffs, d1, g, 0.0, None, residual, 7)
 
     restrict(g, put_b1, half_y, x1, 1, 0, yw, 1)
     grid1 = Grid(x1, y1, LANES, 1, 2, False, geo["chunk1"])
@@ -658,7 +662,7 @@
             place_rows(spread0, 1 + 2 * i + j, spread_z(middle + 0.25 * side, 1, LANES, False), yw // 2)
         return carry
 
-    lax.fori_loop(0, wide0 // 2, fill, 0, unroll=10)
+    lax.fori_loop(0, wide0 // 2, fill, 0, unroll=True)
 
     def start0(at):
         here = pl.ds(at, grid0.size)

time: 52 us -> 51.7 us (level)
  no operation moved by 1% of the time
where the time goes in v6:
time: 51.7 us; the launch traced here: 51.5 us
  starting transfers between devices  23.1 us (45%)
  waiting for transfers between devices  13.1 us (25%)
  Pallas kernels  12.5 us (24%)
  other arithmetic  1.95 us (4%)
  between operations  0.73 us (1%)
    all_to_all x1, starting transfers between devices, on_device(): half = lax.all_to_all(packed, AXES, 0, 0, tiled=True)  14.4 us
    pallas_call x4, Pallas kernels, call(): pl.pallas_call(kernel, out_shape=outs, in_specs=[operand] * (len(ins) - h...  12.5 us
    ppermute x4, waiting for transfers between devices, paired(): return lax.ppermute(v, 'gx', perm)  6.18 us
    ppermute x4, starting transfers between devices, paired(): return lax.ppermute(v, 'gx', perm)  5.73 us
    ppermute x6, waiting for transfers between devices, sibling(): return lax.ppermute(v, 'gy', [(i, i ^ 1) for i in range(ny)])  3.87 us
    all_to_all x1, waiting for transfers between devices, on_device(): half = lax.all_to_all(packed, AXES, 0, 0, tiled=True)  3.04 us
    ppermute x6, starting transfers between devices, sibling(): return lax.ppermute(v, 'gy', [(i, i ^ 1) for i in range(ny)])  1.61 us
    ppermute x2, starting transfers between devices, facing(): lax.ppermute(v, AXES, [(i, perm.get(i, i)) for i in range(nx * ny * nz)])  1.34 us
  transfers between devices with their start and end apart: 13, of which 8 were waited for; matrix products, arithmetic and copies ran while one was open for 0% of the time, Pallas kernels for 1%

profile of v6, /device:TPU:0, one launch (start us, length us, event | category | flops | bytes accessed | tf_op | source)
XLA Modules:
  0.0 51.5 jit_solution(16695737333776271189)
XLA Ops:
  0.6 1.1 %pad_maximum_fusion.refs_0_ = f32[64,16,128]{2,1,0:T(8,128)S(1)} fusion(f32[32,16,128]{2,1,0:T(8,128)} %param.3, f32[32,16,128]{2,1,0:T(8,128)} %param.2), kind=kLoop, calls=%fused_computation | loop fusion | flops 131072 | bytes 1048576 | tf_op jit(solution)/shard_map/concatenate | solution.py:759
  1.7 0.5 %collective-permute-start = (f32[64,16,128]{2,1,0:T(8,128)S(1)}, f32[64,16,128]{2,1,0:T(8,128)S(1)}, u32[]{:S(2)}, u32[]{:S(2)}) collective-permute-start(f32[64,16,128]{2,1,0:T(8,128)S(1)} %pad_maximum_fusion.refs_0_), channel_id=1, source_target_pairs={{0,4},{4,0},{1,5},{5,1},{2,6},{6,2},{3,7},{7,3},{8,12},{12,8},{9,1... | collective-permute-start | bytes 1572872 | tf_op jit(solution)/shard_map/ppermute | solution.py:715
  2.3 2.6 %collective-permute-start.1 = (f32[21,16,128]{2,1,0:T(8,128)S(1)}, f32[21,16,128]{2,1,0:T(8,128)S(1)}, u32[]{:S(2)}, u32[]{:S(2)}) collective-permute-start(f32[21,16,128]{2,1,0:T(8,128)S(1)} %get-tuple-element.36), channel_id=1, source_target_pairs={{0,8},{8,0},{16,24},{24,16},{1,9},{9,1},{17,25},{25,17},{2,10},{10... | collective-permute-start | bytes 516104 | tf_op jit(solution)/shard_map/ppermute | solution.py:724
  4.9 0.0 collective-permute-done.refs_1_
  4.9 0.7 %collective-permute-start.2 = (f32[21,16,128]{2,1,0:T(8,128)S(1)}, f32[21,16,128]{2,1,0:T(8,128)S(1)}, u32[]{:S(2)}, u32[]{:S(2)}) collective-permute-start(f32[21,16,128]{2,1,0:T(8,128)S(1)} %get-tuple-element.19), channel_id=1, source_target_pairs={{0,0},{8,16},{16,8},{24,24},{1,1},{9,17},{17,9},{25,25},{2,2},{10,... | collective-permute-start | bytes 516104 | tf_op jit(solution)/shard_map/ppermute | solution.py:724
  5.5 0.3 pack_box.1
  5.9 0.7 %collective-permute-start.5 = (f32[11,32,128]{2,1,0:T(8,128)S(1)}, f32[11,32,128]{2,1,0:T(8,128)S(1)}, u32[]{:S(2)}, u32[]{:S(2)}) collective-permute-start(f32[11,32,128]{2,1,0:T(8,128)S(1)} %pack_box.1), channel_id=1, source_target_pairs={{0,0},{1,4},{2,5},{3,6},{4,1},{5,2},{6,3},{7,7},{8,8},{9,12},{10,1... | collective-permute-start | bytes 540680 | tf_op jit(solution)/shard_map/ppermute | solution.py:732
  6.6 3.3 %collective-permute-done.1.refs_0_.refs_2_ = f32[21,16,128]{2,1,0:T(8,128)S(1)} collective-permute-done((f32[21,16,128]{2,1,0:T(8,128)S(1)}, f32[21,16,128]{2,1,0:T(8,128)S(1)}, u32[]{:S(2)}, u32[]{:S(2)}) %collective-permute-start.1) | collective-permute-done | bytes 172064 | tf_op jit(solution)/shard_map/ppermute | solution.py:724
  9.9 0.0 collective-permute-start.3
  9.9 0.0 collective-permute-done.2.refs_1_.refs_3_
  9.9 0.5 collective-permute-start.4
  10.4 0.9 %collective-permute-done.3.refs_2_.refs_4_ = f32[21,16,128]{2,1,0:T(8,128)S(1)} collective-permute-done((f32[21,16,128]{2,1,0:T(8,128)S(1)}, f32[21,16,128]{2,1,0:T(8,128)S(1)}, u32[]{:S(2)}, u32[]{:S(2)}) %collective-permute-start.3) | collective-permute-done | bytes 172064 | tf_op jit(solution)/shard_map/ppermute | solution.py:715
  11.3 0.0 collective-permute-done.5.refs_4_.refs_6_
  11.3 0.2 collective-permute-done.4.refs_3_.refs_5_
  11.5 0.2 pack_halo.1
  11.8 0.7 %collective-permute-start.6 = (f32[4,32,128]{2,1,0:T(8,128)S(1)}, f32[4,32,128]{2,1,0:T(8,128)S(1)}, u32[]{:S(2)}, u32[]{:S(2)}) collective-permute-start(f32[4,32,128]{2,1,0:T(8,128)S(1)} %pack_halo.1), channel_id=1, source_target_pairs={{0,0},{1,4},{2,5},{3,6},{4,1},{5,2},{6,3},{7,7},{8,8},{9,12},{10,1... | collective-permute-start | bytes 196616 | tf_op jit(solution)/shard_map/ppermute | solution.py:732
  12.5 0.0 collective-permute-done.6.refs_7_
  12.5 5.6 %down.1 = (f32[32,8,128]{2,1,0:T(8,128)}, f32[9,16,128]{2,1,0:T(8,128)S(1)}, f32[9,16,128]{2,1,0:T(8,128)S(1)}, f32[333,32,128]{2,1,0:T(8,128)}) custom-call(f32[64,16,128]{2,1,0:T(8,128)S(1)} %pad_maximum_fusion.refs_0_, f32[64,16,128]{2,1,0:T(8,128)S(1)} %collective-permute-done.refs_1_, f32[21,16,128]{2,1,0:T(8,128)S(1)} %collective-permute-done.1.refs_0_.refs_2_, ...), custom_call_target="tpu_custom_call" | custom-call | flops 4000000 | bytes 8000000 | tf_op jit(solution)/shard_map/down/pallas_call | solution.py:770
  18.0 14.4 %all-to-all-start = ((f32[32,8,128]{2,1,0:T(8,128)}), f32[32,8,128]{2,1,0:T(8,128)S(1)}, u32[]{:S(2)}, u32[]{:S(2)}) async-start(f32[32,8,128]{2,1,0:T(8,128)} %get-tuple-element.21), calls=%async_computation | async-start | bytes 262144 | tf_op jit(solution)/shard_map/all_to_all | solution.py:817
  32.5 1.8 %collective-permute-start.7 = (f32[9,16,128]{2,1,0:T(8,128)S(1)}, f32[9,16,128]{2,1,0:T(8,128)S(1)}, u32[]{:S(2)}, u32[]{:S(2)}) collective-permute-start(f32[9,16,128]{2,1,0:T(8,128)S(1)} %get-tuple-element.22), channel_id=1, source_target_pairs={{0,8},{8,0},{16,24},{24,16},{1,9},{9,1},{17,25},{25,17},{2,10},{10... | collective-permute-start | bytes 221192 | tf_op jit(solution)/shard_map/ppermute | solution.py:724
  34.3 0.7 %collective-permute-start.8 = (f32[9,16,128]{2,1,0:T(8,128)S(1)}, f32[9,16,128]{2,1,0:T(8,128)S(1)}, u32[]{:S(2)}, u32[]{:S(2)}) collective-permute-start(f32[9,16,128]{2,1,0:T(8,128)S(1)} %get-tuple-element.23), channel_id=1, source_target_pairs={{0,0},{8,16},{16,8},{24,24},{1,1},{9,17},{17,9},{25,25},{2,2},{10,... | collective-permute-start | bytes 221192 | tf_op jit(solution)/shard_map/ppermute | solution.py:724
  35.0 2.9 %collective-permute-done.7.refs_2_ = f32[9,16,128]{2,1,0:T(8,128)S(1)} collective-permute-done((f32[9,16,128]{2,1,0:T(8,128)S(1)}, f32[9,16,128]{2,1,0:T(8,128)S(1)}, u32[]{:S(2)}, u32[]{:S(2)}) %collective-permute-start.7) | collective-permute-done | bytes 73760 | tf_op jit(solution)/shard_map/ppermute | solution.py:724
  37.8 0.0 collective-permute-done.8.refs_3_
  37.8 3.0 %all-to-all-done.refs_0_ = f32[32,8,128]{2,1,0:T(8,128)S(1)} async-done(((f32[32,8,128]{2,1,0:T(8,128)}), f32[32,8,128]{2,1,0:T(8,128)S(1)}, u32[]{:S(2)}, u32[]{:S(2)}) %all-to-all-start) | async-done | bytes 131104 | tf_op jit(solution)/shard_map/all_to_all | solution.py:817
  40.9 0.0 collective-permute-start.9
  40.9 1.3 %collective-permute-done.9.refs_1_ = f32[32,8,128]{2,1,0:T(8,128)S(1)} collective-permute-done((f32[32,8,128]{2,1,0:T(8,128)S(1)}, f32[32,8,128]{2,1,0:T(8,128)S(1)}, u32[]{:S(2)}, u32[]{:S(2)}) %collective-permute-start.9) | collective-permute-done | bytes 131104 | tf_op jit(solution)/shard_map/ppermute | solution.py:715
  42.2 6.4 %up.1 = (f32[32,16,128]{2,1,0:T(8,128)S(1)}, f32[32,16,128]{2,1,0:T(8,128)S(1)}, f32[32,16,128]{2,1,0:T(8,128)S(1)}, f32[32,16,128]{2,1,0:T(8,128)S(1)}) custom-call(f32[32,8,128]{2,1,0:T(8,128)S(1)} %all-to-all-done.refs_0_, f32[32,8,128]{2,1,0:T(8,128)S(1)} %collective-permute-done.9.refs_1_, f32[9,16,128]{2,1,0:T(8,128)S(1)} %collective-permute-done.7.refs_2_, ...), custom_call_target="tpu_custom_call" | custom-call | flops 4000000 | bytes 8000000 | tf_op jit(solution)/shard_map/up/pallas_call | solution.py:770
  48.6 0.2 collective-permute-start.10
  48.8 0.4 collective-permute-start.11
  49.2 1.0 %collective-permute-done.10 = f32[32,16,128]{2,1,0:T(8,128)S(1)} collective-permute-done((f32[32,16,128]{2,1,0:T(8,128)S(1)}, f32[32,16,128]{2,1,0:T(8,128)S(1)}, u32[]{:S(2)}, u32[]{:S(2)}) %collective-permute-start.10) | collective-permute-done | bytes 262176 | tf_op jit(solution)/shard_map/ppermute | solution.py:715
  50.2 0.4 collective-permute-done.11
  50.6 0.9 %broadcast_select_fusion = (f32[32,16,128]{2,1,0:T(8,128)}, f32[32,16,128]{2,1,0:T(8,128)}) fusion(f32[32,16,128]{2,1,0:T(8,128)S(1)} %get-tuple-element.30, f32[32,16,128]{2,1,0:T(8,128)S(1)} %collective-permute-done.11, pred[128]{0:T(512)(128)(4,1)S(1)} %fusion.2, f32[32,16,128]{2,1,0:T(8,128)S(1)} %get-tuple-element.28, ...), kind=kLoop, calls=%fused_computation.5 | loop fusion | flops 131072 | bytes 1572992 | tf_op jit(solution)/shard_map/jit(_where)/select_n | solution.py:840
  (4 shorter events, 0.1 us)
Async XLA Ops:
  1.7 3.2 %collective-permute-start = (f32[64,16,128]{2,1,0:T(8,128)S(1)}, f32[64,16,128]{2,1,0:T(8,128)S(1)}, u32[]{:S(2)}, u32[]{:S(2)}) collective-permute-start(f32[64,16,128]{2,1,0:T(8,128)S(1)} %pad_maximum_fusion.refs_0_), channel_id=1, source_target_pairs={{0,4},{4,0},{1,5},{5,1},{2,6},{6,2},{3,7},{7,3},{8,12},{12,8},{9,1... | collective-permute-start | bytes 1572872 | tf_op jit(solution)/shard_map/ppermute | solution.py:715
  2.3 7.6 %collective-permute-start.1 = (f32[21,16,128]{2,1,0:T(8,128)S(1)}, f32[21,16,128]{2,1,0:T(8,128)S(1)}, u32[]{:S(2)}, u32[]{:S(2)}) collective-permute-start(f32[21,16,128]{2,1,0:T(8,128)S(1)} %get-tuple-element.36), channel_id=1, source_target_pairs={{0,8},{8,0},{16,24},{24,16},{1,9},{9,1},{17,25},{25,17},{2,10},{10... | collective-permute-start | bytes 516104 | tf_op jit(solution)/shard_map/ppermute | solution.py:724
  4.9 5.0 %collective-permute-start.2 = (f32[21,16,128]{2,1,0:T(8,128)S(1)}, f32[21,16,128]{2,1,0:T(8,128)S(1)}, u32[]{:S(2)}, u32[]{:S(2)}) collective-permute-start(f32[21,16,128]{2,1,0:T(8,128)S(1)} %get-tuple-element.19), channel_id=1, source_target_pairs={{0,0},{8,16},{16,8},{24,24},{1,1},{9,17},{17,9},{25,25},{2,2},{10,... | collective-permute-start | bytes 516104 | tf_op jit(solution)/shard_map/ppermute | solution.py:724
  5.9 5.4 %collective-permute-start.5 = (f32[11,32,128]{2,1,0:T(8,128)S(1)}, f32[11,32,128]{2,1,0:T(8,128)S(1)}, u32[]{:S(2)}, u32[]{:S(2)}) collective-permute-start(f32[11,32,128]{2,1,0:T(8,128)S(1)} %pack_box.1), channel_id=1, source_target_pairs={{0,0},{1,4},{2,5},{3,6},{4,1},{5,2},{6,3},{7,7},{8,8},{9,12},{10,1... | collective-permute-start | bytes 540680 | tf_op jit(solution)/shard_map/ppermute | solution.py:732
  9.9 1.4 %collective-permute-start.3 = (f32[21,16,128]{2,1,0:T(8,128)S(1)}, f32[21,16,128]{2,1,0:T(8,128)S(1)}, u32[]{:S(2)}, u32[]{:S(2)}) collective-permute-start(f32[21,16,128]{2,1,0:T(8,128)S(1)} %collective-permute-done.1.refs_0_.refs_2_), channel_id=1, source_target_pairs={{0,4},{4,0},{1,5},{5,1},{2,6},{6,2},{3,7},{7,3},{8,12},{12,8},{9,1... | collective-permute-start | bytes 516104 | tf_op jit(solution)/shard_map/ppermute | solution.py:715
  9.9 1.6 %collective-permute-start.4 = (f32[21,16,128]{2,1,0:T(8,128)S(1)}, f32[21,16,128]{2,1,0:T(8,128)S(1)}, u32[]{:S(2)}, u32[]{:S(2)}) collective-permute-start(f32[21,16,128]{2,1,0:T(8,128)S(1)} %collective-permute-done.2.refs_1_.refs_3_), channel_id=1, source_target_pairs={{0,4},{4,0},{1,5},{5,1},{2,6},{6,2},{3,7},{7,3},{8,12},{12,8},{9,1... | collective-permute-start | bytes 516104 | tf_op jit(solution)/shard_map/ppermute | solution.py:715
  11.8 0.7 %collective-permute-start.6 = (f32[4,32,128]{2,1,0:T(8,128)S(1)}, f32[4,32,128]{2,1,0:T(8,128)S(1)}, u32[]{:S(2)}, u32[]{:S(2)}) collective-permute-start(f32[4,32,128]{2,1,0:T(8,128)S(1)} %pack_halo.1), channel_id=1, source_target_pairs={{0,0},{1,4},{2,5},{3,6},{4,1},{5,2},{6,3},{7,7},{8,8},{9,12},{10,1... | collective-permute-start | bytes 196616 | tf_op jit(solution)/shard_map/ppermute | solution.py:732
  18.0 22.9 %all-to-all-start = ((f32[32,8,128]{2,1,0:T(8,128)}), f32[32,8,128]{2,1,0:T(8,128)S(1)}, u32[]{:S(2)}, u32[]{:S(2)}) async-start(f32[32,8,128]{2,1,0:T(8,128)} %get-tuple-element.21), calls=%async_computation | async-start | bytes 262144 | tf_op jit(solution)/shard_map/all_to_all | solution.py:817
  32.5 5.4 %collective-permute-start.7 = (f32[9,16,128]{2,1,0:T(8,128)S(1)}, f32[9,16,128]{2,1,0:T(8,128)S(1)}, u32[]{:S(2)}, u32[]{:S(2)}) collective-permute-start(f32[9,16,128]{2,1,0:T(8,128)S(1)} %get-tuple-element.22), channel_id=1, source_target_pairs={{0,8},{8,0},{16,24},{24,16},{1,9},{9,1},{17,25},{25,17},{2,10},{10... | collective-permute-start | bytes 221192 | tf_op jit(solution)/shard_map/ppermute | solution.py:724
  34.3 3.5 %collective-permute-start.8 = (f32[9,16,128]{2,1,0:T(8,128)S(1)}, f32[9,16,128]{2,1,0:T(8,128)S(1)}, u32[]{:S(2)}, u32[]{:S(2)}) collective-permute-start(f32[9,16,128]{2,1,0:T(8,128)S(1)} %get-tuple-element.23), channel_id=1, source_target_pairs={{0,0},{8,16},{16,8},{24,24},{1,1},{9,17},{17,9},{25,25},{2,2},{10,... | collective-permute-start | bytes 221192 | tf_op jit(solution)/shard_map/ppermute | solution.py:724
  40.9 1.3 %collective-permute-start.9 = (f32[32,8,128]{2,1,0:T(8,128)S(1)}, f32[32,8,128]{2,1,0:T(8,128)S(1)}, u32[]{:S(2)}, u32[]{:S(2)}) collective-permute-start(f32[32,8,128]{2,1,0:T(8,128)S(1)} %all-to-all-done.refs_0_), channel_id=1, source_target_pairs={{0,4},{4,0},{1,5},{5,1},{2,6},{6,2},{3,7},{7,3},{8,12},{12,8},{9,1... | collective-permute-start | bytes 393224 | tf_op jit(solution)/shard_map/ppermute | solution.py:715
  48.6 1.6 %collective-permute-start.10 = (f32[32,16,128]{2,1,0:T(8,128)S(1)}, f32[32,16,128]{2,1,0:T(8,128)S(1)}, u32[]{:S(2)}, u32[]{:S(2)}) collective-permute-start(f32[32,16,128]{2,1,0:T(8,128)S(1)} %get-tuple-element.29), channel_id=1, source_target_pairs={{0,4},{4,0},{1,5},{5,1},{2,6},{6,2},{3,7},{7,3},{8,12},{12,8},{9,1... | collective-permute-start | bytes 786440 | tf_op jit(solution)/shard_map/ppermute | solution.py:715
  48.8 1.8 %collective-permute-start.11 = (f32[32,16,128]{2,1,0:T(8,128)S(1)}, f32[32,16,128]{2,1,0:T(8,128)S(1)}, u32[]{:S(2)}, u32[]{:S(2)}) collective-permute-start(f32[32,16,128]{2,1,0:T(8,128)S(1)} %get-tuple-element.31), channel_id=1, source_target_pairs={{0,4},{4,0},{1,5},{5,1},{2,6},{6,2},{3,7},{7,3},{8,12},{12,8},{9,1... | collective-permute-start | bytes 786440 | tf_op jit(solution)/shard_map/ppermute | solution.py:715
